TPU v7x, 128 devices: a whole 4x4x4 slice. The times are simulated.
128 devices in a mesh: row: 16 (over y_lo, x, core), col: 8 (over y_hi, z).
Axes of the slice: x: 4, y: 4 (y_hi: 2, y_lo: 2; y = y_hi * 2 + y_lo), z: 4, core: 2. Of those that a mesh axis runs over, the one named last changes fastest.
Arguments:
- child_factor: float32 [4, 16, 256, 1024], P(None, 'row', None, 'col'), may hold values from -1 to 1
- parent: float32 [4, 16, 256, 8, 8, 256], P(None, 'row', None, None, 'col'), may hold values from -6 to 6
- row_map: int32 [2, 32, 256], replicated, may hold values from 0 to 255, each once within a row
- child_listed: int32 [2, 32, 32], replicated, may hold values 0 or 1
- inv_diag: float32 [512, 512], replicated, as said below
- panel_listed: int32 [64, 64], replicated, may hold values 0 or 1
Outputs:
- factored: float32 [4, 16, 256, 8, 8, 256], P(None, 'row', None, None, 'col')
- panel_factor: float32 [4, 16, 256, 512], P(None, 'row')
Inputs may be any that keep to these rules, and one draw needn't show every extreme that they name: `row_map`: for every child and block, the 256 entries are a permutation of 0 to 255. `inv_diag`: lower triangular with a positive diagonal.
All inputs are finite; a program needn't handle non-finite values.
Results may differ from a plain program's by a relative error of at most 0.0001.
Values sent between devices are 32-bit elements; how exact they have to be, the bound alone decides.
No kernel may reach another device: no remote copies, remote signals or barrier semaphores. Data moves between devices by JAX's collectives and lax.ppermute only.
A program may use at most 128 MiB of HBM per device.

v0:
```python
import jax
import jax.numpy as jnp
from jax import lax
from jax.sharding import PartitionSpec as P

BS = 256
KC = 1024
PW = 512
SHIFT = 16


precise = lax.Precision.HIGHEST


def from_partner(block, axis, apart):
    count = lax.axis_size(axis)
    route = []
    for low in range(count):
        high = low | 1 << apart
        if high != low and high < count:
            route += [(low, high), (high, low)]
    return lax.ppermute(block, axis, route)


def spread(value, axis, source):
    kept = jnp.where(lax.axis_index(axis) == source, value, 0).astype(value.dtype)
    return lax.psum(kept, axis)


def contract_rows(left, right):
    return lax.dot_general(
        left, right, (((1,), (1,)), ((), ())), precision=precise, preferred_element_type=jnp.float32
    )


def subtract_block(assembled, piece, row_start, col_start):
    starts = (row_start, 0, col_start, 0)
    region = lax.dynamic_slice(assembled, starts, piece.shape)
    return lax.dynamic_update_slice(assembled, region - piece, starts)


def shards(child_factor, parent, row_map, child_listed, inv_diag, panel_listed):
    row_count = lax.axis_size("row")
    col_count = lax.axis_size("col")
    half_rows = row_count // 2
    row_index = lax.axis_index("row")
    col_index = lax.axis_index("col")
    child_index = row_index // half_rows
    local_row = row_index % half_rows
    slab_count = child_factor.shape[0]
    slice_width = child_factor.shape[3]
    row_slots = parent.shape[0]
    col_slots = parent.shape[3]
    own_rows = child_factor.reshape(slab_count, BS, slice_width)
    child_map = lax.dynamic_index_in_dim(row_map, child_index, 0, keepdims=False)
    own_map = lax.dynamic_index_in_dim(
        child_map.reshape(slab_count, half_rows, BS), local_row, 1, keepdims=False
    )
    slab_ids = jnp.arange(slab_count, dtype=jnp.int32)[:, None]
    within = jnp.broadcast_to(jnp.arange(BS, dtype=jnp.int32)[None, :], (slab_count, BS))
    inverse = jnp.zeros((slab_count, BS), jnp.int32).at[slab_ids, own_map].set(within)
    placed = own_rows[slab_ids, inverse]
    own_full = lax.all_gather(placed, "col", axis=2, tiled=True)
    partner_full = own_full
    for bit_level in range(half_rows.bit_length() - 1):
        received = from_partner(partner_full, "row", bit_level)
        has_data = (local_row ^ col_index) >> bit_level == 0
        partner_full = jnp.where(has_data, partner_full, received)
    update = contract_rows(
        own_full.reshape(slab_count * BS, KC), partner_full.reshape(slab_count * BS, KC)
    )
    listed_child = lax.dynamic_index_in_dim(child_listed, child_index, 0, keepdims=False)
    listed_child = listed_child.reshape(slab_count, half_rows, slab_count, half_rows)
    listed_child = lax.dynamic_index_in_dim(listed_child, local_row, 1, keepdims=False)
    listed_child = lax.dynamic_index_in_dim(listed_child, col_index, 2, keepdims=False).astype(
        jnp.float32
    )
    update = update.reshape(slab_count, BS, slab_count, BS) * listed_child[:, None, :, None]
    paired = update.reshape(slab_count // 2, 2, BS, slab_count, BS)
    retained = lax.dynamic_index_in_dim(paired, child_index, 1, keepdims=False)
    outgoing = lax.dynamic_index_in_dim(paired, 1 - child_index, 1, keepdims=False)
    received_half = from_partner(outgoing, "row", row_count.bit_length() - 2)
    assembled = parent.reshape(row_slots, BS, col_slots, BS)
    row_shift = SHIFT // row_count
    col_shift = SHIFT // col_count
    assembled = subtract_block(
        assembled, retained, row_shift * child_index, col_shift * child_index
    )
    assembled = subtract_block(
        assembled, received_half, row_shift * (1 - child_index), col_shift * (1 - child_index)
    )
    panel_blocks = PW // BS
    lead_columns = assembled[:, :, 0, :].reshape(row_slots * BS, BS)
    inv_block = lax.dynamic_slice_in_dim(inv_diag, col_index * BS, BS, 1)
    partial_panel = jnp.where(col_index < panel_blocks, contract_rows(lead_columns, inv_block), 0.0)
    panel_rows = lax.psum(partial_panel, "col")
    panel_grid = panel_rows.reshape(row_slots, BS, PW)
    copies = []
    for copy_index in range(row_count // col_count):
        copies.append(spread(panel_grid, "row", col_index + col_count * copy_index))
    column_rows = jnp.stack(copies, axis=1).reshape(col_slots * BS, PW)
    product = contract_rows(panel_rows, column_rows).reshape(row_slots, BS, col_slots, BS)
    listed_panel = panel_listed.reshape(row_slots, row_count, col_slots, col_count)
    listed_panel = lax.dynamic_index_in_dim(listed_panel, row_index, 1, keepdims=False)
    listed_panel = lax.dynamic_index_in_dim(listed_panel, col_index, 2, keepdims=False)
    row_blocks = jnp.arange(row_slots)[:, None] * row_count + row_index
    col_blocks = jnp.arange(col_slots)[None, :] * col_count + col_index
    trailing = (row_blocks >= panel_blocks) & (col_blocks >= panel_blocks) & (listed_panel == 1)
    factored = assembled - jnp.where(trailing[:, None, :, None], product, 0.0)
    return (factored.reshape(parent.shape), panel_grid.reshape(row_slots, 1, BS, PW))


def solution(mesh):
    return jax.shard_map(
        shards,
        mesh=mesh,
        in_specs=(
            P(None, "row", None, "col"),
            P(None, "row", None, None, "col", None),
            P(),
            P(),
            P(),
            P(),
        ),
        out_specs=(P(None, "row", None, None, "col", None), P(None, "row", None, None)),
        check_vma=False,
    )
```

profile of v0, /device:TPU:66, one launch (start us, length us, event | category | flops | bytes accessed | tf_op | source)
XLA Modules:
  0.0 646.2 jit_solution(14541791357016119619)
XLA Ops:
  7.3 0.8 dynamic-slice_bitcast_fusion.1
  8.1 0.7 multiply_reduce_fusion
  8.9 0.7 and_reduce_fusion
  9.7 4.3 scatter_custom_fusion
  14.0 16.2 %gather_fusion = f32[1024,128]{1,0:T(8,128)} fusion(f32[4,256,128]{2,1,0:T(8,128)} %bitcast.66, s32[1024]{0:T(1024)S(1)} %bitcast.62), kind=kCustom, calls=%fused_computation | custom fusion | bytes 1056768 | tf_op jit(solution)/shard_map/gather | solution.py:62
  30.4 74.0 %all-gather.2.cloned.1.call-done = f32[4,256,1024]{2,1,0:T(8,128)} async-done(((f32[4,256,128]{2,1,0:T(8,128)}), f32[4,256,1024]{2,1,0:T(8,128)}) %all-gather.2.cloned.1.call-update) | async-done | bytes 4194320 | tf_op jit(solution)/shard_map/all_gather | solution.py:63
  104.3 7.5 %collective-permute-done = f32[4,256,1024]{2,1,0:T(8,128)} collective-permute-done((f32[4,256,1024]{2,1,0:T(8,128)}, f32[4,256,1024]{2,1,0:T(8,128)}, u32[]{:S(2)}, u32[]{:S(2)}) %collective-permute-start) | collective-permute-done | bytes 4194336 | tf_op jit(solution)/shard_map/ppermute | solution.py:22
  111.8 5.6 broadcast_select_fusion
  117.4 0.6 collective-permute-start.1
  117.9 92.4 %collective-permute-done.1 = f32[4,256,1024]{2,1,0:T(8,128)} collective-permute-done((f32[4,256,1024]{2,1,0:T(8,128)}, f32[4,256,1024]{2,1,0:T(8,128)}, u32[]{:S(2)}, u32[]{:S(2)}) %collective-permute-start.1) | collective-permute-done | bytes 4194336 | tf_op jit(solution)/shard_map/ppermute | solution.py:22
  210.3 5.6 broadcast_select_fusion.1
  215.9 2.3 collective-permute-start.2
  218.5 91.2 %collective-permute-done.2 = f32[4,256,1024]{2,1,0:T(8,128)} collective-permute-done((f32[4,256,1024]{2,1,0:T(8,128)}, f32[4,256,1024]{2,1,0:T(8,128)}, u32[]{:S(2)}, u32[]{:S(2)}) %collective-permute-start.2) | collective-permute-done | bytes 4194336 | tf_op jit(solution)/shard_map/ppermute | solution.py:22
  309.8 16.4 %fusion.4 = f32[4,256,4,256]{3,1,2,0:T(8,128)S(1)} fusion(f32[4,256,1024]{2,1,0:T(8,128)} %broadcast_select_fusion.1, f32[4,256,1024]{2,1,0:T(8,128)} %collective-permute-done.2, f32[4,256,1024]{2,1,0:T(8,128)} %all-gather.2.cloned.1.call-done, f32[4,4]{1,0:T(4,128)S(1)} %convert_reduce_fusion, pred[]{:T(512)S(6)} %eq.24), kind=kOutput, calls=%fused_computation.9 | convolution fusion | flops 12886999040 | bytes 16777280 | tf_op jit(solution)/shard_map/dot_general | solution.py:31
  326.2 1.9 copy-done.3
  328.4 1.2 collective-permute-start.3
  329.6 9.3 %copy.42 = f32[4,1,256,8,1,256]{5,2,3,0,4,1:T(8,128)} copy(f32[4,1,256,8,1,256]{5,4,3,2,1,0:T(1,128)} %param.7) | data formatting | bytes 16777216 | tf_op args[1]
  338.9 3.2 constant_dynamic-slice_fusion.2
  342.1 1.8 fusion.9
  343.9 31.1 %collective-permute-done.3 = f32[2,256,4,256]{3,1,2,0:T(8,128)} collective-permute-done((f32[2,256,4,256]{3,1,2,0:T(8,128)S(1)}, f32[2,256,4,256]{3,1,2,0:T(8,128)}, u32[]{:S(2)}, u32[]{:S(2)}) %collective-permute-start.3) | collective-permute-done | bytes 2097184 | tf_op jit(solution)/shard_map/ppermute | solution.py:22
  375.0 3.8 subtract_dynamic-update-slice_fusion
  378.8 1.3 slice.6
  380.1 3.2 convolution_select_fusion
  383.6 88.8 %all-reduce.4.cloned.1.call-done = f32[1024,512]{1,0:T(8,128)} async-done(((f32[1024,512]{1,0:T(8,128)}), f32[1024,512]{1,0:T(8,128)}) %all-reduce.4.cloned.1.call-update) | async-done | bytes 2097168 | tf_op jit(solution)/shard_map/psum | solution.py:96
  472.4 4.3 select_bitcast_fusion.1
  477.2 127.7 %all-reduce.6.cloned.1.call-done = (f32[4,1,256,512]{3,2,0,1:T(8,128)}, f32[4,1,256,512]{3,2,0,1:T(8,128)}) async-done(((f32[4,1,256,512]{3,2,0,1:T(8,128)}, f32[4,1,256,512]{3,2,0,1:T(8,128)}), (f32[4,1,256,512]{3,2,0,1:T(8,128)}, f32[4,1,256,512]{3,2,0,1:T(8,128)})) %all-reduce.6.cloned.1.call-update) | async-done | bytes 4194320 | tf_op jit(solution)/shard_map/psum | solution.py:27
  604.9 2.8 pad_maximum_fusion
  608.3 1.7 slice-done.1
  610.1 0.6 copy-done.2
  610.7 14.7 %subtract_bitcast_fusion = f32[4,1,256,8,1,256]{5,2,3,0,4,1:T(8,128)S(1)} fusion(f32[4,256,8,256]{3,1,2,0:T(8,128)S(1)} %bitcast.65, pred[4,8]{1,0:T(4,128)(4,1)S(1)} %and_bitcast_fusion, f32[4,256,512,1]{2,1,3,0:T(8,128)S(1)} %bitcast.68, f32[8,256,512,1]{2,1,0,3:T(8,128)S(1)} %bitcast.72), kind=kOutput, calls=%fused_computation.3 | convolution fusion | flops 12889096192 | bytes 23068704 | tf_op jit(solution)/shard_map/dot_general | solution.py:31
  625.4 12.7 %copy.33 = f32[4,1,256,8,1,256]{5,4,3,2,1,0:T(1,128)} copy(f32[4,1,256,8,1,256]{5,2,3,0,4,1:T(8,128)S(1)} %subtract_bitcast_fusion) | data formatting | bytes 16777216
  638.1 1.3 copy.48
  (44 shorter events, 2.0 us)
Async XLA Ops:
  7.2 373.0 %copy-start = (f32[512,512]{1,0:T(8,128)S(1)}, f32[512,512]{1,0:T(8,128)}, u32[]{:S(2)}) copy-start(f32[512,512]{1,0:T(8,128)} %param.10) | copy-start | bytes 3145732
  7.2 97.1 %all-gather.2.cloned.1.call-start = ((), (), s32[]{:S(2)}) async-start(), calls=%async_computation | async-start | bytes 4718592 | tf_op jit(solution)/shard_map/all_gather | solution.py:63
  30.3 442.1 %all-reduce.4.cloned.1.call-start = ((), (), s32[]{:S(2)}) async-start(), calls=%async_computation.1 | async-start | bytes 4194304 | tf_op jit(solution)/shard_map/psum | solution.py:96
  104.3 7.5 %collective-permute-start = (f32[4,256,1024]{2,1,0:T(8,128)}, f32[4,256,1024]{2,1,0:T(8,128)}, u32[]{:S(2)}, u32[]{:S(2)}) collective-permute-start(f32[4,256,1024]{2,1,0:T(8,128)} %all-gather.2.cloned.1.call-done), channel_id=1, source_target_pairs={{0,8},{8,0},{16,24},{24,16},{32,40},{40,32},{48,56},{56,48},{64,72... | collective-permute-start | bytes 12582920 | tf_op jit(solution)/shard_map/ppermute | solution.py:22
  117.4 92.9 %collective-permute-start.1 = (f32[4,256,1024]{2,1,0:T(8,128)}, f32[4,256,1024]{2,1,0:T(8,128)}, u32[]{:S(2)}, u32[]{:S(2)}) collective-permute-start(f32[4,256,1024]{2,1,0:T(8,128)} %broadcast_select_fusion), channel_id=1, source_target_pairs={{0,16},{16,0},{8,24},{24,8},{32,48},{48,32},{40,56},{56,40},{64,80... | collective-permute-start | bytes 12582920 | tf_op jit(solution)/shard_map/ppermute | solution.py:22
  117.9 100.3 %copy-start.6 = (s32[2,32,32]{2,1,0:T(8,128)S(1)}, s32[2,32,32]{2,1,0:T(8,128)}, u32[]{:S(2)}) copy-start(s32[2,32,32]{2,1,0:T(8,128)} %param.9) | copy-start | bytes 24580
  215.9 93.9 %collective-permute-start.2 = (f32[4,256,1024]{2,1,0:T(8,128)}, f32[4,256,1024]{2,1,0:T(8,128)}, u32[]{:S(2)}, u32[]{:S(2)}) collective-permute-start(f32[4,256,1024]{2,1,0:T(8,128)} %broadcast_select_fusion.1), channel_id=1, source_target_pairs={{0,32},{32,0},{8,40},{40,8},{16,48},{48,16},{24,56},{56,24},{64,96... | collective-permute-start | bytes 12582920 | tf_op jit(solution)/shard_map/ppermute | solution.py:22
  326.2 1.9 copy-start.3
  328.4 46.6 %collective-permute-start.3 = (f32[2,256,4,256]{3,1,2,0:T(8,128)S(1)}, f32[2,256,4,256]{3,1,2,0:T(8,128)}, u32[]{:S(2)}, u32[]{:S(2)}) collective-permute-start(f32[2,256,4,256]{3,1,2,0:T(8,128)S(1)} %dynamic-slice_bitcast_fusion), channel_id=1, source_target_pairs={{0,64},{64,0},{8,72},{72,8},{16,80},{80,16},{24,88},{88,24},{32,96... | collective-permute-start | bytes 6291464 | tf_op jit(solution)/shard_map/ppermute | solution.py:22
  338.9 3.2 copy-start.4
  383.3 221.6 %all-reduce.6.cloned.1.call-start = ((), (), s32[]{:S(2)}) async-start(), calls=%async_computation.2 | async-start | bytes 8388608 | tf_op jit(solution)/shard_map/psum | solution.py:27
  472.4 4.3 copy-start.5
  604.9 3.4 slice-start
  607.7 2.3 slice-start.1
  607.7 2.9 copy-start.2
  625.4 14.0 %copy-start.1 = (f32[512,512]{1,0:T(8,128)S(1)}, f32[512,512]{1,0:T(8,128)}, u32[]{:S(2)}) copy-start(f32[512,512]{1,0:T(8,128)} %param.10) | copy-start | bytes 3145732
Sparse Core Ops, SparseCore 0:
  30.4 73.8 all-gather.1
  383.5 88.8 all-reduce.3
  476.8 127.9 all-reduce.5
where the time goes:
time: 655 us; the launch traced here: 646 us
  waiting for transfers between devices  513 us (78%)
  local copies, waits for them, and re-layouts  54.8 us (8%)
  matrix products  34.3 us (5%)
  other arithmetic  25.7 us (4%)
  between operations  14.3 us (2%)
    ppermute x4, waiting for transfers between devices, from_partner(): return lax.ppermute(block, axis, route)  222 us
    psum x1, waiting for transfers between devices, spread(): return lax.psum(kept, axis)  128 us
    psum x1, waiting for transfers between devices, shards(): panel_rows = lax.psum(partial_panel, 'col')  88.8 us
    all_gather x1, waiting for transfers between devices, shards(): own_full = lax.all_gather(placed, 'col', axis=2, tiled=True)  74 us
    dot_general x3, matrix products, contract_rows(): lax.dot_general(left, right, (((1,), (1,)), ((), ())), precision=precise,...  34.3 us
    unnamed x27, local copies, waits for them, and re-layouts  32.3 us
    gather x1, local copies, waits for them, and re-layouts, shards(): placed = own_rows[slab_ids, inverse]  16.2 us
  transfers between devices with their start and end apart: 7, of which 7 were waited for; matrix products, arithmetic and copies ran while one was open for 2% of the time, Pallas kernels for 0%

commit v1 on v0

v1 whole, which is shorter than its diff:
```python
import itertools
import jax
import jax.numpy as jnp
from jax import lax
from jax.experimental import pallas as pl
from jax.experimental.pallas import tpu as pltpu
from jax.sharding import Mesh, PartitionSpec as P

BS = 256
AXES = ("ylo", "x", "core", "yhi", "z")
SIZES = (2, 4, 2, 2, 4)
NT = (((1,), (1,)), ((), ()))
STEPS = 7


def route(move, keep=lambda dev: True):
    pairs = []
    for spot in itertools.product(*[range(n) for n in SIZES]):
        dev = dict(zip(AXES, spot))
        if not keep(dev):
            continue
        far = dict(dev)
        far.update(move(dev))
        flat = []
        for d in (dev, far):
            i = 0
            for a, n in zip(AXES, SIZES):
                i = i * n + d[a] % n
            flat.append(i)
        pairs.append(tuple(flat))
    return pairs


def send(value, pairs):
    return lax.ppermute(value, AXES, pairs)


def home(dev):
    return 2 * dev["yhi"] + dev["z"] // 2


def away(dev):
    apart = dev["x"] - home(dev)
    return (apart if dev["core"] == 0 else -apart) % 4


def halves(value):
    high = value.astype(jnp.bfloat16)
    return high, (value - high.astype(jnp.float32)).astype(jnp.bfloat16)


def mul3(ah, al, bh, bl):
    def dot(u, v):
        return lax.dot_general(u, v, NT, preferred_element_type=jnp.float32)

    return dot(ah, bh) + (dot(ah, bl) + dot(al, bh))


def place_kernel(where, own, maps, out):
    half = where[0]
    for s in range(4):
        spots = lax.broadcasted_iota(jnp.int32, (BS, BS), 0)
        pick = jnp.where(spots == maps[s, :][None, :], 1.0, 0.0).astype(jnp.bfloat16)
        value = own[s]
        total = None
        for _ in range(3):
            part = value.astype(jnp.bfloat16)
            value = value - part.astype(jnp.float32)
            moved = jnp.dot(pick, part, preferred_element_type=jnp.float32)
            total = moved if total is None else total + moved
        out[lax.rem(half + s, 2), s // 2] = total


def place(half, own, maps):
    return pl.pallas_call(
        place_kernel,
        out_shape=jax.ShapeDtypeStruct((2, 2, BS, 128), jnp.float32),
        in_specs=[
            pl.BlockSpec(memory_space=pltpu.SMEM),
            pl.BlockSpec(memory_space=pltpu.VMEM),
            pl.BlockSpec(memory_space=pltpu.VMEM),
        ],
        out_specs=pl.BlockSpec(memory_space=pltpu.VMEM),
        name="place",
    )(half, own, maps)


def final_kernel(
    spot, child_mask, panel_mask, inv, lead_all, parent, *refs
):
    pieces = refs[:12]
    columns = [refs[12 + STEPS * n : 12 + STEPS * (n + 1)] for n in range(4)]
    (out, panel) = refs[12 + 4 * STEPS : 14 + 4 * STEPS]
    (
        rh, rl, ch, cl, eh, el, lead_o, lead_c, ph, pll, qh, ql, vh, vl, stage_r, stage_c, acc, sems,
    ) = refs[14 + 4 * STEPS :]
    p, x, core, yhi, z = (spot[n] for n in range(5))
    q = 2 * x + core
    c = 4 * yhi + z
    apart = lax.rem(x - (2 * yhi + z // 2) + 4, 4)
    apart = jnp.where(core == 0, apart, lax.rem(4 - apart, 4))
    apart_other = lax.rem(4 - apart, 4)
    slot = pl.program_id(0)

    def put_rows(block, count, high, low, base, z_from, yhi_at):
        for yr in range(2):
            start = pl.multiple_of(z_from * 256 + lax.rem(yhi_at + yr, 2) * 128, 128)
            for i in range(2):
                a, b = halves(block[yr * 2 + i])
                high[base + count * i, :, pl.ds(start, 128)] = a
                low[base + count * i, :, pl.ds(start, 128)] = b

    def put_lead(block, first, lead, base, lane, z_from):
        right = jnp.logical_or(z_from == 1, z_from == 2).astype(jnp.int32)
        at = base + jnp.where(z_from >= 2, 2, 0) + lane
        for half in range(2):
            start = pl.multiple_of(right * 256 + half * 128, 128)
            lead[at, :, pl.ds(start, 128)] = block[first + half]

    @pl.when(slot == 0)
    def _():
        jobs = []
        turn = jnp.where(core == 0, 1, 3)
        turn_c = jnp.where(lax.rem(z, 2) == 0, 1, 3)
        for k in range(4):
            z_from = lax.rem(z + 4 * 4 - turn * k, 4)
            for lane in range(2):
                jobs.append(("row", pieces[3 * k + lane], lane, z_from))
            jobs.append(("lead", pieces[3 * k + 2], 0, z_from))
        for u in range(4):
            z_from = lax.rem(z + 4 * 4 - turn_c * u, 4)
            for n in range(4):
                jobs.append(("col", columns[n], (n, u), z_from))

        def at_of(job, slot_n):
            kind, ref, info, _ = job
            if kind == "row" or kind == "lead":
                return [(None, ref, stage_r.at[slot_n])]
            n, u = info
            dist = apart if n < 2 else apart_other
            return [(u + dist == t, ref[t], stage_c.at[slot_n]) for t in range(u, u + 4)]

        def begin(n):
            for cond, src, dst in at_of(jobs[n], n % 4):
                def go(src=src, dst=dst):
                    pltpu.make_async_copy(src, dst, sems.at[n % 4]).start()
                if cond is None:
                    go()
                else:
                    pl.when(cond)(go)

        def finish(n):
            _, src, dst = at_of(jobs[n], n % 4)[0]
            pltpu.make_async_copy(src, dst, sems.at[n % 4]).wait()

        def use(n):
            kind, _, info, z_from = jobs[n]
            if kind == "row":
                child = lax.rem(p + info, 2)
                put_rows(stage_r.at[n % 4], 1, rh, rl, child * 2, z_from, yhi)
            elif kind == "lead":
                for lane in range(2):
                    put_lead(stage_r.at[n % 4], 2 * lane, lead_o, 0, lane, z_from)
            else:
                which, _ = info
                lane = core if which < 2 else 1 - core
                plane = p if which % 2 == 0 else 1 - p
                child = lax.rem(plane + lane, 2)
                put_rows(stage_c.at[n % 4], 2, ch, cl, child * 4 + plane, z_from, yhi)
                put_lead(stage_c.at[n % 4], 4, lead_c, plane * 4, lane, z_from)

        for n in range(3):
            begin(n)
        a, b = halves(inv[...])
        vh[...] = a
        vl[...] = b
        for j in range(2):
            for k in range(8):
                a, b = halves(lead_all[j, k])
                at = (k % 4) * 256 + (k // 4) * 128
                eh[j, :, at : at + 128] = a
                el[j, :, at : at + 128] = b
        for n in range(len(jobs)):
            if n + 3 < len(jobs):
                begin(n + 3)
            finish(n)
            use(n)

        def panel_of(lead, at):
            ah, al = halves(lead[at])
            left = mul3(ah[:, :256], al[:, :256], vh[:256, :256], vl[:256, :256])
            right = mul3(ah, al, vh[256:, :], vl[256:, :])
            return jnp.concatenate([left, right], axis=1)

        for i in range(2):
            for j in range(2):
                @pl.when(child_mask[0, (p + 2 * i) * 8 + q, j] == 1)
                def _():
                    lead_o[i, :, j * 256 : j * 256 + 256] -= mul3(rh[i], rl[i], eh[j], el[j])

        for i in range(4):
            value = panel_of(lead_o, i)
            panel[i] = value
            a, b = halves(value)
            ph[i] = a
            pll[i] = b

        for plane in range(2):
            for i in range(2):
                for j in range(2):
                    @pl.when(child_mask[0, (plane + 2 * i) * 8 + c, j] == 1)
                    def _():
                        s = plane + 2 * i
                        lead_c[plane * 4 + i, :, j * 256 : j * 256 + 256] -= mul3(
                            ch[s], cl[s], eh[j], el[j]
                        )

        for n in range(8):
            a, b = halves(panel_of(lead_c, n))
            qh[n] = a
            ql[n] = b

    row_block = 16 * slot + 8 * p + q
    for j in range(8):
        for half in range(2):
            acc[:, half * 128 : half * 128 + 128] = parent[pl.ds(2 * j + half, BS, stride=16), :]
        for child in range(2):
            s = j - 2 * child
            if s < 0 or s >= 4:
                continue
            i = jnp.clip(slot - child, 0, 1)
            listed = child_mask[child, (p + 2 * i) * 8 + q, s * 8 + c] == 1
            @pl.when(jnp.logical_and(listed, slot - child == i))
            def _():
                acc[...] -= mul3(rh[child * 2 + i], rl[child * 2 + i], ch[child * 4 + s], cl[child * 4 + s])
        col_block = 8 * j + c
        trailing = jnp.logical_and(row_block >= 2, col_block >= 2)
        @pl.when(jnp.logical_and(trailing, panel_mask[row_block, col_block] == 1))
        def _():
            n = (j % 2) * 4 + j // 2
            acc[...] -= mul3(ph[slot], pll[slot], qh[n], ql[n])
        for half in range(2):
            out[pl.ds(2 * j + half, BS, stride=16), :] = acc[:, half * 128 : half * 128 + 128]


def finish_all(spot, child_mask, panel_mask, inv, lead_all, parent, pieces, columns):
    f32, bf16 = jnp.float32, jnp.bfloat16
    vmem = pl.BlockSpec(memory_space=pltpu.VMEM)
    smem = pl.BlockSpec(memory_space=pltpu.SMEM)
    far = pl.BlockSpec(memory_space=pl.ANY)
    arrays = list(pieces) + [ref for group in columns for ref in group]
    return pl.pallas_call(
        final_kernel,
        grid=(4,),
        out_shape=(
            jax.ShapeDtypeStruct((4 * BS * 16, 128), f32),
            jax.ShapeDtypeStruct((4, BS, 512), f32),
        ),
        in_specs=[smem, smem, smem, vmem, vmem, pl.BlockSpec((BS * 16, 128), lambda i: (i, 0))]
        + [far] * len(arrays),
        out_specs=(
            pl.BlockSpec((BS * 16, 128), lambda i: (i, 0)),
            pl.BlockSpec((4, BS, 512), lambda i: (0, 0, 0)),
        ),
        scratch_shapes=[
            pltpu.VMEM((4, BS, 1024), bf16),
            pltpu.VMEM((4, BS, 1024), bf16),
            pltpu.VMEM((8, BS, 1024), bf16),
            pltpu.VMEM((8, BS, 1024), bf16),
            pltpu.VMEM((2, BS, 1024), bf16),
            pltpu.VMEM((2, BS, 1024), bf16),
            pltpu.VMEM((4, BS, 512), f32),
            pltpu.VMEM((8, BS, 512), f32),
            pltpu.VMEM((4, BS, 512), bf16),
            pltpu.VMEM((4, BS, 512), bf16),
            pltpu.VMEM((8, BS, 512), bf16),
            pltpu.VMEM((8, BS, 512), bf16),
            pltpu.VMEM((512, 512), bf16),
            pltpu.VMEM((512, 512), bf16),
            pltpu.VMEM((4, 4, BS, 128), f32),
            pltpu.VMEM((4, 6, BS, 128), f32),
            pltpu.VMEM((BS, BS), f32),
            pltpu.SemaphoreType.DMA((4,)),
        ],
        compiler_params=pltpu.CompilerParams(vmem_limit_bytes=52 * 1024 * 1024),
        cost_estimate=pl.CostEstimate(flops=22_000_000_000, bytes_accessed=36_000_000, transcendentals=0),
        name="finish",
    )(spot, child_mask, panel_mask, inv, lead_all, parent, *arrays)


def shards(child_factor, parent, row_map, child_listed, inv_diag, panel_listed):
    p, x, core, yhi, z = (lax.axis_index(a) for a in AXES)
    spot = jnp.stack([p, x, core, yhi, z]).astype(jnp.int32)
    q = 2 * x + core
    first = core == 0
    own = child_factor.reshape(4, BS, 128)
    own_map = lax.dynamic_slice(row_map.reshape(2, 4, 8, BS), (p, 0, q, 0), (1, 4, 1, BS)).reshape(4, BS)
    placed = place(spot[:1], own, own_map)
    mine, other = placed[0], placed[1]

    flat = parent.reshape(4 * BS * 16, 128)
    lead = parent.reshape(4, BS, 16, 128)[:, :, :2, :].transpose(0, 2, 1, 3)

    source = jnp.where((p == 0) & (x == 0), mine[0], 0.0)
    lead_all = lax.all_gather(lax.psum(source, ("ylo", "x")), ("core", "yhi", "z")).reshape(2, 8, BS, 128)

    near = send(mine, route(lambda d: {"yhi": 1 - d["yhi"]}))
    cross = send(other, route(lambda d: {"ylo": 1 - d["ylo"]}))
    cross_far = send(other, route(lambda d: {"ylo": 1 - d["ylo"], "yhi": 1 - d["yhi"]}))
    spread = send(lead[2:], route(lambda d: {"z": 3 - d["z"]}, lambda d: d["yhi"] == 0 and d["z"] < 2))
    lead_piece = jnp.where(z < 2, lead[:2], spread)
    spread = send(lead_piece, route(lambda d: {"yhi": 1}, lambda d: d["yhi"] == 0))
    lead_piece = jnp.where(yhi == 0, lead_piece, spread).reshape(4, BS, 128)

    blocks = [
        jnp.stack([mine, near]).reshape(4, BS, 128),
        jnp.stack([cross, cross_far]).reshape(4, BS, 128),
        lead_piece,
    ]
    ring = route(lambda d: {"z": d["z"] + (1 if d["core"] == 0 else -1)})
    rounds = [blocks]
    for _ in range(3):
        rounds.append([send(block, ring) for block in rounds[-1]])

    to_twin = route(
        lambda d: {"core": 1 - d["core"]}, lambda d: d["x"] == home(d) and d["core"] == d["z"] % 2
    )
    holder = core == z % 2
    units = []
    for own_child, cross_child, leads in rounds:
        kept = jnp.concatenate(
            [jnp.where(first, own_child, cross_child), jnp.where(first, leads[:2], leads[2:])]
        )
        given = jnp.concatenate(
            [jnp.where(first, cross_child, own_child), jnp.where(first, leads[2:], leads[:2])]
        )
        units.append(jnp.where(holder, kept, send(given, to_twin)))

    apart = (x - (2 * yhi + z // 2)) % 4
    apart = jnp.where(first, apart, (-apart) % 4)
    chain = []
    received = None
    for t in range(STEPS):
        if t == 0:
            now = units[0]
        elif t < 4:
            now = jnp.where(apart == 0, units[t], received)
        else:
            now = received
        chain.append(now)
        if t < STEPS - 1:
            received = send(
                now,
                route(
                    lambda d: {"x": d["x"] + (1 if d["core"] == 0 else -1)},
                    lambda d: away(d) < 3 and 0 <= t - away(d) <= 3,
                ),
            )
    swapped, twin, twin_swapped = [], [], []
    for t in range(STEPS):
        good = lambda d: 0 <= t - away(d) <= 3
        swapped.append(send(chain[t], route(lambda d: {"ylo": 1 - d["ylo"]}, good)))
        twin.append(send(chain[t], route(lambda d: {"core": 1 - d["core"]}, good)))
        twin_swapped.append(send(swapped[t], route(lambda d: {"core": 1 - d["core"]}, good)))

    factored, panel = finish_all(
        spot,
        child_listed,
        panel_listed,
        inv_diag,
        lead_all,
        flat,
        [piece for group in rounds for piece in group],
        [chain, swapped, twin, twin_swapped],
    )
    return factored.reshape(parent.shape), panel.reshape(4, 1, BS, 512)


def solution(mesh):
    grid = Mesh(mesh.devices.reshape(SIZES), AXES)
    row, col = ("ylo", "x", "core"), ("yhi", "z")
    return jax.shard_map(
        shards,
        mesh=grid,
        in_specs=(
            P(None, row, None, col),
            P(None, row, None, None, col, None),
            P(),
            P(),
            P(),
            P(),
        ),
        out_specs=(P(None, row, None, None, col, None), P(None, row, None, None)),
        check_vma=False,
    )
```

time: 655 us -> 327 us (0.50)
  waiting for transfers between devices: 513 us -> 157 us
  starting transfers between devices: 4.39 us -> 82 us
  Pallas kernels: 0 us -> 53.8 us
  local copies, waits for them, and re-layouts: 54.8 us -> 4.45 us
  matrix products: 34.3 us -> 0 us
  other arithmetic: 25.7 us -> 11.8 us
    ppermute x4 -> x45, waiting for transfers between devices: 222 us -> 78.4 us  [send(): return lax.ppermute(value, AXES, pairs)]
    psum x2 -> x1, waiting for transfers between devices: 216 us -> 78.6 us  [shards(): lax.psum(source, ('ylo', 'x'))]
    ppermute x4 -> x45, starting transfers between devices: 4.09 us -> 82 us  [send(): return lax.ppermute(value, AXES, pairs)]
    all_gather x1, waiting for transfers between devices: 74 us -> 0.01 us  [shards(): lax.all_gather(lax.psum(source, ('ylo', 'x')), ('core', 'yhi', 'z'))]
    pallas_call x0 -> x2, Pallas kernels: none -> 53.8 us  [the longest x1 51.4 us: finish_all(): pl.pallas_call(final_kernel, grid=(4,), out_shape=(jax.ShapeDtypeStruct((...]
    dot_general x3 -> x0, matrix products: 34.3 us -> none  [contract_rows(): lax.dot_general(left, right, (((1,), (1,)), ((), ())), precision=precise,...]
    unnamed x27 -> x48, local copies, waits for them, and re-layouts: 32.3 us -> 0.77 us
    gather x1 -> x0, local copies, waits for them, and re-layouts: 16.2 us -> none  [shards(): placed = own_rows[slab_ids, inverse]]
  transfers between devices with their start and end apart: 7 -> 47, of which waited for: 7 -> 13; matrix products, arithmetic and copies ran while one was open for 2% -> 4% of each run, Pallas kernels for 0% -> 1%
where the time goes in v1:
time: 327 us; the launch traced here: 324 us
  waiting for transfers between devices  157 us (48%)
  starting transfers between devices  82 us (25%)
  Pallas kernels  53.8 us (16%)
  between operations  14.7 us (4%)
  other arithmetic  11.8 us (4%)
  local copies, waits for them, and re-layouts  4.45 us (1%)
    ppermute x45, starting transfers between devices, send(): return lax.ppermute(value, AXES, pairs)  82 us
    psum x1, waiting for transfers between devices, shards(): lax.psum(source, ('ylo', 'x'))  78.6 us
    ppermute x45, waiting for transfers between devices, send(): return lax.ppermute(value, AXES, pairs)  78.4 us
    pallas_call x1, Pallas kernels, finish_all(): pl.pallas_call(final_kernel, grid=(4,), out_shape=(jax.ShapeDtypeStruct((...  51.4 us
  transfers between devices with their start and end apart: 47, of which 13 were waited for; matrix products, arithmetic and copies ran while one was open for 4% of the time, Pallas kernels for 1%

profile of v1, /device:TPU:66, one launch (start us, length us, event | category | flops | bytes accessed | tf_op | source)
XLA Modules:
  0.0 323.9 jit_solution(8637259460425148721)
XLA Ops:
  7.2 2.5 slice.71
  11.8 2.4 place.1
  15.3 2.5 collective-permute-start.2
  17.9 2.1 collective-permute-start
  20.0 5.3 %collective-permute-done.3 = f32[2,2,256,128]{3,2,1,0:T(8,128)S(1)} collective-permute-done((f32[2,2,256,128]{3,2,1,0:T(8,128)S(1)}, f32[2,2,256,128]{3,2,1,0:T(8,128)S(1)}, u32[]{:S(2)}, u32[]{:S(2)}) %collective-permute-start.3) | collective-permute-done | bytes 524320 | tf_op jit(solution)/shard_map/ppermute | solution.py:35
  28.1 2.6 collective-permute-start.6
  33.2 7.0 %collective-permute-done.4 = f32[2,2,256,128]{3,2,1,0:T(8,128)S(1)} collective-permute-done((f32[2,2,256,128]{3,2,1,0:T(8,128)S(1)}, f32[2,2,256,128]{3,2,1,0:T(8,128)S(1)}, u32[]{:S(2)}, u32[]{:S(2)}) %collective-permute-start.4) | collective-permute-done | bytes 524320 | tf_op jit(solution)/shard_map/ppermute | solution.py:35
  42.9 2.2 collective-permute-start.14
  45.1 2.0 collective-permute-start.9
  51.6 2.2 collective-permute-start.15
  55.8 3.6 %collective-permute-start.16 = (f32[6,256,128]{2,1,0:T(8,128)}, f32[6,256,128]{2,1,0:T(8,128)S(1)}, u32[]{:S(2)}, u32[]{:S(2)}) collective-permute-start(f32[6,256,128]{2,1,0:T(8,128)} %maximum_select_fusion.refs_12_), channel_id=1, source_target_pairs={{0,16},{1,17},{8,56},{9,57},{18,34},{19,35},{26,10},{27,11},{36,52... | collective-permute-start | bytes 2359304 | tf_op jit(solution)/shard_map/ppermute | solution.py:35
  59.6 5.0 %collective-permute-start.12 = (f32[4,256,128]{2,1,0:T(8,128)}, f32[4,256,128]{2,1,0:T(8,128)S(1)}, u32[]{:S(2)}, u32[]{:S(2)}) collective-permute-start(f32[4,256,128]{2,1,0:T(8,128)} %collective-permute-done.9.refs_7_), channel_id=1, source_target_pairs={{0,1},{1,2},{2,3},{3,0},{4,5},{5,6},{6,7},{7,4},{8,11},{9,8},{10,9... | collective-permute-start | bytes 1572872 | tf_op jit(solution)/shard_map/ppermute | solution.py:35
  67.6 2.6 collective-permute-start.17
  71.1 2.9 collective-permute-start.18
  74.0 3.6 %collective-permute-done.11.refs_9_ = f32[4,256,128]{2,1,0:T(8,128)S(1)} collective-permute-done((f32[4,256,128]{2,1,0:T(8,128)}, f32[4,256,128]{2,1,0:T(8,128)S(1)}, u32[]{:S(2)}, u32[]{:S(2)}) %collective-permute-start.11) | collective-permute-done | bytes 524320 | tf_op jit(solution)/shard_map/ppermute | solution.py:35
  77.7 5.5 %collective-permute-done.13.refs_11_ = f32[4,256,128]{2,1,0:T(8,128)S(1)} collective-permute-done((f32[4,256,128]{2,1,0:T(8,128)}, f32[4,256,128]{2,1,0:T(8,128)S(1)}, u32[]{:S(2)}, u32[]{:S(2)}) %collective-permute-start.13) | collective-permute-done | bytes 524320 | tf_op jit(solution)/shard_map/ppermute | solution.py:35
  83.3 3.3 %collective-permute-start.19 = (f32[6,256,128]{2,1,0:T(8,128)S(1)}, f32[6,256,128]{2,1,0:T(8,128)}, u32[]{:S(2)}, u32[]{:S(2)}) collective-permute-start(f32[6,256,128]{2,1,0:T(8,128)S(1)} %pad_maximum_fusion.3), channel_id=1, source_target_pairs={{0,8},{9,1},{18,26},{27,19},{36,44},{45,37},{54,62},{63,55},{64,72... | collective-permute-start | bytes 2359304 | tf_op jit(solution)/shard_map/ppermute | solution.py:35
  87.6 2.6 collective-permute-start.20
  91.9 78.6 %all-reduce.2.cloned.1.call-done = f32[1,256,128]{2,1,0:T(8,128)} async-done(((f32[1,256,128]{2,1,0:T(8,128)}), f32[1,256,128]{2,1,0:T(8,128)}) %all-reduce.2.cloned.1.call-update) | async-done | bytes 131088 | tf_op jit(solution)/shard_map/psum | solution.py:305
  170.5 1.9 collective-permute-start.31
  172.4 2.5 collective-permute-start.24
  174.9 3.3 %collective-permute-start.25 = (f32[6,256,128]{2,1,0:T(8,128)}, f32[6,256,128]{2,1,0:T(8,128)S(1)}, u32[]{:S(2)}, u32[]{:S(2)}) collective-permute-start(f32[6,256,128]{2,1,0:T(8,128)} %copy-done.4), channel_id=1, source_target_pairs={{0,64},{1,65},{6,70},{7,71},{8,72},{9,73},{10,74},{11,75},{16,80},... | collective-permute-start | bytes 2359304 | tf_op jit(solution)/shard_map/ppermute | solution.py:35
  180.3 15.9 %collective-permute-done.24.refs_19_ = f32[6,256,128]{2,1,0:T(8,128)S(1)} collective-permute-done((f32[6,256,128]{2,1,0:T(8,128)}, f32[6,256,128]{2,1,0:T(8,128)S(1)}, u32[]{:S(2)}, u32[]{:S(2)}) %collective-permute-start.24) | collective-permute-done | bytes 786464 | tf_op jit(solution)/shard_map/ppermute | solution.py:35
  198.2 2.4 collective-permute-start.32
  200.6 2.5 collective-permute-start.26
  203.1 14.5 %collective-permute-done.25.refs_20_ = f32[6,256,128]{2,1,0:T(8,128)S(1)} collective-permute-done((f32[6,256,128]{2,1,0:T(8,128)}, f32[6,256,128]{2,1,0:T(8,128)S(1)}, u32[]{:S(2)}, u32[]{:S(2)}) %collective-permute-start.25) | collective-permute-done | bytes 786464 | tf_op jit(solution)/shard_map/ppermute | solution.py:35
  217.7 1.9 collective-permute-start.39
  221.8 2.1 collective-permute-start.33
  224.0 11.6 %collective-permute-done.26.refs_21_ = f32[6,256,128]{2,1,0:T(8,128)S(1)} collective-permute-done((f32[6,256,128]{2,1,0:T(8,128)}, f32[6,256,128]{2,1,0:T(8,128)S(1)}, u32[]{:S(2)}, u32[]{:S(2)}) %collective-permute-start.26) | collective-permute-done | bytes 786464 | tf_op jit(solution)/shard_map/ppermute | solution.py:35
  235.6 1.9 collective-permute-start.40
  239.7 12.3 %collective-permute-done.27.refs_22_ = f32[6,256,128]{2,1,0:T(8,128)S(1)} collective-permute-done((f32[6,256,128]{2,1,0:T(8,128)S(1)}, f32[6,256,128]{2,1,0:T(8,128)S(1)}, u32[]{:S(2)}, u32[]{:S(2)}) %collective-permute-start.27) | collective-permute-done | bytes 786464 | tf_op jit(solution)/shard_map/ppermute | solution.py:35
  265.6 51.4 %finish.1 = (f32[16384,128]{1,0:T(8,128)}, f32[4,256,512]{2,1,0:T(8,128)}) custom-call(s32[5]{0:T(128)S(1)} %stack.38.spot, s32[2,32,32]{2,1,0:T(8,128)S(1)} %copy-done.2, s32[64,64]{1,0:T(8,128)S(1)} %copy-done.3, f32[512,512]{1,0:T(8,128)} %inv.1, f32[2,8,256,128]{3,2,1,0:T(8,128)} %bitcast.55, f32[16384,128]{1,0:T(8,128)} %bitcast.53, ...), custom_call_target="tpu_custom_call" | custom-call | flops 22000001024 | bytes 36000000 | tf_op jit(solution)/shard_map/finish/pallas_call | solution.py:252
  (140 shorter events, 46.2 us)
Async XLA Ops:
  7.2 163.3 %all-reduce.2.cloned.1.call-start = ((), (), s32[]{:S(2)}) async-start(), calls=%async_computation | async-start | bytes 262144 | tf_op jit(solution)/shard_map/psum | solution.py:305
  9.8 15.6 %collective-permute-start.3 = (f32[2,2,256,128]{3,2,1,0:T(8,128)S(1)}, f32[2,2,256,128]{3,2,1,0:T(8,128)S(1)}, u32[]{:S(2)}, u32[]{:S(2)}) collective-permute-start(f32[2,2,256,128]{3,2,1,0:T(8,128)S(1)} %slice.73), channel_id=1, source_target_pairs={{0,3},{1,2},{8,11},{9,10},{16,19},{17,18},{24,27},{25,26},{32,35},... | collective-permute-start | bytes 1572872 | tf_op jit(solution)/shard_map/ppermute | solution.py:35
  17.9 13.5 %collective-permute-start = (f32[2,256,128]{2,1,0:T(8,128)S(1)}, f32[2,256,128]{2,1,0:T(8,128)S(1)}, u32[]{:S(2)}, u32[]{:S(2)}) collective-permute-start(f32[2,256,128]{2,1,0:T(8,128)S(1)} %get-tuple-element.29), channel_id=1, source_target_pairs={{0,4},{1,5},{2,6},{3,7},{4,0},{5,1},{6,2},{7,3},{8,12},{9,13},{10,... | collective-permute-start | bytes 786440 | tf_op jit(solution)/shard_map/ppermute | solution.py:35
  25.4 14.8 %collective-permute-start.4 = (f32[2,2,256,128]{3,2,1,0:T(8,128)S(1)}, f32[2,2,256,128]{3,2,1,0:T(8,128)S(1)}, u32[]{:S(2)}, u32[]{:S(2)}) collective-permute-start(f32[2,2,256,128]{3,2,1,0:T(8,128)S(1)} %slice_select_fusion), channel_id=1, source_target_pairs={{0,4},{1,5},{2,6},{3,7},{8,12},{9,13},{10,14},{11,15},{16,20},{17,... | collective-permute-start | bytes 1572872 | tf_op jit(solution)/shard_map/ppermute | solution.py:35
  28.1 17.0 %collective-permute-start.6 = (f32[4,256,128]{2,1,0:T(8,128)S(1)}, f32[4,256,128]{2,1,0:T(8,128)}, u32[]{:S(2)}, u32[]{:S(2)}) collective-permute-start(f32[4,256,128]{2,1,0:T(8,128)S(1)} %bitcast.41), channel_id=1, source_target_pairs={{0,1},{1,2},{2,3},{3,0},{4,5},{5,6},{6,7},{7,4},{8,11},{9,8},{10,9... | collective-permute-start | bytes 1572872 | tf_op jit(solution)/shard_map/ppermute | solution.py:35
  31.4 15.7 %collective-permute-start.5 = (f32[4,256,128]{2,1,0:T(8,128)S(1)}, f32[4,256,128]{2,1,0:T(8,128)}, u32[]{:S(2)}, u32[]{:S(2)}) collective-permute-start(f32[4,256,128]{2,1,0:T(8,128)S(1)} %bitcast.43), channel_id=1, source_target_pairs={{0,1},{1,2},{2,3},{3,0},{4,5},{5,6},{6,7},{7,4},{8,11},{9,8},{10,9... | collective-permute-start | bytes 1572872 | tf_op jit(solution)/shard_map/ppermute | solution.py:35
  45.1 14.4 %collective-permute-start.9 = (f32[4,256,128]{2,1,0:T(8,128)}, f32[4,256,128]{2,1,0:T(8,128)}, u32[]{:S(2)}, u32[]{:S(2)}) collective-permute-start(f32[4,256,128]{2,1,0:T(8,128)} %collective-permute-done.6.refs_4_), channel_id=1, source_target_pairs={{0,1},{1,2},{2,3},{3,0},{4,5},{5,6},{6,7},{7,4},{8,11},{9,8},{10,9... | collective-permute-start | bytes 1572872 | tf_op jit(solution)/shard_map/ppermute | solution.py:35
  47.1 17.4 %collective-permute-start.8 = (f32[4,256,128]{2,1,0:T(8,128)}, f32[4,256,128]{2,1,0:T(8,128)}, u32[]{:S(2)}, u32[]{:S(2)}) collective-permute-start(f32[4,256,128]{2,1,0:T(8,128)} %collective-permute-done.5.refs_3_), channel_id=1, source_target_pairs={{0,1},{1,2},{2,3},{3,0},{4,5},{5,6},{6,7},{7,4},{8,11},{9,8},{10,9... | collective-permute-start | bytes 1572872 | tf_op jit(solution)/shard_map/ppermute | solution.py:35
  51.6 18.7 %collective-permute-start.15 = (f32[6,256,128]{2,1,0:T(8,128)}, f32[6,256,128]{2,1,0:T(8,128)}, u32[]{:S(2)}, u32[]{:S(2)}) collective-permute-start(f32[6,256,128]{2,1,0:T(8,128)} %pad_maximum_fusion.1), channel_id=1, source_target_pairs={{0,8},{9,1},{18,26},{27,19},{36,44},{45,37},{54,62},{63,55},{64,72... | collective-permute-start | bytes 2359304 | tf_op jit(solution)/shard_map/ppermute | solution.py:35
  55.8 15.1 %collective-permute-start.16 = (f32[6,256,128]{2,1,0:T(8,128)}, f32[6,256,128]{2,1,0:T(8,128)S(1)}, u32[]{:S(2)}, u32[]{:S(2)}) collective-permute-start(f32[6,256,128]{2,1,0:T(8,128)} %maximum_select_fusion.refs_12_), channel_id=1, source_target_pairs={{0,16},{1,17},{8,56},{9,57},{18,34},{19,35},{26,10},{27,11},{36,52... | collective-permute-start | bytes 2359304 | tf_op jit(solution)/shard_map/ppermute | solution.py:35
  59.6 14.4 %collective-permute-start.12 = (f32[4,256,128]{2,1,0:T(8,128)}, f32[4,256,128]{2,1,0:T(8,128)S(1)}, u32[]{:S(2)}, u32[]{:S(2)}) collective-permute-start(f32[4,256,128]{2,1,0:T(8,128)} %collective-permute-done.9.refs_7_), channel_id=1, source_target_pairs={{0,1},{1,2},{2,3},{3,0},{4,5},{5,6},{6,7},{7,4},{8,11},{9,8},{10,9... | collective-permute-start | bytes 1572872 | tf_op jit(solution)/shard_map/ppermute | solution.py:35
  64.6 13.0 %collective-permute-start.11 = (f32[4,256,128]{2,1,0:T(8,128)}, f32[4,256,128]{2,1,0:T(8,128)S(1)}, u32[]{:S(2)}, u32[]{:S(2)}) collective-permute-start(f32[4,256,128]{2,1,0:T(8,128)} %collective-permute-done.8.refs_6_), channel_id=1, source_target_pairs={{0,1},{1,2},{2,3},{3,0},{4,5},{5,6},{6,7},{7,4},{8,11},{9,8},{10,9... | collective-permute-start | bytes 1572872 | tf_op jit(solution)/shard_map/ppermute | solution.py:35
  67.6 19.0 %collective-permute-start.17 = (f32[6,256,128]{2,1,0:T(8,128)S(1)}, f32[6,256,128]{2,1,0:T(8,128)S(1)}, u32[]{:S(2)}, u32[]{:S(2)}) collective-permute-start(f32[6,256,128]{2,1,0:T(8,128)S(1)} %pad_maximum_fusion.2), channel_id=1, source_target_pairs={{0,8},{9,1},{18,26},{27,19},{36,44},{45,37},{54,62},{63,55},{64,72... | collective-permute-start | bytes 2359304 | tf_op jit(solution)/shard_map/ppermute | solution.py:35
  70.3 12.9 %collective-permute-start.13 = (f32[4,256,128]{2,1,0:T(8,128)}, f32[4,256,128]{2,1,0:T(8,128)S(1)}, u32[]{:S(2)}, u32[]{:S(2)}) collective-permute-start(f32[4,256,128]{2,1,0:T(8,128)} %collective-permute-done.10.refs_8_), channel_id=1, source_target_pairs={{0,1},{1,2},{2,3},{3,0},{4,5},{5,6},{6,7},{7,4},{8,11},{9,8},{10,9... | collective-permute-start | bytes 1572872 | tf_op jit(solution)/shard_map/ppermute | solution.py:35
  71.1 15.5 %collective-permute-start.18 = (f32[6,256,128]{2,1,0:T(8,128)S(1)}, f32[6,256,128]{2,1,0:T(8,128)S(1)}, u32[]{:S(2)}, u32[]{:S(2)}) collective-permute-start(f32[6,256,128]{2,1,0:T(8,128)S(1)} %fusion.refs_13_), channel_id=1, source_target_pairs={{0,16},{1,17},{6,22},{7,23},{8,56},{9,57},{10,58},{11,59},{16,32},... | collective-permute-start | bytes 2359304 | tf_op jit(solution)/shard_map/ppermute | solution.py:35
  83.3 95.0 %collective-permute-start.19 = (f32[6,256,128]{2,1,0:T(8,128)S(1)}, f32[6,256,128]{2,1,0:T(8,128)}, u32[]{:S(2)}, u32[]{:S(2)}) collective-permute-start(f32[6,256,128]{2,1,0:T(8,128)S(1)} %pad_maximum_fusion.3), channel_id=1, source_target_pairs={{0,8},{9,1},{18,26},{27,19},{36,44},{45,37},{54,62},{63,55},{64,72... | collective-permute-start | bytes 2359304 | tf_op jit(solution)/shard_map/ppermute | solution.py:35
  87.6 90.7 %collective-permute-start.20 = (f32[6,256,128]{2,1,0:T(8,128)}, f32[6,256,128]{2,1,0:T(8,128)}, u32[]{:S(2)}, u32[]{:S(2)}) collective-permute-start(f32[6,256,128]{2,1,0:T(8,128)} %fusion.1.refs_14_), channel_id=1, source_target_pairs={{0,16},{1,17},{4,20},{5,21},{6,22},{7,23},{8,56},{9,57},{10,58},{1... | collective-permute-start | bytes 2359304 | tf_op jit(solution)/shard_map/ppermute | solution.py:35
  91.8 173.7 %all-gather.2.cloned.1.call-start = ((), (), s32[]{:S(2)}) async-start(), calls=%async_computation.1 | async-start | bytes 2228224 | tf_op jit(solution)/shard_map/all_gather | solution.py:305
  170.5 30.1 %collective-permute-start.31 = (f32[6,256,128]{2,1,0:T(8,128)}, f32[6,256,128]{2,1,0:T(8,128)S(1)}, u32[]{:S(2)}, u32[]{:S(2)}) collective-permute-start(f32[6,256,128]{2,1,0:T(8,128)} %maximum_select_fusion.refs_12_), channel_id=1, source_target_pairs={{0,8},{1,9},{8,0},{9,1},{18,26},{19,27},{26,18},{27,19},{36,44},{3... | collective-permute-start | bytes 2359304 | tf_op jit(solution)/shard_map/ppermute | solution.py:35
  172.4 23.8 %collective-permute-start.24 = (f32[6,256,128]{2,1,0:T(8,128)}, f32[6,256,128]{2,1,0:T(8,128)S(1)}, u32[]{:S(2)}, u32[]{:S(2)}) collective-permute-start(f32[6,256,128]{2,1,0:T(8,128)} %maximum_select_fusion.refs_12_), channel_id=1, source_target_pairs={{0,64},{1,65},{8,72},{9,73},{18,82},{19,83},{26,90},{27,91},{36,10... | collective-permute-start | bytes 2359304 | tf_op jit(solution)/shard_map/ppermute | solution.py:35
  174.9 42.7 %collective-permute-start.25 = (f32[6,256,128]{2,1,0:T(8,128)}, f32[6,256,128]{2,1,0:T(8,128)S(1)}, u32[]{:S(2)}, u32[]{:S(2)}) collective-permute-start(f32[6,256,128]{2,1,0:T(8,128)} %copy-done.4), channel_id=1, source_target_pairs={{0,64},{1,65},{6,70},{7,71},{8,72},{9,73},{10,74},{11,75},{16,80},... | collective-permute-start | bytes 2359304 | tf_op jit(solution)/shard_map/ppermute | solution.py:35
  178.4 41.1 %collective-permute-start.21 = (f32[6,256,128]{2,1,0:T(8,128)S(1)}, f32[6,256,128]{2,1,0:T(8,128)S(1)}, u32[]{:S(2)}, u32[]{:S(2)}) collective-permute-start(f32[6,256,128]{2,1,0:T(8,128)S(1)} %fusion.2.refs_15_), channel_id=1, source_target_pairs={{0,16},{1,17},{4,20},{5,21},{6,22},{7,23},{8,56},{9,57},{10,58},{1... | collective-permute-start | bytes 2359304 | tf_op jit(solution)/shard_map/ppermute | solution.py:35
  196.3 24.9 %collective-permute-start.38 = (f32[6,256,128]{2,1,0:T(8,128)S(1)}, f32[6,256,128]{2,1,0:T(8,128)S(1)}, u32[]{:S(2)}, u32[]{:S(2)}) collective-permute-start(f32[6,256,128]{2,1,0:T(8,128)S(1)} %collective-permute-done.24.refs_19_), channel_id=1, source_target_pairs={{0,8},{1,9},{8,0},{9,1},{18,26},{19,27},{26,18},{27,19},{36,44},{3... | collective-permute-start | bytes 2359304 | tf_op jit(solution)/shard_map/ppermute | solution.py:35
  198.2 23.7 %collective-permute-start.32 = (f32[6,256,128]{2,1,0:T(8,128)}, f32[6,256,128]{2,1,0:T(8,128)S(1)}, u32[]{:S(2)}, u32[]{:S(2)}) collective-permute-start(f32[6,256,128]{2,1,0:T(8,128)} %copy-done.4), channel_id=1, source_target_pairs={{0,8},{1,9},{6,14},{7,15},{8,0},{9,1},{10,2},{11,3},{16,24},{17,25... | collective-permute-start | bytes 2359304 | tf_op jit(solution)/shard_map/ppermute | solution.py:35
  200.6 35.0 %collective-permute-start.26 = (f32[6,256,128]{2,1,0:T(8,128)}, f32[6,256,128]{2,1,0:T(8,128)S(1)}, u32[]{:S(2)}, u32[]{:S(2)}) collective-permute-start(f32[6,256,128]{2,1,0:T(8,128)} %fusion.1.refs_14_), channel_id=1, source_target_pairs={{0,64},{1,65},{4,68},{5,69},{6,70},{7,71},{8,72},{9,73},{10,74},{1... | collective-permute-start | bytes 2359304 | tf_op jit(solution)/shard_map/ppermute | solution.py:35
  217.7 19.8 %collective-permute-start.39 = (f32[6,256,128]{2,1,0:T(8,128)S(1)}, f32[6,256,128]{2,1,0:T(8,128)S(1)}, u32[]{:S(2)}, u32[]{:S(2)}) collective-permute-start(f32[6,256,128]{2,1,0:T(8,128)S(1)} %collective-permute-done.25.refs_20_), channel_id=1, source_target_pairs={{0,8},{1,9},{6,14},{7,15},{8,0},{9,1},{10,2},{11,3},{16,24},{17,25... | collective-permute-start | bytes 2359304 | tf_op jit(solution)/shard_map/ppermute | solution.py:35
  219.6 18.5 %collective-permute-start.22 = (f32[6,256,128]{2,1,0:T(8,128)S(1)}, f32[6,256,128]{2,1,0:T(8,128)}, u32[]{:S(2)}, u32[]{:S(2)}) collective-permute-start(f32[6,256,128]{2,1,0:T(8,128)S(1)} %collective-permute-done.21.refs_16_), channel_id=1, source_target_pairs={{4,20},{5,21},{6,22},{7,23},{10,58},{11,59},{12,60},{13,61},{16,32... | collective-permute-start | bytes 2359304 | tf_op jit(solution)/shard_map/ppermute | solution.py:35
  221.1 30.9 %collective-permute-start.27 = (f32[6,256,128]{2,1,0:T(8,128)S(1)}, f32[6,256,128]{2,1,0:T(8,128)S(1)}, u32[]{:S(2)}, u32[]{:S(2)}) collective-permute-start(f32[6,256,128]{2,1,0:T(8,128)S(1)} %fusion.2.refs_15_), channel_id=1, source_target_pairs={{0,64},{1,65},{2,66},{3,67},{4,68},{5,69},{6,70},{7,71},{8,72},{9,... | collective-permute-start | bytes 2359304 | tf_op jit(solution)/shard_map/ppermute | solution.py:35
  221.8 30.2 %collective-permute-start.33 = (f32[6,256,128]{2,1,0:T(8,128)}, f32[6,256,128]{2,1,0:T(8,128)S(1)}, u32[]{:S(2)}, u32[]{:S(2)}) collective-permute-start(f32[6,256,128]{2,1,0:T(8,128)} %fusion.1.refs_14_), channel_id=1, source_target_pairs={{0,8},{1,9},{4,12},{5,13},{6,14},{7,15},{8,0},{9,1},{10,2},{11,3},... | collective-permute-start | bytes 2359304 | tf_op jit(solution)/shard_map/ppermute | solution.py:35
  235.6 18.0 %collective-permute-start.40 = (f32[6,256,128]{2,1,0:T(8,128)S(1)}, f32[6,256,128]{2,1,0:T(8,128)S(1)}, u32[]{:S(2)}, u32[]{:S(2)}) collective-permute-start(f32[6,256,128]{2,1,0:T(8,128)S(1)} %collective-permute-done.26.refs_21_), channel_id=1, source_target_pairs={{0,8},{1,9},{4,12},{5,13},{6,14},{7,15},{8,0},{9,1},{10,2},{11,3},... | collective-permute-start | bytes 2359304 | tf_op jit(solution)/shard_map/ppermute | solution.py:35
  237.5 16.8 %collective-permute-start.34 = (f32[6,256,128]{2,1,0:T(8,128)S(1)}, f32[6,256,128]{2,1,0:T(8,128)S(1)}, u32[]{:S(2)}, u32[]{:S(2)}) collective-permute-start(f32[6,256,128]{2,1,0:T(8,128)S(1)} %fusion.2.refs_15_), channel_id=1, source_target_pairs={{0,8},{1,9},{2,10},{3,11},{4,12},{5,13},{6,14},{7,15},{8,0},{9,1},... | collective-permute-start | bytes 2359304 | tf_op jit(solution)/shard_map/ppermute | solution.py:35
  238.1 17.9 %collective-permute-start.23 = (f32[6,256,128]{2,1,0:T(8,128)}, f32[6,256,128]{2,1,0:T(8,128)}, u32[]{:S(2)}, u32[]{:S(2)}) collective-permute-start(f32[6,256,128]{2,1,0:T(8,128)} %collective-permute-done.22.refs_17_), channel_id=1, source_target_pairs={{4,20},{5,21},{12,60},{13,61},{22,38},{23,39},{30,14},{31,15},{32,... | collective-permute-start | bytes 2359304 | tf_op jit(solution)/shard_map/ppermute | solution.py:35
  (38 other events, 1132.7 us)
Sparse Core Ops, SparseCore 0:
  91.9 78.4 all-reduce.1
  173.2 50.9 all-gather.1

commit v2 on v0

v2 whole, which is shorter than its diff:
```python
import functools
import itertools
import jax
import jax.numpy as jnp
from jax import lax
from jax.experimental import pallas as pl
from jax.experimental.pallas import tpu as pltpu
from jax.sharding import Mesh, PartitionSpec as P

BS = 256
AXES = ("ylo", "x", "core", "yhi", "z")
SIZES = (2, 4, 2, 2, 4)
NT = (((1,), (1,)), ((), ()))


def route(move, keep=lambda dev: True):
    pairs = []
    for spot in itertools.product(*[range(n) for n in SIZES]):
        dev = dict(zip(AXES, spot))
        if not keep(dev):
            continue
        far = dict(dev)
        far.update(move(dev))
        flat = []
        for d in (dev, far):
            i = 0
            for a, n in zip(AXES, SIZES):
                i = i * n + d[a] % n
            flat.append(i)
        pairs.append(tuple(flat))
    return pairs


def send(value, pairs):
    return lax.ppermute(value, AXES, pairs)


def home(dev):
    return 2 * dev["yhi"] + dev["z"] // 2


def away(dev):
    apart = dev["x"] - home(dev)
    return (apart if dev["core"] == 0 else -apart) % 4


def halves(value):
    high = value.astype(jnp.bfloat16)
    return high, (value - high.astype(jnp.float32)).astype(jnp.bfloat16)


def mul3(ah, al, bh, bl):
    def dot(u, v):
        return lax.dot_general(u, v, NT, preferred_element_type=jnp.float32)

    return dot(ah, bh) + (dot(ah, bl) + dot(al, bh))


def place_kernel(where, own, maps, out, token):
    half = where[0]
    token[...] = jnp.zeros_like(token)
    for s in range(4):
        spots = lax.broadcasted_iota(jnp.int32, (BS, BS), 0)
        pick = jnp.where(spots == maps[s, :][None, :], 1.0, 0.0).astype(jnp.bfloat16)
        value = own[s]
        total = None
        for _ in range(3):
            part = value.astype(jnp.bfloat16)
            value = value - part.astype(jnp.float32)
            moved = jnp.dot(pick, part, preferred_element_type=jnp.float32)
            total = moved if total is None else total + moved
        out[lax.rem(half + s, 2), s // 2] = total


def place(half, own, maps):
    return pl.pallas_call(
        place_kernel,
        out_shape=(
            jax.ShapeDtypeStruct((2, 2, BS, 128), jnp.float32),
            jax.ShapeDtypeStruct((8, 128), jnp.float32),
        ),
        in_specs=[
            pl.BlockSpec(memory_space=pltpu.SMEM),
            pl.BlockSpec(memory_space=pltpu.VMEM),
            pl.BlockSpec(memory_space=pltpu.VMEM),
        ],
        out_specs=[pl.BlockSpec(memory_space=pltpu.VMEM)] * 2,
        name="place",
    )(half, own, maps)


def rows_kernel(spot, child_mask, inv, *refs):
    gathered = refs[0:4]
    leads = refs[4:8]
    edge_twin = refs[8]
    panel, to_send, rh, rl, ph, pll = refs[9:15]
    eh, el, lead, vh, vl = refs[15:]
    p, x, core, yhi, z = (spot[n] for n in range(5))
    q = 2 * x + core
    turn = jnp.where(core == 0, 1, 3)

    a, b = halves(inv[...])
    vh[...] = a
    vl[...] = b
    for k in range(4):
        own_z = lax.rem(z + 16 - turn * k, 4)
        twin_z = lax.rem(z + turn * k, 4)
        for yr in range(2):
            y_at = lax.rem(yhi + yr, 2)
            start = pl.multiple_of(own_z * 256 + y_at * 128, 128)
            for lane in range(2):
                child = lax.rem(p + lane, 2)
                for i in range(2):
                    a, b = halves(gathered[k][lane * 4 + yr * 2 + i])
                    rh[child * 2 + i, :, pl.ds(start, 128)] = a
                    rl[child * 2 + i, :, pl.ds(start, 128)] = b
            a, b = halves(leads[k][4 + yr])
            eh[core, :, pl.ds(start, 128)] = a
            el[core, :, pl.ds(start, 128)] = b
            start = pl.multiple_of(twin_z * 256 + y_at * 128, 128)
            a, b = halves(edge_twin[k * 2 + yr])
            eh[1 - core, :, pl.ds(start, 128)] = a
            el[1 - core, :, pl.ds(start, 128)] = b
        right = jnp.logical_or(own_z == 1, own_z == 2).astype(jnp.int32)
        for lane in range(2):
            at = jnp.where(own_z >= 2, 2, 0) + lane
            for half in range(2):
                start = pl.multiple_of(right * 256 + half * 128, 128)
                lead[at, :, pl.ds(start, 128)] = leads[k][lane * 2 + half]

    for j in range(2):
        change = mul3(
            rh[0:2].reshape(512, 1024), rl[0:2].reshape(512, 1024), eh[j], el[j]
        )
        for i in range(2):
            listed = child_mask[0, (p + 2 * i) * 8 + q, j] == 1
            part = change[i * 256 : i * 256 + 256]
            lead[i, :, j * 256 : j * 256 + 256] -= jnp.where(listed, part, 0.0)

    for pair in range(2):
        ah, al = halves(lead[2 * pair : 2 * pair + 2].reshape(512, 512))
        left = mul3(ah[:, :256], al[:, :256], vh[:256, :256], vl[:256, :256])
        right = mul3(ah, al, vh[256:, :], vl[256:, :])
        for half, value in enumerate((left, right)):
            a, b = halves(value)
            cols = slice(half * 256, half * 256 + 256)
            for i in range(2):
                rows = slice(i * 256, i * 256 + 256)
                panel[2 * pair + i, :, cols] = value[rows]
                ph[2 * pair + i, :, cols] = a[rows]
                pll[2 * pair + i, :, cols] = b[rows]
                for n in range(2):
                    to_send[2 * pair + i, 2 * half + n] = value[rows, n * 128 : n * 128 + 128]


def rows_step(spot, child_mask, inv, gathered, leads, edge_twin):
    f32, bf16 = jnp.float32, jnp.bfloat16
    vmem = pl.BlockSpec(memory_space=pltpu.VMEM)
    smem = pl.BlockSpec(memory_space=pltpu.SMEM)
    return pl.pallas_call(
        rows_kernel,
        out_shape=(
            jax.ShapeDtypeStruct((4, BS, 512), f32),
            jax.ShapeDtypeStruct((4, 4, BS, 128), f32),
            jax.ShapeDtypeStruct((4, BS, 1024), bf16),
            jax.ShapeDtypeStruct((4, BS, 1024), bf16),
            jax.ShapeDtypeStruct((4, BS, 512), bf16),
            jax.ShapeDtypeStruct((4, BS, 512), bf16),
        ),
        in_specs=[smem, smem] + [vmem] * 10,
        out_specs=[vmem] * 6,
        scratch_shapes=[
            pltpu.VMEM((2, BS, 1024), bf16),
            pltpu.VMEM((2, BS, 1024), bf16),
            pltpu.VMEM((4, BS, 512), f32),
            pltpu.VMEM((512, 512), bf16),
            pltpu.VMEM((512, 512), bf16),
        ],
        compiler_params=pltpu.CompilerParams(vmem_limit_bytes=40 * 1024 * 1024),
        cost_estimate=pl.CostEstimate(flops=4_000_000_000, bytes_accessed=18_000_000, transcendentals=0),
        name="rows",
    )(spot, child_mask, inv, *gathered, *leads, edge_twin)


def update_kernel(spot, child_mask, parent, rh, rl, *refs):
    arrays, (out, ch, cl, acc) = refs[:8], refs[8:]
    p, x, core, yhi, z = (spot[n] for n in range(5))
    q = 2 * x + core
    c = 4 * yhi + z
    slot = pl.program_id(0)

    @pl.when(slot == 0)
    def _():
        for n in range(8):
            lane = core if n < 4 else 1 - core
            z_from = lax.rem(z + x + (0, 1, 3, 2)[n % 4] - (2 * yhi + z // 2) + 4, 4)
            for part in range(2):
                plane = p if part == 0 else 1 - p
                child = lax.rem(plane + lane, 2)
                for yr in range(2):
                    start = pl.multiple_of(z_from * 256 + lax.rem(yhi + yr, 2) * 128, 128)
                    for i in range(2):
                        a, b = halves(arrays[n][part * 4 + yr * 2 + i])
                        ch[child * 4 + plane + 2 * i, :, pl.ds(start, 128)] = a
                        cl[child * 4 + plane + 2 * i, :, pl.ds(start, 128)] = b

    for j in range(8):
        touched = j < 6
        for half in range(2):
            at = pl.ds(2 * j + half, BS, stride=16)
            if touched:
                acc[:, half * 128 : half * 128 + 128] = parent[at, :]
            else:
                out[at, :] = parent[at, :]
        if not touched:
            continue
        for child in range(2):
            s = j - 2 * child
            if s < 0 or s >= 4:
                continue
            i = jnp.clip(slot - child, 0, 1)
            listed = child_mask[child, (p + 2 * i) * 8 + q, s * 8 + c] == 1

            @pl.when(jnp.logical_and(listed, slot - child == i))
            def _():
                acc[...] -= mul3(
                    rh[child * 2 + i], rl[child * 2 + i], ch[child * 4 + s], cl[child * 4 + s]
                )

        for half in range(2):
            out[pl.ds(2 * j + half, BS, stride=16), :] = acc[:, half * 128 : half * 128 + 128]


def update_step(spot, child_mask, flat, rh, rl, arrays):
    vmem = pl.BlockSpec(memory_space=pltpu.VMEM)
    smem = pl.BlockSpec(memory_space=pltpu.SMEM)
    block = pl.BlockSpec((BS * 16, 128), lambda i: (i, 0))
    return pl.pallas_call(
        update_kernel,
        grid=(4,),
        out_shape=jax.ShapeDtypeStruct(flat.shape, jnp.float32),
        in_specs=[smem, smem, block] + [vmem] * (2 + len(arrays)),
        out_specs=block,
        scratch_shapes=[
            pltpu.VMEM((8, BS, 1024), jnp.bfloat16),
            pltpu.VMEM((8, BS, 1024), jnp.bfloat16),
            pltpu.VMEM((BS, BS), jnp.float32),
        ],
        compiler_params=pltpu.CompilerParams(vmem_limit_bytes=40 * 1024 * 1024),
        cost_estimate=pl.CostEstimate(flops=6_400_000_000, bytes_accessed=28_000_000, transcendentals=0),
        name="update",
    )(spot, child_mask, flat, rh, rl, *arrays)


def trail_kernel(spot, panel_mask, assembled, ph, pll, *refs):
    arrays, (out, qh, ql) = refs[:8], refs[8:]
    p, x, core, yhi, z = (spot[n] for n in range(5))
    r = 8 * p + 2 * x + core
    c = 4 * yhi + z
    right, slot = pl.program_id(0), pl.program_id(1)

    @pl.when(jnp.logical_and(right == 0, slot == 0))
    def _():
        for n in range(8):
            lane = core if n < 4 else 1 - core
            from_slot = lax.rem(x + (0, 1, 3, 2)[n % 4] - (2 * yhi + z // 2) + 4, 4)
            for part in range(2):
                plane = p if part == 0 else 1 - p
                for half in range(2):
                    start = pl.multiple_of(lane * 256 + half * 128, 128)
                    a, b = halves(arrays[n][part * 2 + half])
                    qh[plane * 4 + from_slot, :, pl.ds(start, 128)] = a
                    ql[plane * 4 + from_slot, :, pl.ds(start, 128)] = b

    row_block = 16 * slot + r
    for jj in range(4):
        j = 4 * right + jj
        col_block = 8 * j + c
        n = lax.rem(j, 2) * 4 + j // 2
        use = jnp.logical_and(row_block >= 2, col_block >= 2)
        use = jnp.logical_and(use, panel_mask[row_block, col_block] == 1)

        @pl.when(use)
        def _():
            product = mul3(ph[slot], pll[slot], qh[n], ql[n])
            for half in range(2):
                out[:, 2 * jj + half, :] = (
                    assembled[:, 2 * jj + half, :] - product[:, half * 128 : half * 128 + 128]
                )

        @pl.when(jnp.logical_not(use))
        def _():
            for half in range(2):
                out[:, 2 * jj + half, :] = assembled[:, 2 * jj + half, :]


def trail_step(spot, panel_mask, assembled, ph, pll, arrays):
    vmem = pl.BlockSpec(memory_space=pltpu.VMEM)
    smem = pl.BlockSpec(memory_space=pltpu.SMEM)
    block = pl.BlockSpec((BS, 8, 128), lambda j, i: (i, j, 0))
    return pl.pallas_call(
        trail_kernel,
        grid=(2, 4),
        out_shape=jax.ShapeDtypeStruct((4 * BS, 16, 128), jnp.float32),
        in_specs=[smem, smem, block] + [vmem] * (2 + len(arrays)),
        out_specs=block,
        scratch_shapes=[
            pltpu.VMEM((8, BS, 512), jnp.bfloat16),
            pltpu.VMEM((8, BS, 512), jnp.bfloat16),
        ],
        compiler_params=pltpu.CompilerParams(vmem_limit_bytes=40 * 1024 * 1024),
        cost_estimate=pl.CostEstimate(flops=6_400_000_000, bytes_accessed=22_000_000, transcendentals=0),
        name="trail",
    )(spot, panel_mask, assembled, ph, pll, *arrays)


def gate_kernel(*refs):
    pass


def gate(values, after):
    far = pl.BlockSpec(memory_space=pl.ANY)
    return pl.pallas_call(
        gate_kernel,
        out_shape=[jax.ShapeDtypeStruct(v.shape, v.dtype) for v in values],
        in_specs=[far] * (len(values) + len(after)),
        out_specs=[far] * len(values),
        input_output_aliases={i: i for i in range(len(values))},
        compiler_params=pltpu.CompilerParams(vmem_limit_bytes=1024 * 1024),
        cost_estimate=pl.CostEstimate(flops=0, bytes_accessed=0, transcendentals=0),
        name="gate",
    )(*values, *after)


def shards(child_factor, parent, row_map, child_listed, inv_diag, panel_listed):
    p, x, core, yhi, z = (lax.axis_index(a) for a in AXES)
    spot = jnp.stack([p, x, core, yhi, z]).astype(jnp.int32)
    q = 2 * x + core
    first = core == 0
    own = child_factor.reshape(4, BS, 128)
    own_map = lax.dynamic_slice(row_map.reshape(2, 4, 8, BS), (p, 0, q, 0), (1, 4, 1, BS)).reshape(4, BS)
    placed, nothing = place(spot[:1], own, own_map)
    mine, other = placed[0], placed[1]

    late = parent.reshape(4, BS, 16, 128)[:, :, :2, :].transpose(0, 2, 1, 3) + nothing[0, 0]
    flat = parent.reshape(4 * BS * 16, 128)
    edge = mine[0]

    at_zero = lambda d: d["ylo"] == 0 and d["x"] == 0
    near = send(mine, route(lambda d: {"yhi": 1 - d["yhi"]}))
    cross = send(other, route(lambda d: {"ylo": 1 - d["ylo"]}))
    cross_far = send(other, route(lambda d: {"ylo": 1 - d["ylo"], "yhi": 1 - d["yhi"]}))
    spread = send(late[2:], route(lambda d: {"z": 3 - d["z"]}, lambda d: d["yhi"] == 0 and d["z"] < 2))
    moved = [send(edge, route(lambda d: {"x": n}, at_zero)) for n in (1, 3, 2)]
    near, cross, cross_far, spread, *moved = gate([near, cross, cross_far, spread] + moved, [])

    block = jnp.concatenate([mine, near, cross, cross_far])
    lead_piece = jnp.where(z < 2, late[:2], spread)
    edge = jnp.where(x == 0, edge, jnp.where(x == 1, moved[0], jnp.where(x == 3, moved[1], moved[2])))

    ring = route(lambda d: {"z": d["z"] + (1 if d["core"] == 0 else -1)})
    twin = route(lambda d: {"core": 1 - d["core"]})
    swap = route(lambda d: {"ylo": 1 - d["ylo"]})
    around = [route(lambda d: {"x": d["x"] - n}) for n in (1, 3, 2)]

    def target(lane):
        def move(d):
            z_to = 2 * (d["x"] % 2) + d["core"]
            return {"x": d["x"] + d["z"] - z_to, "z": z_to, "core": lane}

        return route(move, lambda d: d["yhi"] == d["x"] // 2)

    def scatter(parts):
        return [send(part, target(lane)) for lane, part in enumerate(parts)]

    gathered = [block]
    low = lambda d: d["ylo"] == 0
    arrived = send(block, ring)
    spread = send(lead_piece, route(lambda d: {"yhi": 1}, lambda d: d["yhi"] == 0))
    edge_up = send(edge, route(lambda d: {"ylo": 1}, low))
    edge_far = send(edge, route(lambda d: {"yhi": 1 - d["yhi"]}, low))
    edge_up_far = send(edge, route(lambda d: {"ylo": 1, "yhi": 1 - d["yhi"]}, low))
    pieces = scatter([block[:4], block[4:]])
    arrived, spread, edge_up, edge_far, edge_up_far, *pieces = gate(
        [arrived, spread, edge_up, edge_far, edge_up_far] + pieces, []
    )
    gathered.append(arrived)
    lead_piece = jnp.where(yhi == 0, lead_piece, spread).reshape(4, BS, 128)
    edge = jnp.stack([jnp.where(p == 0, edge, edge_up), jnp.where(p == 0, edge_far, edge_up_far)])
    leads = [jnp.concatenate([lead_piece, edge])]
    quarter = jnp.where(first, pieces[0], pieces[1])

    arrived = send(gathered[-1], ring)
    lead_next = send(leads[-1], ring)
    other_quarter = send(quarter, swap)
    arrived, lead_next, other_quarter = gate([arrived, lead_next, other_quarter], [])
    gathered.append(arrived)
    leads.append(lead_next)

    columns = [jnp.concatenate([quarter, other_quarter])]
    arrived = send(gathered[-1], ring)
    lead_next = send(leads[-1], ring)
    moving = [send(columns[0], pairs) for pairs in around]
    arrived, lead_next = gate([arrived, lead_next], [])
    gathered.append(arrived)
    leads.append(lead_next)
    leads.append(send(leads[-1], ring))
    moving = gate(moving + [leads[-1]], [])
    columns += moving[:3]
    leads[-1] = moving[3]

    edge_own = jnp.concatenate([block[4:] for block in leads])
    edge_twin = send(edge_own, twin)
    panel, to_send, rh, rl, ph, pll = rows_step(
        spot, child_listed, inv_diag, gathered, leads, edge_twin
    )
    turn = (z - (2 * (x % 2) + core)) % 4
    mine = lax.dynamic_index_in_dim(to_send, turn, 0, keepdims=False)
    pieces = scatter([mine[:2], mine[2:]])
    arrays = [send(value, twin) for value in columns[:2]]
    *pieces, arrays[0], arrays[1] = gate(pieces + arrays, [])
    quarter = jnp.where(first, pieces[0], pieces[1])
    other_quarter = send(quarter, swap)
    arrays += [send(value, twin) for value in columns[2:]]
    other_quarter, arrays[2], arrays[3] = gate([other_quarter] + arrays[2:], [])
    panels = [jnp.concatenate([quarter, other_quarter])]
    panels += [send(panels[0], pairs) for pairs in around]
    assembled = update_step(spot, child_listed, flat, rh, rl, columns + arrays)
    panels[1:] = gate(panels[1:], [assembled])
    panels += [send(value, twin) for value in panels]
    factored = trail_step(
        spot, panel_listed, assembled.reshape(4 * BS, 16, 128), ph, pll, panels
    )
    return factored.reshape(parent.shape), panel.reshape(4, 1, BS, 512)


def solution(mesh):
    grid = Mesh(mesh.devices.reshape(SIZES), AXES)
    row, col = ("ylo", "x", "core"), ("yhi", "z")
    return jax.shard_map(
        shards,
        mesh=grid,
        in_specs=(
            P(None, row, None, col),
            P(None, row, None, None, col, None),
            P(),
            P(),
            P(),
            P(),
        ),
        out_specs=(P(None, row, None, None, col, None), P(None, row, None, None)),
        check_vma=False,
    )
```

time: 655 us -> 248 us (0.38)
  the two profiles are of different devices: /device:TPU:66 before, /device:TPU:39 now
where the time goes in v2:
time: 248 us; the launch traced here: 247 us
  waiting for transfers between devices  109 us (44%)
  starting transfers between devices  52.8 us (21%)
  Pallas kernels  52 us (21%)
  local copies, waits for them, and re-layouts  23.2 us (9%)
  other arithmetic  9.01 us (4%)
    ppermute x38, waiting for transfers between devices, send(): return lax.ppermute(value, AXES, pairs)  109 us
    ppermute x38, starting transfers between devices, send(): return lax.ppermute(value, AXES, pairs)  52.8 us
    pallas_call x1, Pallas kernels, update_step(): pl.pallas_call(update_kernel, grid=(4,), out_shape=jax.ShapeDtypeStruct(f...  23 us
    unnamed x63, local copies, waits for them, and re-layouts  18.6 us
    pallas_call x1, Pallas kernels, trail_step(): pl.pallas_call(trail_kernel, grid=(2, 4), out_shape=jax.ShapeDtypeStruct(...  17.9 us
    pallas_call x1, Pallas kernels, rows_step(): pl.pallas_call(rows_kernel, out_shape=(jax.ShapeDtypeStruct((4, BS, 512),...  8.64 us
  transfers between devices with their start and end apart: 38, of which 18 were waited for; matrix products, arithmetic and copies ran while one was open for 4% of the time, Pallas kernels for 13%

profile of v2, /device:TPU:39, one launch (start us, length us, event | category | flops | bytes accessed | tf_op | source)
XLA Modules:
  0.0 246.7 jit_solution(4543378307554422825)
XLA Ops:
  2.1 2.5 slice.62
  4.5 2.4 place.1
  9.0 3.6 %collective-permute-start.3 = (f32[2,2,256,128]{3,2,1,0:T(8,128)S(1)}, f32[2,2,256,128]{3,2,1,0:T(8,128)S(1)}, u32[]{:S(2)}, u32[]{:S(2)}) collective-permute-start(f32[2,2,256,128]{3,2,1,0:T(8,128)S(1)} %slice.63), channel_id=1, source_target_pairs={{0,3},{1,2},{8,11},{9,10},{16,19},{17,18},{24,27},{25,26},{32,35},... | collective-permute-start | bytes 1572872 | tf_op jit(solution)/shard_map/ppermute | solution.py:35
  15.5 2.5 %collective-permute-start.2 = (f32[2,256,128]{2,1,0:T(8,128)S(1)}, f32[2,256,128]{2,1,0:T(8,128)S(1)}, u32[]{:S(2)}, u32[]{:S(2)}) collective-permute-start(f32[2,256,128]{2,1,0:T(8,128)S(1)} %get-tuple-element.94), channel_id=1, source_target_pairs={{0,68},{1,69},{2,70},{3,71},{4,64},{5,65},{6,66},{7,67},{8,76},{9,... | collective-permute-start | bytes 786440 | tf_op jit(solution)/shard_map/ppermute | solution.py:35
  18.0 2.5 %collective-permute-done.5.refs_5_ = f32[256,128]{1,0:T(8,128)S(1)} collective-permute-done((f32[256,128]{1,0:T(8,128)S(1)}, f32[256,128]{1,0:T(8,128)S(1)}, u32[]{:S(2)}, u32[]{:S(2)}) %collective-permute-start.5) | collective-permute-done | bytes 131104 | tf_op jit(solution)/shard_map/ppermute | solution.py:35
  23.1 3.6 %collective-permute-done.1.refs_1_ = f32[2,256,128]{2,1,0:T(8,128)S(1)} collective-permute-done((f32[2,256,128]{2,1,0:T(8,128)S(1)}, f32[2,256,128]{2,1,0:T(8,128)S(1)}, u32[]{:S(2)}, u32[]{:S(2)}) %collective-permute-start.1) | collective-permute-done | bytes 262176 | tf_op jit(solution)/shard_map/ppermute | solution.py:35
  26.7 3.3 %collective-permute-done.2.refs_2_ = f32[2,256,128]{2,1,0:T(8,128)S(1)} collective-permute-done((f32[2,256,128]{2,1,0:T(8,128)S(1)}, f32[2,256,128]{2,1,0:T(8,128)S(1)}, u32[]{:S(2)}, u32[]{:S(2)}) %collective-permute-start.2) | collective-permute-done | bytes 262176 | tf_op jit(solution)/shard_map/ppermute | solution.py:35
  34.0 2.2 collective-permute-start.8
  41.7 2.2 collective-permute-start.9
  44.0 6.3 %collective-permute-done.9.refs_2_ = f32[256,128]{1,0:T(8,128)S(1)} collective-permute-done((f32[256,128]{1,0:T(8,128)S(1)}, f32[256,128]{1,0:T(8,128)S(1)}, u32[]{:S(2)}, u32[]{:S(2)}) %collective-permute-start.9) | collective-permute-done | bytes 131104 | tf_op jit(solution)/shard_map/ppermute | solution.py:35
  50.2 3.6 %collective-permute-start.10 = (f32[256,128]{1,0:T(8,128)S(1)}, f32[256,128]{1,0:T(8,128)S(1)}, u32[]{:S(2)}, u32[]{:S(2)}) collective-permute-start(f32[256,128]{1,0:T(8,128)S(1)} %select_select_fusion), channel_id=1, source_target_pairs={{0,4},{1,5},{2,6},{3,7},{4,0},{5,1},{6,2},{7,3},{8,12},{9,13},{10,... | collective-permute-start | bytes 393224 | tf_op jit(solution)/shard_map/ppermute | solution.py:35
  53.8 3.9 %collective-permute-done.10.refs_3_ = f32[256,128]{1,0:T(8,128)S(1)} collective-permute-done((f32[256,128]{1,0:T(8,128)S(1)}, f32[256,128]{1,0:T(8,128)S(1)}, u32[]{:S(2)}, u32[]{:S(2)}) %collective-permute-start.10) | collective-permute-done | bytes 131104 | tf_op jit(solution)/shard_map/ppermute | solution.py:35
  61.0 6.6 %collective-permute-done.13.refs_6_ = f32[4,256,128]{2,1,0:T(8,128)S(1)} collective-permute-done((f32[4,256,128]{2,1,0:T(8,128)}, f32[4,256,128]{2,1,0:T(8,128)S(1)}, u32[]{:S(2)}, u32[]{:S(2)}) %collective-permute-start.13) | collective-permute-done | bytes 524320 | tf_op jit(solution)/shard_map/ppermute | solution.py:35
  70.2 5.9 %collective-permute-start.15 = (f32[6,256,128]{2,1,0:T(8,128)S(1)}, f32[6,256,128]{2,1,0:T(8,128)S(1)}, u32[]{:S(2)}, u32[]{:S(2)}) collective-permute-start(f32[6,256,128]{2,1,0:T(8,128)S(1)} %pad_maximum_fusion.2.refs_4_), channel_id=1, source_target_pairs={{0,1},{1,2},{2,3},{3,0},{4,5},{5,6},{6,7},{7,4},{8,11},{9,8},{10,9... | collective-permute-start | bytes 2359304 | tf_op jit(solution)/shard_map/ppermute | solution.py:35
  76.3 10.3 %collective-permute-done.16.refs_2_ = f32[4,256,128]{2,1,0:T(8,128)S(1)} collective-permute-done((f32[4,256,128]{2,1,0:T(8,128)S(1)}, f32[4,256,128]{2,1,0:T(8,128)S(1)}, u32[]{:S(2)}, u32[]{:S(2)}) %collective-permute-start.16) | collective-permute-done | bytes 524320 | tf_op jit(solution)/shard_map/ppermute | solution.py:35
  86.5 3.4 %collective-permute-done.15.refs_1_ = f32[6,256,128]{2,1,0:T(8,128)S(1)} collective-permute-done((f32[6,256,128]{2,1,0:T(8,128)S(1)}, f32[6,256,128]{2,1,0:T(8,128)S(1)}, u32[]{:S(2)}, u32[]{:S(2)}) %collective-permute-start.15) | collective-permute-done | bytes 786464 | tf_op jit(solution)/shard_map/ppermute | solution.py:35
  90.0 3.8 %collective-permute-start.17 = (f32[8,256,128]{2,1,0:T(8,128)S(1)}, f32[8,256,128]{2,1,0:T(8,128)S(1)}, u32[]{:S(2)}, u32[]{:S(2)}) collective-permute-start(f32[8,256,128]{2,1,0:T(8,128)S(1)} %get-tuple-element.59.refs_2_), channel_id=1, source_target_pairs={{0,1},{1,2},{2,3},{3,0},{4,5},{5,6},{6,7},{7,4},{8,11},{9,8},{10,9... | collective-permute-start | bytes 3145736 | tf_op jit(solution)/shard_map/ppermute | solution.py:35
  93.7 3.1 %collective-permute-start.18 = (f32[6,256,128]{2,1,0:T(8,128)S(1)}, f32[6,256,128]{2,1,0:T(8,128)S(1)}, u32[]{:S(2)}, u32[]{:S(2)}) collective-permute-start(f32[6,256,128]{2,1,0:T(8,128)S(1)} %get-tuple-element.60.refs_5_), channel_id=1, source_target_pairs={{0,1},{1,2},{2,3},{3,0},{4,5},{5,6},{6,7},{7,4},{8,11},{9,8},{10,9... | collective-permute-start | bytes 2359304 | tf_op jit(solution)/shard_map/ppermute | solution.py:35
  97.0 2.7 %collective-permute-start.20 = (f32[8,256,128]{2,1,0:T(8,128)S(1)}, f32[8,256,128]{2,1,0:T(8,128)S(1)}, u32[]{:S(2)}, u32[]{:S(2)}) collective-permute-start(f32[8,256,128]{2,1,0:T(8,128)S(1)} %pad_maximum_fusion.1.refs_0_), channel_id=1, source_target_pairs={{0,16},{1,17},{2,18},{3,19},{4,20},{5,21},{6,22},{7,23},{8,24},{9,... | collective-permute-start | bytes 3145736 | tf_op jit(solution)/shard_map/ppermute | solution.py:35
  99.7 14.9 %collective-permute-done.18.refs_1_ = f32[6,256,128]{2,1,0:T(8,128)S(1)} collective-permute-done((f32[6,256,128]{2,1,0:T(8,128)S(1)}, f32[6,256,128]{2,1,0:T(8,128)S(1)}, u32[]{:S(2)}, u32[]{:S(2)}) %collective-permute-start.18) | collective-permute-done | bytes 786464 | tf_op jit(solution)/shard_map/ppermute | solution.py:35
  114.6 2.5 %collective-permute-start.22 = (f32[6,256,128]{2,1,0:T(8,128)S(1)}, f32[6,256,128]{2,1,0:T(8,128)S(1)}, u32[]{:S(2)}, u32[]{:S(2)}) collective-permute-start(f32[6,256,128]{2,1,0:T(8,128)S(1)} %get-tuple-element.62.refs_6_), channel_id=1, source_target_pairs={{0,1},{1,2},{2,3},{3,0},{4,5},{5,6},{6,7},{7,4},{8,11},{9,8},{10,9... | collective-permute-start | bytes 2359304 | tf_op jit(solution)/shard_map/ppermute | solution.py:35
  118.6 23.5 %collective-permute-done.19.refs_0_ = f32[8,256,128]{2,1,0:T(8,128)} collective-permute-done((f32[8,256,128]{2,1,0:T(8,128)S(1)}, f32[8,256,128]{2,1,0:T(8,128)}, u32[]{:S(2)}, u32[]{:S(2)}) %collective-permute-start.19) | collective-permute-done | bytes 1048608 | tf_op jit(solution)/shard_map/ppermute | solution.py:35
  147.1 3.1 %collective-permute-done.23.refs_8_ = f32[8,256,128]{2,1,0:T(8,128)} collective-permute-done((f32[8,256,128]{2,1,0:T(8,128)}, f32[8,256,128]{2,1,0:T(8,128)}, u32[]{:S(2)}, u32[]{:S(2)}) %collective-permute-start.23) | collective-permute-done | bytes 1048608 | tf_op jit(solution)/shard_map/ppermute | solution.py:35
  159.6 8.6 %rows.1 = (f32[4,256,512]{2,1,0:T(8,128)}, f32[4,4,256,128]{3,2,1,0:T(8,128)S(1)}, bf16[4,256,1024]{2,1,0:T(8,128)(2,1)}, bf16[4,256,1024]{2,1,0:T(8,128)(2,1)},...) custom-call(s32[5]{0:T(128)S(1)} %stack.30.spot, s32[2,32,32]{2,1,0:T(8,128)S(1)} %copy-done.23, ...), custom_call_target="tpu_custom_call" | custom-call | flops 4000000000 | bytes 18000000 | tf_op jit(solution)/shard_map/rows/pallas_call | solution.py:160
  170.3 15.7 %collective-permute-done.25.refs_1_ = f32[2,256,128]{2,1,0:T(8,128)S(1)} collective-permute-done((f32[2,256,128]{2,1,0:T(8,128)S(1)}, f32[2,256,128]{2,1,0:T(8,128)S(1)}, u32[]{:S(2)}, u32[]{:S(2)}) %collective-permute-start.25) | collective-permute-done | bytes 262176 | tf_op jit(solution)/shard_map/ppermute | solution.py:35
  186.9 4.6 %collective-permute-done.28.refs_0_ = f32[2,256,128]{2,1,0:T(8,128)S(1)} collective-permute-done((f32[2,256,128]{2,1,0:T(8,128)S(1)}, f32[2,256,128]{2,1,0:T(8,128)S(1)}, u32[]{:S(2)}, u32[]{:S(2)}) %collective-permute-start.28) | collective-permute-done | bytes 262176 | tf_op jit(solution)/shard_map/ppermute | solution.py:35
  191.7 2.7 %collective-permute-start.32 = (f32[4,256,128]{2,1,0:T(8,128)S(1)}, f32[4,256,128]{2,1,0:T(8,128)S(1)}, u32[]{:S(2)}, u32[]{:S(2)}) collective-permute-start(f32[4,256,128]{2,1,0:T(8,128)S(1)} %pad_maximum_fusion.5.refs_0_), channel_id=1, source_target_pairs={{0,16},{1,17},{2,18},{3,19},{4,20},{5,21},{6,22},{7,23},{8,24},{9,... | collective-permute-start | bytes 1572872 | tf_op jit(solution)/shard_map/ppermute | solution.py:35
  194.3 2.1 collective-permute-start.33
  196.4 2.5 %collective-permute-start.34 = (f32[4,256,128]{2,1,0:T(8,128)S(1)}, f32[4,256,128]{2,1,0:T(8,128)S(1)}, u32[]{:S(2)}, u32[]{:S(2)}) collective-permute-start(f32[4,256,128]{2,1,0:T(8,128)S(1)} %pad_maximum_fusion.5.refs_0_), channel_id=1, source_target_pairs={{0,8},{1,9},{2,10},{3,11},{4,12},{5,13},{6,14},{7,15},{8,0},{9,1},... | collective-permute-start | bytes 1572872 | tf_op jit(solution)/shard_map/ppermute | solution.py:35
  198.9 23.0 %update.1.refs_3_ = f32[16384,128]{1,0:T(8,128)} custom-call(s32[5]{0:T(128)S(1)} %stack.30.spot, s32[2,32,32]{2,1,0:T(8,128)S(1)} %copy-done.23, f32[16384,128]{1,0:T(8,128)} %bitcast.42, bf16[4,256,1024]{2,1,0:T(8,128)(2,1)S(1)} %copy-done.7, bf16[4,256,1024]{2,1,0:T(8,128)(2,1)S(1)} %copy-done.8, f32[8,256,128]{2,1,0:T(8,128)S(1)} %pad_maximum_fusion.1.refs_0_, ...), custom_call_target="tpu_custom_call" | custom-call | flops 6400000000 | bytes 28000000 | tf_op jit(solution)/shard_map/update/pallas_call | solution.py:238
  222.0 3.4 %copy-done.2 = f32[16384,128]{1,0:T(8,128)S(1)} copy-done((f32[16384,128]{1,0:T(8,128)S(1)}, f32[16384,128]{1,0:T(8,128)}, u32[]{:S(2)}) %copy-start.2) | copy-done | bytes 8388632
  228.8 17.9 %trail.1 = f32[1024,16,128]{2,1,0:T(8,128)} custom-call(s32[5]{0:T(128)S(1)} %stack.30.spot, s32[64,64]{1,0:T(8,128)S(1)} %copy-done.25, f32[1024,16,128]{2,1,0:T(8,128)} %bitcast.40, bf16[4,256,512]{2,1,0:T(8,128)(2,1)S(1)} %get-tuple-element.77.ph, bf16[4,256,512]{2,1,0:T(8,128)(2,1)S(1)} %get-tuple-element.78.pll, ...), custom_call_target="tpu_custom_call" | custom-call | flops 6400000000 | bytes 22000000 | tf_op jit(solution)/shard_map/trail/pallas_call | solution.py:301
  (142 shorter events, 46.7 us)
Async XLA Ops:
  9.0 21.1 %collective-permute-start.3 = (f32[2,2,256,128]{3,2,1,0:T(8,128)S(1)}, f32[2,2,256,128]{3,2,1,0:T(8,128)S(1)}, u32[]{:S(2)}, u32[]{:S(2)}) collective-permute-start(f32[2,2,256,128]{3,2,1,0:T(8,128)S(1)} %slice.63), channel_id=1, source_target_pairs={{0,3},{1,2},{8,11},{9,10},{16,19},{17,18},{24,27},{25,26},{32,35},... | collective-permute-start | bytes 1572872 | tf_op jit(solution)/shard_map/ppermute | solution.py:35
  13.3 7.2 %collective-permute-start.5 = (f32[256,128]{1,0:T(8,128)S(1)}, f32[256,128]{1,0:T(8,128)S(1)}, u32[]{:S(2)}, u32[]{:S(2)}) collective-permute-start(f32[256,128]{1,0:T(8,128)S(1)} %slice_bitcast_fusion.2), channel_id=1, source_target_pairs={{0,48},{1,49},{2,50},{3,51},{4,52},{5,53},{6,54},{7,55},{8,56},{9,... | collective-permute-start | bytes 393224 | tf_op jit(solution)/shard_map/ppermute | solution.py:35
  14.6 8.5 %collective-permute-start = (f32[2,256,128]{2,1,0:T(8,128)S(1)}, f32[2,256,128]{2,1,0:T(8,128)S(1)}, u32[]{:S(2)}, u32[]{:S(2)}) collective-permute-start(f32[2,256,128]{2,1,0:T(8,128)S(1)} %get-tuple-element.95), channel_id=1, source_target_pairs={{0,4},{1,5},{2,6},{3,7},{4,0},{5,1},{6,2},{7,3},{8,12},{9,13},{10,... | collective-permute-start | bytes 786440 | tf_op jit(solution)/shard_map/ppermute | solution.py:35
  14.7 12.0 %collective-permute-start.1 = (f32[2,256,128]{2,1,0:T(8,128)S(1)}, f32[2,256,128]{2,1,0:T(8,128)S(1)}, u32[]{:S(2)}, u32[]{:S(2)}) collective-permute-start(f32[2,256,128]{2,1,0:T(8,128)S(1)} %get-tuple-element.94), channel_id=1, source_target_pairs={{0,64},{1,65},{2,66},{3,67},{4,68},{5,69},{6,70},{7,71},{8,72},{9,... | collective-permute-start | bytes 786440 | tf_op jit(solution)/shard_map/ppermute | solution.py:35
  15.5 14.6 %collective-permute-start.2 = (f32[2,256,128]{2,1,0:T(8,128)S(1)}, f32[2,256,128]{2,1,0:T(8,128)S(1)}, u32[]{:S(2)}, u32[]{:S(2)}) collective-permute-start(f32[2,256,128]{2,1,0:T(8,128)S(1)} %get-tuple-element.94), channel_id=1, source_target_pairs={{0,68},{1,69},{2,70},{3,71},{4,64},{5,65},{6,66},{7,67},{8,76},{9,... | collective-permute-start | bytes 786440 | tf_op jit(solution)/shard_map/ppermute | solution.py:35
  31.2 36.4 %collective-permute-start.7 = (f32[8,256,128]{2,1,0:T(8,128)}, f32[8,256,128]{2,1,0:T(8,128)S(1)}, u32[]{:S(2)}, u32[]{:S(2)}) collective-permute-start(f32[8,256,128]{2,1,0:T(8,128)} %pad_maximum_fusion.refs_0_), channel_id=1, source_target_pairs={{0,1},{1,2},{2,3},{3,0},{4,5},{5,6},{6,7},{7,4},{8,11},{9,8},{10,9... | collective-permute-start | bytes 3145736 | tf_op jit(solution)/shard_map/ppermute | solution.py:35
  34.0 27.0 %collective-permute-start.8 = (f32[2,2,256,128]{3,2,1,0:T(8,128)}, f32[2,2,256,128]{3,2,1,0:T(8,128)S(1)}, u32[]{:S(2)}, u32[]{:S(2)}) collective-permute-start(f32[2,2,256,128]{3,2,1,0:T(8,128)} %slice_select_fusion), channel_id=1, source_target_pairs={{0,4},{1,5},{2,6},{3,7},{8,12},{9,13},{10,14},{11,15},{16,20},{17,... | collective-permute-start | bytes 1572872 | tf_op jit(solution)/shard_map/ppermute | solution.py:35
  38.0 23.0 %collective-permute-start.12 = (f32[4,256,128]{2,1,0:T(8,128)}, f32[4,256,128]{2,1,0:T(8,128)S(1)}, u32[]{:S(2)}, u32[]{:S(2)}) collective-permute-start(f32[4,256,128]{2,1,0:T(8,128)} %pad_maximum_fusion.3), channel_id=1, source_target_pairs={{0,0},{1,16},{2,32},{3,48},{8,49},{9,1},{10,17},{11,33},{16,50},{1... | collective-permute-start | bytes 1572872 | tf_op jit(solution)/shard_map/ppermute | solution.py:35
  39.5 28.1 %collective-permute-start.13 = (f32[4,256,128]{2,1,0:T(8,128)}, f32[4,256,128]{2,1,0:T(8,128)S(1)}, u32[]{:S(2)}, u32[]{:S(2)}) collective-permute-start(f32[4,256,128]{2,1,0:T(8,128)} %pad_maximum_fusion.4), channel_id=1, source_target_pairs={{0,8},{1,24},{2,40},{3,56},{8,57},{9,9},{10,25},{11,41},{16,58},{1... | collective-permute-start | bytes 1572872 | tf_op jit(solution)/shard_map/ppermute | solution.py:35
  41.7 8.5 %collective-permute-start.9 = (f32[256,128]{1,0:T(8,128)S(1)}, f32[256,128]{1,0:T(8,128)S(1)}, u32[]{:S(2)}, u32[]{:S(2)}) collective-permute-start(f32[256,128]{1,0:T(8,128)S(1)} %select_select_fusion), channel_id=1, source_target_pairs={{0,64},{1,65},{2,66},{3,67},{4,68},{5,69},{6,70},{7,71},{8,72},{9,... | collective-permute-start | bytes 393224 | tf_op jit(solution)/shard_map/ppermute | solution.py:35
  50.2 7.5 %collective-permute-start.10 = (f32[256,128]{1,0:T(8,128)S(1)}, f32[256,128]{1,0:T(8,128)S(1)}, u32[]{:S(2)}, u32[]{:S(2)}) collective-permute-start(f32[256,128]{1,0:T(8,128)S(1)} %select_select_fusion), channel_id=1, source_target_pairs={{0,4},{1,5},{2,6},{3,7},{4,0},{5,1},{6,2},{7,3},{8,12},{9,13},{10,... | collective-permute-start | bytes 393224 | tf_op jit(solution)/shard_map/ppermute | solution.py:35
  57.7 3.2 %collective-permute-start.11 = (f32[256,128]{1,0:T(8,128)S(1)}, f32[256,128]{1,0:T(8,128)S(1)}, u32[]{:S(2)}, u32[]{:S(2)}) collective-permute-start(f32[256,128]{1,0:T(8,128)S(1)} %select_select_fusion), channel_id=1, source_target_pairs={{0,68},{1,69},{2,70},{3,71},{4,64},{5,65},{6,66},{7,67},{8,76},{9,... | collective-permute-start | bytes 393224 | tf_op jit(solution)/shard_map/ppermute | solution.py:35
  67.6 22.4 %collective-permute-start.14 = (f32[8,256,128]{2,1,0:T(8,128)S(1)}, f32[8,256,128]{2,1,0:T(8,128)S(1)}, u32[]{:S(2)}, u32[]{:S(2)}) collective-permute-start(f32[8,256,128]{2,1,0:T(8,128)S(1)} %get-tuple-element.52.refs_1_), channel_id=1, source_target_pairs={{0,1},{1,2},{2,3},{3,0},{4,5},{5,6},{6,7},{7,4},{8,11},{9,8},{10,9... | collective-permute-start | bytes 3145736 | tf_op jit(solution)/shard_map/ppermute | solution.py:35
  70.2 19.8 %collective-permute-start.15 = (f32[6,256,128]{2,1,0:T(8,128)S(1)}, f32[6,256,128]{2,1,0:T(8,128)S(1)}, u32[]{:S(2)}, u32[]{:S(2)}) collective-permute-start(f32[6,256,128]{2,1,0:T(8,128)S(1)} %pad_maximum_fusion.2.refs_4_), channel_id=1, source_target_pairs={{0,1},{1,2},{2,3},{3,0},{4,5},{5,6},{6,7},{7,4},{8,11},{9,8},{10,9... | collective-permute-start | bytes 2359304 | tf_op jit(solution)/shard_map/ppermute | solution.py:35
  76.2 10.4 %collective-permute-start.16 = (f32[4,256,128]{2,1,0:T(8,128)S(1)}, f32[4,256,128]{2,1,0:T(8,128)S(1)}, u32[]{:S(2)}, u32[]{:S(2)}) collective-permute-start(f32[4,256,128]{2,1,0:T(8,128)S(1)} %broadcast_select_fusion), channel_id=1, source_target_pairs={{0,64},{1,65},{2,66},{3,67},{4,68},{5,69},{6,70},{7,71},{8,72},{9,... | collective-permute-start | bytes 1572872 | tf_op jit(solution)/shard_map/ppermute | solution.py:35
  90.0 24.7 %collective-permute-start.17 = (f32[8,256,128]{2,1,0:T(8,128)S(1)}, f32[8,256,128]{2,1,0:T(8,128)S(1)}, u32[]{:S(2)}, u32[]{:S(2)}) collective-permute-start(f32[8,256,128]{2,1,0:T(8,128)S(1)} %get-tuple-element.59.refs_2_), channel_id=1, source_target_pairs={{0,1},{1,2},{2,3},{3,0},{4,5},{5,6},{6,7},{7,4},{8,11},{9,8},{10,9... | collective-permute-start | bytes 3145736 | tf_op jit(solution)/shard_map/ppermute | solution.py:35
  93.7 20.9 %collective-permute-start.18 = (f32[6,256,128]{2,1,0:T(8,128)S(1)}, f32[6,256,128]{2,1,0:T(8,128)S(1)}, u32[]{:S(2)}, u32[]{:S(2)}) collective-permute-start(f32[6,256,128]{2,1,0:T(8,128)S(1)} %get-tuple-element.60.refs_5_), channel_id=1, source_target_pairs={{0,1},{1,2},{2,3},{3,0},{4,5},{5,6},{6,7},{7,4},{8,11},{9,8},{10,9... | collective-permute-start | bytes 2359304 | tf_op jit(solution)/shard_map/ppermute | solution.py:35
  96.9 45.1 %collective-permute-start.19 = (f32[8,256,128]{2,1,0:T(8,128)S(1)}, f32[8,256,128]{2,1,0:T(8,128)}, u32[]{:S(2)}, u32[]{:S(2)}) collective-permute-start(f32[8,256,128]{2,1,0:T(8,128)S(1)} %pad_maximum_fusion.1.refs_0_), channel_id=1, source_target_pairs={{0,48},{1,49},{2,50},{3,51},{4,52},{5,53},{6,54},{7,55},{8,56},{9,... | collective-permute-start | bytes 3145736 | tf_op jit(solution)/shard_map/ppermute | solution.py:35
  97.0 45.0 %collective-permute-start.20 = (f32[8,256,128]{2,1,0:T(8,128)S(1)}, f32[8,256,128]{2,1,0:T(8,128)S(1)}, u32[]{:S(2)}, u32[]{:S(2)}) collective-permute-start(f32[8,256,128]{2,1,0:T(8,128)S(1)} %pad_maximum_fusion.1.refs_0_), channel_id=1, source_target_pairs={{0,16},{1,17},{2,18},{3,19},{4,20},{5,21},{6,22},{7,23},{8,24},{9,... | collective-permute-start | bytes 3145736 | tf_op jit(solution)/shard_map/ppermute | solution.py:35
  99.7 42.3 %collective-permute-start.21 = (f32[8,256,128]{2,1,0:T(8,128)S(1)}, f32[8,256,128]{2,1,0:T(8,128)S(1)}, u32[]{:S(2)}, u32[]{:S(2)}) collective-permute-start(f32[8,256,128]{2,1,0:T(8,128)S(1)} %pad_maximum_fusion.1.refs_0_), channel_id=1, source_target_pairs={{0,32},{1,33},{2,34},{3,35},{4,36},{5,37},{6,38},{7,39},{8,40},{9,... | collective-permute-start | bytes 3145736 | tf_op jit(solution)/shard_map/ppermute | solution.py:35
  114.6 27.4 %collective-permute-start.22 = (f32[6,256,128]{2,1,0:T(8,128)S(1)}, f32[6,256,128]{2,1,0:T(8,128)S(1)}, u32[]{:S(2)}, u32[]{:S(2)}) collective-permute-start(f32[6,256,128]{2,1,0:T(8,128)S(1)} %get-tuple-element.62.refs_6_), channel_id=1, source_target_pairs={{0,1},{1,2},{2,3},{3,0},{4,5},{5,6},{6,7},{7,4},{8,11},{9,8},{10,9... | collective-permute-start | bytes 2359304 | tf_op jit(solution)/shard_map/ppermute | solution.py:35
  145.7 4.5 %collective-permute-start.23 = (f32[8,256,128]{2,1,0:T(8,128)}, f32[8,256,128]{2,1,0:T(8,128)}, u32[]{:S(2)}, u32[]{:S(2)}) collective-permute-start(f32[8,256,128]{2,1,0:T(8,128)} %slice_dynamic-update-slice_fusion), channel_id=1, source_target_pairs={{0,8},{1,9},{2,10},{3,11},{4,12},{5,13},{6,14},{7,15},{8,0},{9,1},... | collective-permute-start | bytes 3145736 | tf_op jit(solution)/shard_map/ppermute | solution.py:35
  145.7 23.3 %collective-permute-start.26 = (f32[8,256,128]{2,1,0:T(8,128)S(1)}, f32[8,256,128]{2,1,0:T(8,128)S(1)}, u32[]{:S(2)}, u32[]{:S(2)}) collective-permute-start(f32[8,256,128]{2,1,0:T(8,128)S(1)} %pad_maximum_fusion.1.refs_0_), channel_id=1, source_target_pairs={{0,8},{1,9},{2,10},{3,11},{4,12},{5,13},{6,14},{7,15},{8,0},{9,1},... | collective-permute-start | bytes 3145736 | tf_op jit(solution)/shard_map/ppermute | solution.py:35
  146.2 24.1 %collective-permute-start.27 = (f32[8,256,128]{2,1,0:T(8,128)}, f32[8,256,128]{2,1,0:T(8,128)S(1)}, u32[]{:S(2)}, u32[]{:S(2)}) collective-permute-start(f32[8,256,128]{2,1,0:T(8,128)} %get-tuple-element.67.refs_1_), channel_id=1, source_target_pairs={{0,8},{1,9},{2,10},{3,11},{4,12},{5,13},{6,14},{7,15},{8,0},{9,1},... | collective-permute-start | bytes 3145736 | tf_op jit(solution)/shard_map/ppermute | solution.py:35
  146.3 40.6 %collective-permute-start.29 = (f32[8,256,128]{2,1,0:T(8,128)}, f32[8,256,128]{2,1,0:T(8,128)S(1)}, u32[]{:S(2)}, u32[]{:S(2)}) collective-permute-start(f32[8,256,128]{2,1,0:T(8,128)} %copy-done.3), channel_id=1, source_target_pairs={{0,8},{1,9},{2,10},{3,11},{4,12},{5,13},{6,14},{7,15},{8,0},{9,1},... | collective-permute-start | bytes 3145736 | tf_op jit(solution)/shard_map/ppermute | solution.py:35
  146.8 40.1 %collective-permute-start.30 = (f32[8,256,128]{2,1,0:T(8,128)}, f32[8,256,128]{2,1,0:T(8,128)S(1)}, u32[]{:S(2)}, u32[]{:S(2)}) collective-permute-start(f32[8,256,128]{2,1,0:T(8,128)} %copy-done.5), channel_id=1, source_target_pairs={{0,8},{1,9},{2,10},{3,11},{4,12},{5,13},{6,14},{7,15},{8,0},{9,1},... | collective-permute-start | bytes 3145736 | tf_op jit(solution)/shard_map/ppermute | solution.py:35
  169.0 17.0 %collective-permute-start.25 = (f32[2,256,128]{2,1,0:T(8,128)S(1)}, f32[2,256,128]{2,1,0:T(8,128)S(1)}, u32[]{:S(2)}, u32[]{:S(2)}) collective-permute-start(f32[2,256,128]{2,1,0:T(8,128)S(1)} %get-tuple-element.92), channel_id=1, source_target_pairs={{0,8},{1,24},{2,40},{3,56},{8,57},{9,9},{10,25},{11,41},{16,58},{1... | collective-permute-start | bytes 786440 | tf_op jit(solution)/shard_map/ppermute | solution.py:35
  186.1 5.5 %collective-permute-start.28 = (f32[2,256,128]{2,1,0:T(8,128)S(1)}, f32[2,256,128]{2,1,0:T(8,128)S(1)}, u32[]{:S(2)}, u32[]{:S(2)}) collective-permute-start(f32[2,256,128]{2,1,0:T(8,128)S(1)} %broadcast_select_fusion.2), channel_id=1, source_target_pairs={{0,64},{1,65},{2,66},{3,67},{4,68},{5,69},{6,70},{7,71},{8,72},{9,... | collective-permute-start | bytes 786440 | tf_op jit(solution)/shard_map/ppermute | solution.py:35
  191.6 30.4 %collective-permute-start.31 = (f32[4,256,128]{2,1,0:T(8,128)S(1)}, f32[4,256,128]{2,1,0:T(8,128)S(1)}, u32[]{:S(2)}, u32[]{:S(2)}) collective-permute-start(f32[4,256,128]{2,1,0:T(8,128)S(1)} %pad_maximum_fusion.5.refs_0_), channel_id=1, source_target_pairs={{0,48},{1,49},{2,50},{3,51},{4,52},{5,53},{6,54},{7,55},{8,56},{9,... | collective-permute-start | bytes 1572872 | tf_op jit(solution)/shard_map/ppermute | solution.py:35
  191.7 30.3 %collective-permute-start.32 = (f32[4,256,128]{2,1,0:T(8,128)S(1)}, f32[4,256,128]{2,1,0:T(8,128)S(1)}, u32[]{:S(2)}, u32[]{:S(2)}) collective-permute-start(f32[4,256,128]{2,1,0:T(8,128)S(1)} %pad_maximum_fusion.5.refs_0_), channel_id=1, source_target_pairs={{0,16},{1,17},{2,18},{3,19},{4,20},{5,21},{6,22},{7,23},{8,24},{9,... | collective-permute-start | bytes 1572872 | tf_op jit(solution)/shard_map/ppermute | solution.py:35
  194.3 27.6 %collective-permute-start.33 = (f32[4,256,128]{2,1,0:T(8,128)S(1)}, f32[4,256,128]{2,1,0:T(8,128)S(1)}, u32[]{:S(2)}, u32[]{:S(2)}) collective-permute-start(f32[4,256,128]{2,1,0:T(8,128)S(1)} %pad_maximum_fusion.5.refs_0_), channel_id=1, source_target_pairs={{0,32},{1,33},{2,34},{3,35},{4,36},{5,37},{6,38},{7,39},{8,40},{9,... | collective-permute-start | bytes 1572872 | tf_op jit(solution)/shard_map/ppermute | solution.py:35
  196.4 29.5 %collective-permute-start.34 = (f32[4,256,128]{2,1,0:T(8,128)S(1)}, f32[4,256,128]{2,1,0:T(8,128)S(1)}, u32[]{:S(2)}, u32[]{:S(2)}) collective-permute-start(f32[4,256,128]{2,1,0:T(8,128)S(1)} %pad_maximum_fusion.5.refs_0_), channel_id=1, source_target_pairs={{0,8},{1,9},{2,10},{3,11},{4,12},{5,13},{6,14},{7,15},{8,0},{9,1},... | collective-permute-start | bytes 1572872 | tf_op jit(solution)/shard_map/ppermute | solution.py:35
  (36 other events, 345.0 us)

commit v3 on v2

--- a/solution.py
+++ b/solution.py
@@ -90,11 +90,17 @@
 
 
 def rows_kernel(spot, child_mask, inv, *refs):
-    gathered = refs[0:4]
-    leads = refs[4:8]
-    edge_twin = refs[8]
+    sources = refs[0:9]
     panel, to_send, rh, rl, ph, pll = refs[9:15]
-    eh, el, lead, vh, vl = refs[15:]
+    eh, el, lead, vh, vl, held, held_leads, edge_twin, sems = refs[15:]
+    gathered = [held.at[k] for k in range(4)]
+    leads = [held_leads.at[k] for k in range(4)]
+    copies = [
+        pltpu.make_async_copy(source, spot_of, sems.at[n])
+        for n, (source, spot_of) in enumerate(zip(sources, gathered + leads + [edge_twin]))
+    ]
+    for n in (0, 4, 8, 1, 5, 2, 6, 3, 7):
+        copies[n].start()
     p, x, core, yhi, z = (spot[n] for n in range(5))
     q = 2 * x + core
     turn = jnp.where(core == 0, 1, 3)
@@ -102,7 +108,10 @@
     a, b = halves(inv[...])
     vh[...] = a
     vl[...] = b
+    copies[8].wait()
     for k in range(4):
+        copies[k].wait()
+        copies[4 + k].wait()
         own_z = lax.rem(z + 16 - turn * k, 4)
         twin_z = lax.rem(z + turn * k, 4)
         for yr in range(2):
@@ -167,7 +176,7 @@
             jax.ShapeDtypeStruct((4, BS, 512), bf16),
             jax.ShapeDtypeStruct((4, BS, 512), bf16),
         ),
-        in_specs=[smem, smem] + [vmem] * 10,
+        in_specs=[smem, smem, vmem] + [pl.BlockSpec(memory_space=pltpu.HBM)] * 9,
         out_specs=[vmem] * 6,
         scratch_shapes=[
             pltpu.VMEM((2, BS, 1024), bf16),
@@ -175,8 +184,12 @@
             pltpu.VMEM((4, BS, 512), f32),
             pltpu.VMEM((512, 512), bf16),
             pltpu.VMEM((512, 512), bf16),
+            pltpu.VMEM((4, 8, BS, 128), f32),
+            pltpu.VMEM((4, 6, BS, 128), f32),
+            pltpu.VMEM((8, BS, 128), f32),
+            pltpu.SemaphoreType.DMA((9,)),
         ],
-        compiler_params=pltpu.CompilerParams(vmem_limit_bytes=40 * 1024 * 1024),
+        compiler_params=pltpu.CompilerParams(vmem_limit_bytes=60 * 1024 * 1024),
         cost_estimate=pl.CostEstimate(flops=4_000_000_000, bytes_accessed=18_000_000, transcendentals=0),
         name="rows",
     )(spot, child_mask, inv, *gathered, *leads, edge_twin)
@@ -319,14 +332,14 @@
 
 
 def gate(values, after):
-    far = pl.BlockSpec(memory_space=pl.ANY)
+    far = pl.BlockSpec(memory_space=pltpu.HBM)
     return pl.pallas_call(
         gate_kernel,
         out_shape=[jax.ShapeDtypeStruct(v.shape, v.dtype) for v in values],
         in_specs=[far] * (len(values) + len(after)),
         out_specs=[far] * len(values),
         input_output_aliases={i: i for i in range(len(values))},
-        compiler_params=pltpu.CompilerParams(vmem_limit_bytes=1024 * 1024),
+        compiler_params=pltpu.CompilerParams(vmem_limit_bytes=60 * 1024 * 1024),
         cost_estimate=pl.CostEstimate(flops=0, bytes_accessed=0, transcendentals=0),
         name="gate",
     )(*values, *after)
@@ -344,49 +357,40 @@
 
     late = parent.reshape(4, BS, 16, 128)[:, :, :2, :].transpose(0, 2, 1, 3) + nothing[0, 0]
     flat = parent.reshape(4 * BS * 16, 128)
-    edge = mine[0]
-
-    at_zero = lambda d: d["ylo"] == 0 and d["x"] == 0
+
+    edges = lax.all_gather(lax.all_gather(mine[0], "x")[0], ("ylo", "yhi"))[:2]
+    edge = jnp.where(yhi == 0, edges, edges[::-1])
     near = send(mine, route(lambda d: {"yhi": 1 - d["yhi"]}))
     cross = send(other, route(lambda d: {"ylo": 1 - d["ylo"]}))
     cross_far = send(other, route(lambda d: {"ylo": 1 - d["ylo"], "yhi": 1 - d["yhi"]}))
     spread = send(late[2:], route(lambda d: {"z": 3 - d["z"]}, lambda d: d["yhi"] == 0 and d["z"] < 2))
-    moved = [send(edge, route(lambda d: {"x": n}, at_zero)) for n in (1, 3, 2)]
-    near, cross, cross_far, spread, *moved = gate([near, cross, cross_far, spread] + moved, [])
+    near, cross, cross_far, spread = gate([near, cross, cross_far, spread], [])
 
     block = jnp.concatenate([mine, near, cross, cross_far])
     lead_piece = jnp.where(z < 2, late[:2], spread)
-    edge = jnp.where(x == 0, edge, jnp.where(x == 1, moved[0], jnp.where(x == 3, moved[1], moved[2])))
-
     ring = route(lambda d: {"z": d["z"] + (1 if d["core"] == 0 else -1)})
     twin = route(lambda d: {"core": 1 - d["core"]})
     swap = route(lambda d: {"ylo": 1 - d["ylo"]})
     around = [route(lambda d: {"x": d["x"] - n}) for n in (1, 3, 2)]
 
-    def target(lane):
+    def target(lane, cross=False):
         def move(d):
             z_to = 2 * (d["x"] % 2) + d["core"]
-            return {"x": d["x"] + d["z"] - z_to, "z": z_to, "core": lane}
+            plane = d["ylo"] + 1 if cross else d["ylo"]
+            return {"ylo": plane, "x": d["x"] + d["z"] - z_to, "z": z_to, "core": lane}
 
         return route(move, lambda d: d["yhi"] == d["x"] // 2)
 
-    def scatter(parts):
-        return [send(part, target(lane)) for lane, part in enumerate(parts)]
+    def scatter(parts, cross=False):
+        return [send(part, target(lane, cross)) for lane, part in enumerate(parts)]
 
     gathered = [block]
-    low = lambda d: d["ylo"] == 0
     arrived = send(block, ring)
     spread = send(lead_piece, route(lambda d: {"yhi": 1}, lambda d: d["yhi"] == 0))
-    edge_up = send(edge, route(lambda d: {"ylo": 1}, low))
-    edge_far = send(edge, route(lambda d: {"yhi": 1 - d["yhi"]}, low))
-    edge_up_far = send(edge, route(lambda d: {"ylo": 1, "yhi": 1 - d["yhi"]}, low))
     pieces = scatter([block[:4], block[4:]])
-    arrived, spread, edge_up, edge_far, edge_up_far, *pieces = gate(
-        [arrived, spread, edge_up, edge_far, edge_up_far] + pieces, []
-    )
+    arrived, spread, *pieces = gate([arrived, spread] + pieces, [])
     gathered.append(arrived)
     lead_piece = jnp.where(yhi == 0, lead_piece, spread).reshape(4, BS, 128)
-    edge = jnp.stack([jnp.where(p == 0, edge, edge_up), jnp.where(p == 0, edge_far, edge_up_far)])
     leads = [jnp.concatenate([lead_piece, edge])]
     quarter = jnp.where(first, pieces[0], pieces[1])
 
@@ -400,14 +404,18 @@
     columns = [jnp.concatenate([quarter, other_quarter])]
     arrived = send(gathered[-1], ring)
     lead_next = send(leads[-1], ring)
-    moving = [send(columns[0], pairs) for pairs in around]
-    arrived, lead_next = gate([arrived, lead_next], [])
+    moving = [send(columns[0], pairs) for pairs in around[:2]]
+    arrived, lead_next, *moving = gate([arrived, lead_next] + moving, [])
     gathered.append(arrived)
     leads.append(lead_next)
-    leads.append(send(leads[-1], ring))
-    moving = gate(moving + [leads[-1]], [])
-    columns += moving[:3]
-    leads[-1] = moving[3]
+    columns += moving
+    onward = route(lambda d: {"x": d["x"] + (1 if d["core"] == 0 else -1)})
+    lead_next = send(leads[-1], ring)
+    relayed = send(jnp.where(first, columns[2], columns[1]), onward)
+    arrays = [send(value, twin) for value in columns]
+    lead_next, relayed, *arrays = gate([lead_next, relayed] + arrays, [])
+    leads.append(lead_next)
+    columns.append(relayed)
 
     edge_own = jnp.concatenate([block[4:] for block in leads])
     edge_twin = send(edge_own, twin)
@@ -416,17 +424,14 @@
     )
     turn = (z - (2 * (x % 2) + core)) % 4
     mine = lax.dynamic_index_in_dim(to_send, turn, 0, keepdims=False)
-    pieces = scatter([mine[:2], mine[2:]])
-    arrays = [send(value, twin) for value in columns[:2]]
-    *pieces, arrays[0], arrays[1] = gate(pieces + arrays, [])
+    pieces = scatter([mine[:2], mine[2:]]) + scatter([mine[:2], mine[2:]], True)
+    arrays.append(send(columns[3], twin))
+    assembled = update_step(spot, child_listed, flat, rh, rl, columns + arrays)
+    *pieces, assembled = gate(pieces + [assembled], [])
     quarter = jnp.where(first, pieces[0], pieces[1])
-    other_quarter = send(quarter, swap)
-    arrays += [send(value, twin) for value in columns[2:]]
-    other_quarter, arrays[2], arrays[3] = gate([other_quarter] + arrays[2:], [])
+    other_quarter = jnp.where(first, pieces[2], pieces[3])
     panels = [jnp.concatenate([quarter, other_quarter])]
     panels += [send(panels[0], pairs) for pairs in around]
-    assembled = update_step(spot, child_listed, flat, rh, rl, columns + arrays)
-    panels[1:] = gate(panels[1:], [assembled])
     panels += [send(value, twin) for value in panels]
     factored = trail_step(
         spot, panel_listed, assembled.reshape(4 * BS, 16, 128), ph, pll, panels

time: 248 us -> 254 us (1.024)
  the two profiles are of different devices: /device:TPU:39 before, /device:TPU:66 now
where the time goes in v3:
time: 254 us; the launch traced here: 250 us
  waiting for transfers between devices  81 us (32%)
  Pallas kernels  53.8 us (21%)
  starting transfers between devices  53 us (21%)
  blocking collectives  30.2 us (12%)
  local copies, waits for them, and re-layouts  21.3 us (8%)
  other arithmetic  9.06 us (4%)
    ppermute x33, waiting for transfers between devices, send(): return lax.ppermute(value, AXES, pairs)  81 us
    ppermute x33, starting transfers between devices, send(): return lax.ppermute(value, AXES, pairs)  53 us
    all_gather x2, blocking collectives, shards(): edges = lax.all_gather(lax.all_gather(mine[0], 'x')[0], ('ylo', 'yhi'))[:2]  30.2 us
    pallas_call x1, Pallas kernels, update_step(): pl.pallas_call(update_kernel, grid=(4,), out_shape=jax.ShapeDtypeStruct(f...  22.1 us
    pallas_call x1, Pallas kernels, trail_step(): pl.pallas_call(trail_kernel, grid=(2, 4), out_shape=jax.ShapeDtypeStruct(...  17.5 us
    unnamed x85, local copies, waits for them, and re-layouts  12.3 us
    pallas_call x1, Pallas kernels, rows_step(): pl.pallas_call(rows_kernel, out_shape=(jax.ShapeDtypeStruct((4, BS, 512),...  11.8 us
  transfers between devices with their start and end apart: 33, of which 12 were waited for; matrix products, arithmetic and copies ran while one was open for 3% of the time, Pallas kernels for 14%

profile of v3, /device:TPU:66, one launch (start us, length us, event | category | flops | bytes accessed | tf_op | source)
XLA Modules:
  0.0 249.6 jit_solution(12091333767111826215)
XLA Ops:
  2.1 2.5 slice.77
  4.5 2.4 place.1
  11.8 2.6 %collective-permute-start = (f32[2,256,128]{2,1,0:T(8,128)S(1)}, f32[2,256,128]{2,1,0:T(8,128)S(1)}, u32[]{:S(2)}, u32[]{:S(2)}) collective-permute-start(f32[2,256,128]{2,1,0:T(8,128)S(1)} %get-tuple-element.77), channel_id=1, source_target_pairs={{0,4},{1,5},{2,6},{3,7},{4,0},{5,1},{6,2},{7,3},{8,12},{9,13},{10,... | collective-permute-start | bytes 786440 | tf_op jit(solution)/shard_map/ppermute | solution.py:35
  16.1 13.4 %all-gather = f32[4,1,256,128]{3,2,1,0:T(8,128)S(1)} all-gather(f32[1,1,256,128]{3,2,1,0:T(8,128)S(1)} %slice.64), channel_id=2, replica_groups=mesh['ylo'=2,'x'=4,'core'=2,'yhi'=2,'z'=4] {'x'}, dimensions={0}, use_global_device_ids=true | all-gather | bytes 655360 | tf_op jit(solution)/shard_map/all_gather | solution.py:361
  31.2 2.3 pad_maximum_fusion.refs_0_
  33.5 1.6 collective-permute-start.4
  35.2 4.4 %collective-permute-start.5 = (f32[2,2,256,128]{3,2,1,0:T(8,128)S(1)}, f32[2,2,256,128]{3,2,1,0:T(8,128)S(1)}, u32[]{:S(2)}, u32[]{:S(2)}) collective-permute-start(f32[2,2,256,128]{3,2,1,0:T(8,128)S(1)} %slice_select_fusion), channel_id=1, source_target_pairs={{0,4},{1,5},{2,6},{3,7},{8,12},{9,13},{10,14},{11,15},{16,20},{17,... | collective-permute-start | bytes 1572872 | tf_op jit(solution)/shard_map/ppermute | solution.py:35
  41.2 6.2 %collective-permute-start.7 = (f32[4,256,128]{2,1,0:T(8,128)}, f32[4,256,128]{2,1,0:T(8,128)S(1)}, u32[]{:S(2)}, u32[]{:S(2)}) collective-permute-start(f32[4,256,128]{2,1,0:T(8,128)} %pad_maximum_fusion.5), channel_id=1, source_target_pairs={{0,8},{1,24},{2,40},{3,56},{8,57},{9,9},{10,25},{11,41},{16,58},{1... | collective-permute-start | bytes 1572872 | tf_op jit(solution)/shard_map/ppermute | solution.py:35
  47.3 16.8 %all-gather.1 = f32[4,1,256,128]{3,2,1,0:T(8,128)S(1)} all-gather(f32[1,1,256,128]{3,2,1,0:T(8,128)S(1)} %slice.80), channel_id=3, replica_groups=mesh['ylo'=2,'x'=4,'core'=2,'yhi'=2,'z'=4] {'ylo','yhi'}, dimensions={0}, use_global_device_ids=true | all-gather | bytes 655360 | tf_op jit(solution)/shard_map/all_gather | solution.py:361
  65.4 3.4 %collective-permute-start.8 = (f32[8,256,128]{2,1,0:T(8,128)}, f32[8,256,128]{2,1,0:T(8,128)}, u32[]{:S(2)}, u32[]{:S(2)}) collective-permute-start(f32[8,256,128]{2,1,0:T(8,128)} %get-tuple-element.41.refs_1_), channel_id=1, source_target_pairs={{0,1},{1,2},{2,3},{3,0},{4,5},{5,6},{6,7},{7,4},{8,11},{9,8},{10,9... | collective-permute-start | bytes 3145736 | tf_op jit(solution)/shard_map/ppermute | solution.py:35
  69.4 12.6 %collective-permute-done.10.refs_2_ = f32[4,256,128]{2,1,0:T(8,128)S(1)} collective-permute-done((f32[4,256,128]{2,1,0:T(8,128)S(1)}, f32[4,256,128]{2,1,0:T(8,128)S(1)}, u32[]{:S(2)}, u32[]{:S(2)}) %collective-permute-start.10) | collective-permute-done | bytes 524320 | tf_op jit(solution)/shard_map/ppermute | solution.py:35
  82.0 7.6 %collective-permute-done.9.refs_1_ = f32[6,256,128]{2,1,0:T(8,128)S(1)} collective-permute-done((f32[6,256,128]{2,1,0:T(8,128)S(1)}, f32[6,256,128]{2,1,0:T(8,128)S(1)}, u32[]{:S(2)}, u32[]{:S(2)}) %collective-permute-start.9) | collective-permute-done | bytes 786464 | tf_op jit(solution)/shard_map/ppermute | solution.py:35
  90.6 2.5 collective-permute-start.11
  93.1 2.1 pad_maximum_fusion.1.refs_0_
  95.2 2.0 collective-permute-start.14
  98.4 15.6 %collective-permute-done.12.refs_1_ = f32[6,256,128]{2,1,0:T(8,128)S(1)} collective-permute-done((f32[6,256,128]{2,1,0:T(8,128)S(1)}, f32[6,256,128]{2,1,0:T(8,128)S(1)}, u32[]{:S(2)}, u32[]{:S(2)}) %collective-permute-start.12) | collective-permute-done | bytes 786464 | tf_op jit(solution)/shard_map/ppermute | solution.py:35
  114.0 5.2 %collective-permute-done.13.refs_2_ = f32[8,256,128]{2,1,0:T(8,128)S(1)} collective-permute-done((f32[8,256,128]{2,1,0:T(8,128)}, f32[8,256,128]{2,1,0:T(8,128)S(1)}, u32[]{:S(2)}, u32[]{:S(2)}) %collective-permute-start.13) | collective-permute-done | bytes 1048608 | tf_op jit(solution)/shard_map/ppermute | solution.py:35
  119.3 2.8 %collective-permute-done.14.refs_3_ = f32[8,256,128]{2,1,0:T(8,128)S(1)} collective-permute-done((f32[8,256,128]{2,1,0:T(8,128)}, f32[8,256,128]{2,1,0:T(8,128)S(1)}, u32[]{:S(2)}, u32[]{:S(2)}) %collective-permute-start.14) | collective-permute-done | bytes 1048608 | tf_op jit(solution)/shard_map/ppermute | solution.py:35
  125.7 2.2 collective-permute-start.15
  128.9 8.8 %collective-permute-done.15.refs_0_ = f32[6,256,128]{2,1,0:T(8,128)S(1)} collective-permute-done((f32[6,256,128]{2,1,0:T(8,128)S(1)}, f32[6,256,128]{2,1,0:T(8,128)S(1)}, u32[]{:S(2)}, u32[]{:S(2)}) %collective-permute-start.15) | collective-permute-done | bytes 786464 | tf_op jit(solution)/shard_map/ppermute | solution.py:35
  137.7 2.7 %collective-permute-done.16.refs_1_ = f32[8,256,128]{2,1,0:T(8,128)} collective-permute-done((f32[8,256,128]{2,1,0:T(8,128)S(1)}, f32[8,256,128]{2,1,0:T(8,128)}, u32[]{:S(2)}, u32[]{:S(2)}) %collective-permute-start.16) | collective-permute-done | bytes 1048608 | tf_op jit(solution)/shard_map/ppermute | solution.py:35
  143.6 1.7 collective-permute-done.20.refs_8_
  145.3 11.8 %rows.1 = (f32[4,256,512]{2,1,0:T(8,128)}, f32[4,4,256,128]{3,2,1,0:T(8,128)}, bf16[4,256,1024]{2,1,0:T(8,128)(2,1)}, bf16[4,256,1024]{2,1,0:T(8,128)(2,1)}, bf1...) custom-call(s32[5]{0:T(128)} %stack.23.spot, s32[2,32,32]{2,1,0:T(8,128)} %child_mask.3, f32[512,512]{1,0:T(8,128)} %inv.1, ...), custom_call_target="tpu_custom_call" | custom-call | flops 4000000000 | bytes 18000000 | tf_op jit(solution)/shard_map/rows/pallas_call | solution.py:169
  158.8 2.7 %collective-permute-start.23 = (f32[2,256,128]{2,1,0:T(8,128)S(1)}, f32[2,256,128]{2,1,0:T(8,128)S(1)}, u32[]{:S(2)}, u32[]{:S(2)}) collective-permute-start(f32[2,256,128]{2,1,0:T(8,128)S(1)} %get-tuple-element.75), channel_id=1, source_target_pairs={{0,64},{1,80},{2,96},{3,112},{8,113},{9,65},{10,81},{11,97},{16,11... | collective-permute-start | bytes 786440 | tf_op jit(solution)/shard_map/ppermute | solution.py:35
  161.6 11.2 %collective-permute-start.22 = (f32[2,256,128]{2,1,0:T(8,128)S(1)}, f32[2,256,128]{2,1,0:T(8,128)S(1)}, u32[]{:S(2)}, u32[]{:S(2)}) collective-permute-start(f32[2,256,128]{2,1,0:T(8,128)S(1)} %get-tuple-element.74), channel_id=1, source_target_pairs={{0,8},{1,24},{2,40},{3,56},{8,57},{9,9},{10,25},{11,41},{16,58},{1... | collective-permute-start | bytes 786440 | tf_op jit(solution)/shard_map/ppermute | solution.py:35
  172.8 3.8 %collective-permute-start.24 = (f32[2,256,128]{2,1,0:T(8,128)S(1)}, f32[2,256,128]{2,1,0:T(8,128)}, u32[]{:S(2)}, u32[]{:S(2)}) collective-permute-start(f32[2,256,128]{2,1,0:T(8,128)S(1)} %get-tuple-element.74), channel_id=1, source_target_pairs={{0,72},{1,88},{2,104},{3,120},{8,121},{9,73},{10,89},{11,105},{16,... | collective-permute-start | bytes 786440 | tf_op jit(solution)/shard_map/ppermute | solution.py:35
  177.9 1.6 copy-done.10
  179.5 1.6 copy-done.11
  181.0 22.1 %update.1.refs_4_ = f32[16384,128]{1,0:T(8,128)} custom-call(s32[5]{0:T(128)S(1)} %copy-done.13, s32[2,32,32]{2,1,0:T(8,128)S(1)} %copy-done.12, f32[16384,128]{1,0:T(8,128)} %bitcast.35, bf16[4,256,1024]{2,1,0:T(8,128)(2,1)S(1)} %copy-done.10, bf16[4,256,1024]{2,1,0:T(8,128)(2,1)S(1)} %copy-done.11, f32[8,256,128]{2,1,0:T(8,128)} %pad_maximum_fusion.1.refs_0_, ...), custom_call_target="tpu_custom_call" | custom-call | flops 6400000000 | bytes 28000000 | tf_op jit(solution)/shard_map/update/pallas_call | solution.py:251
  205.4 2.0 collective-permute-start.27
  207.4 21.2 %collective-permute-done.26.refs_1_ = f32[4,256,128]{2,1,0:T(8,128)S(1)} collective-permute-done((f32[4,256,128]{2,1,0:T(8,128)S(1)}, f32[4,256,128]{2,1,0:T(8,128)S(1)}, u32[]{:S(2)}, u32[]{:S(2)}) %collective-permute-start.26) | collective-permute-done | bytes 524320 | tf_op jit(solution)/shard_map/ppermute | solution.py:35
  232.0 17.5 %trail.1 = f32[1024,16,128]{2,1,0:T(8,128)} custom-call(s32[5]{0:T(128)S(1)} %copy-done.13, s32[64,64]{1,0:T(8,128)S(1)} %copy-done.14, f32[1024,16,128]{2,1,0:T(8,128)} %bitcast.33, bf16[4,256,512]{2,1,0:T(8,128)(2,1)S(1)} %copy-done.15, bf16[4,256,512]{2,1,0:T(8,128)(2,1)S(1)} %copy-done.16, f32[4,256,128]{2,1,0:T(8,128)S(1)} %pad_maximum_fusion.6.refs_0_, ...), custom_call_target="tpu_custom_call" | custom-call | flops 6400000000 | bytes 22000000 | tf_op jit(solution)/shard_map/trail/pallas_call | solution.py:314
  (158 shorter events, 31.6 us)
Async XLA Ops:
  9.8 19.8 %collective-permute-start.3 = (f32[2,2,256,128]{3,2,1,0:T(8,128)}, f32[2,2,256,128]{3,2,1,0:T(8,128)S(1)}, u32[]{:S(2)}, u32[]{:S(2)}) collective-permute-start(f32[2,2,256,128]{3,2,1,0:T(8,128)} %slice.78), channel_id=1, source_target_pairs={{0,3},{1,2},{8,11},{9,10},{16,19},{17,18},{24,27},{25,26},{32,35},... | collective-permute-start | bytes 1572872 | tf_op jit(solution)/shard_map/ppermute | solution.py:35
  11.8 17.7 %collective-permute-start = (f32[2,256,128]{2,1,0:T(8,128)S(1)}, f32[2,256,128]{2,1,0:T(8,128)S(1)}, u32[]{:S(2)}, u32[]{:S(2)}) collective-permute-start(f32[2,256,128]{2,1,0:T(8,128)S(1)} %get-tuple-element.77), channel_id=1, source_target_pairs={{0,4},{1,5},{2,6},{3,7},{4,0},{5,1},{6,2},{7,3},{8,12},{9,13},{10,... | collective-permute-start | bytes 786440 | tf_op jit(solution)/shard_map/ppermute | solution.py:35
  14.4 15.1 %collective-permute-start.1 = (f32[2,256,128]{2,1,0:T(8,128)}, f32[2,256,128]{2,1,0:T(8,128)S(1)}, u32[]{:S(2)}, u32[]{:S(2)}) collective-permute-start(f32[2,256,128]{2,1,0:T(8,128)} %get-tuple-element.76), channel_id=1, source_target_pairs={{0,64},{1,65},{2,66},{3,67},{4,68},{5,69},{6,70},{7,71},{8,72},{9,... | collective-permute-start | bytes 786440 | tf_op jit(solution)/shard_map/ppermute | solution.py:35
  15.1 14.5 %collective-permute-start.2 = (f32[2,256,128]{2,1,0:T(8,128)}, f32[2,256,128]{2,1,0:T(8,128)S(1)}, u32[]{:S(2)}, u32[]{:S(2)}) collective-permute-start(f32[2,256,128]{2,1,0:T(8,128)} %get-tuple-element.76), channel_id=1, source_target_pairs={{0,68},{1,69},{2,70},{3,71},{4,64},{5,65},{6,66},{7,67},{8,76},{9,... | collective-permute-start | bytes 786440 | tf_op jit(solution)/shard_map/ppermute | solution.py:35
  33.5 30.8 %collective-permute-start.4 = (f32[8,256,128]{2,1,0:T(8,128)}, f32[8,256,128]{2,1,0:T(8,128)}, u32[]{:S(2)}, u32[]{:S(2)}) collective-permute-start(f32[8,256,128]{2,1,0:T(8,128)} %pad_maximum_fusion.refs_0_), channel_id=1, source_target_pairs={{0,1},{1,2},{2,3},{3,0},{4,5},{5,6},{6,7},{7,4},{8,11},{9,8},{10,9... | collective-permute-start | bytes 3145736 | tf_op jit(solution)/shard_map/ppermute | solution.py:35
  35.2 29.0 %collective-permute-start.5 = (f32[2,2,256,128]{3,2,1,0:T(8,128)S(1)}, f32[2,2,256,128]{3,2,1,0:T(8,128)S(1)}, u32[]{:S(2)}, u32[]{:S(2)}) collective-permute-start(f32[2,2,256,128]{3,2,1,0:T(8,128)S(1)} %slice_select_fusion), channel_id=1, source_target_pairs={{0,4},{1,5},{2,6},{3,7},{8,12},{9,13},{10,14},{11,15},{16,20},{17,... | collective-permute-start | bytes 1572872 | tf_op jit(solution)/shard_map/ppermute | solution.py:35
  39.6 24.6 %collective-permute-start.6 = (f32[4,256,128]{2,1,0:T(8,128)S(1)}, f32[4,256,128]{2,1,0:T(8,128)S(1)}, u32[]{:S(2)}, u32[]{:S(2)}) collective-permute-start(f32[4,256,128]{2,1,0:T(8,128)S(1)} %pad_maximum_fusion.4), channel_id=1, source_target_pairs={{0,0},{1,16},{2,32},{3,48},{8,49},{9,1},{10,17},{11,33},{16,50},{1... | collective-permute-start | bytes 1572872 | tf_op jit(solution)/shard_map/ppermute | solution.py:35
  41.2 23.1 %collective-permute-start.7 = (f32[4,256,128]{2,1,0:T(8,128)}, f32[4,256,128]{2,1,0:T(8,128)S(1)}, u32[]{:S(2)}, u32[]{:S(2)}) collective-permute-start(f32[4,256,128]{2,1,0:T(8,128)} %pad_maximum_fusion.5), channel_id=1, source_target_pairs={{0,8},{1,24},{2,40},{3,56},{8,57},{9,9},{10,25},{11,41},{16,58},{1... | collective-permute-start | bytes 1572872 | tf_op jit(solution)/shard_map/ppermute | solution.py:35
  65.4 24.3 %collective-permute-start.8 = (f32[8,256,128]{2,1,0:T(8,128)}, f32[8,256,128]{2,1,0:T(8,128)}, u32[]{:S(2)}, u32[]{:S(2)}) collective-permute-start(f32[8,256,128]{2,1,0:T(8,128)} %get-tuple-element.41.refs_1_), channel_id=1, source_target_pairs={{0,1},{1,2},{2,3},{3,0},{4,5},{5,6},{6,7},{7,4},{8,11},{9,8},{10,9... | collective-permute-start | bytes 3145736 | tf_op jit(solution)/shard_map/ppermute | solution.py:35
  68.9 20.8 %collective-permute-start.9 = (f32[6,256,128]{2,1,0:T(8,128)S(1)}, f32[6,256,128]{2,1,0:T(8,128)S(1)}, u32[]{:S(2)}, u32[]{:S(2)}) collective-permute-start(f32[6,256,128]{2,1,0:T(8,128)S(1)} %pad_maximum_fusion.3.refs_4_), channel_id=1, source_target_pairs={{0,1},{1,2},{2,3},{3,0},{4,5},{5,6},{6,7},{7,4},{8,11},{9,8},{10,9... | collective-permute-start | bytes 2359304 | tf_op jit(solution)/shard_map/ppermute | solution.py:35
  69.0 13.0 %collective-permute-start.10 = (f32[4,256,128]{2,1,0:T(8,128)S(1)}, f32[4,256,128]{2,1,0:T(8,128)S(1)}, u32[]{:S(2)}, u32[]{:S(2)}) collective-permute-start(f32[4,256,128]{2,1,0:T(8,128)S(1)} %broadcast_select_fusion.1), channel_id=1, source_target_pairs={{0,64},{1,65},{2,66},{3,67},{4,68},{5,69},{6,70},{7,71},{8,72},{9,... | collective-permute-start | bytes 1572872 | tf_op jit(solution)/shard_map/ppermute | solution.py:35
  90.6 23.4 %collective-permute-start.11 = (f32[8,256,128]{2,1,0:T(8,128)}, f32[8,256,128]{2,1,0:T(8,128)S(1)}, u32[]{:S(2)}, u32[]{:S(2)}) collective-permute-start(f32[8,256,128]{2,1,0:T(8,128)} %get-tuple-element.45.refs_2_), channel_id=1, source_target_pairs={{0,1},{1,2},{2,3},{3,0},{4,5},{5,6},{6,7},{7,4},{8,11},{9,8},{10,9... | collective-permute-start | bytes 3145736 | tf_op jit(solution)/shard_map/ppermute | solution.py:35
  95.2 24.1 %collective-permute-start.13 = (f32[8,256,128]{2,1,0:T(8,128)}, f32[8,256,128]{2,1,0:T(8,128)S(1)}, u32[]{:S(2)}, u32[]{:S(2)}) collective-permute-start(f32[8,256,128]{2,1,0:T(8,128)} %pad_maximum_fusion.1.refs_0_), channel_id=1, source_target_pairs={{0,48},{1,49},{2,50},{3,51},{4,52},{5,53},{6,54},{7,55},{8,56},{9,... | collective-permute-start | bytes 3145736 | tf_op jit(solution)/shard_map/ppermute | solution.py:35
  95.2 26.9 %collective-permute-start.14 = (f32[8,256,128]{2,1,0:T(8,128)}, f32[8,256,128]{2,1,0:T(8,128)S(1)}, u32[]{:S(2)}, u32[]{:S(2)}) collective-permute-start(f32[8,256,128]{2,1,0:T(8,128)} %pad_maximum_fusion.1.refs_0_), channel_id=1, source_target_pairs={{0,16},{1,17},{2,18},{3,19},{4,20},{5,21},{6,22},{7,23},{8,24},{9,... | collective-permute-start | bytes 3145736 | tf_op jit(solution)/shard_map/ppermute | solution.py:35
  97.2 16.8 %collective-permute-start.12 = (f32[6,256,128]{2,1,0:T(8,128)S(1)}, f32[6,256,128]{2,1,0:T(8,128)S(1)}, u32[]{:S(2)}, u32[]{:S(2)}) collective-permute-start(f32[6,256,128]{2,1,0:T(8,128)S(1)} %copy-done.33), channel_id=1, source_target_pairs={{0,1},{1,2},{2,3},{3,0},{4,5},{5,6},{6,7},{7,4},{8,11},{9,8},{10,9... | collective-permute-start | bytes 2359304 | tf_op jit(solution)/shard_map/ppermute | solution.py:35
  98.4 30.5 %collective-permute-start.17 = (f32[8,256,128]{2,1,0:T(8,128)}, f32[8,256,128]{2,1,0:T(8,128)S(1)}, u32[]{:S(2)}, u32[]{:S(2)}) collective-permute-start(f32[8,256,128]{2,1,0:T(8,128)} %pad_maximum_fusion.1.refs_0_), channel_id=1, source_target_pairs={{0,8},{1,9},{2,10},{3,11},{4,12},{5,13},{6,14},{7,15},{8,0},{9,1},... | collective-permute-start | bytes 3145736 | tf_op jit(solution)/shard_map/ppermute | solution.py:35
  124.5 15.9 %collective-permute-start.16 = (f32[8,256,128]{2,1,0:T(8,128)S(1)}, f32[8,256,128]{2,1,0:T(8,128)}, u32[]{:S(2)}, u32[]{:S(2)}) collective-permute-start(f32[8,256,128]{2,1,0:T(8,128)S(1)} %broadcast_select_fusion), channel_id=1, source_target_pairs={{0,16},{1,17},{2,18},{3,19},{4,20},{5,21},{6,22},{7,23},{8,56},{9,... | collective-permute-start | bytes 3145736 | tf_op jit(solution)/shard_map/ppermute | solution.py:35
  125.2 15.2 %collective-permute-start.18 = (f32[8,256,128]{2,1,0:T(8,128)S(1)}, f32[8,256,128]{2,1,0:T(8,128)S(1)}, u32[]{:S(2)}, u32[]{:S(2)}) collective-permute-start(f32[8,256,128]{2,1,0:T(8,128)S(1)} %copy-done.3), channel_id=1, source_target_pairs={{0,8},{1,9},{2,10},{3,11},{4,12},{5,13},{6,14},{7,15},{8,0},{9,1},... | collective-permute-start | bytes 3145736 | tf_op jit(solution)/shard_map/ppermute | solution.py:35
  125.2 16.2 %collective-permute-start.19 = (f32[8,256,128]{2,1,0:T(8,128)S(1)}, f32[8,256,128]{2,1,0:T(8,128)}, u32[]{:S(2)}, u32[]{:S(2)}) collective-permute-start(f32[8,256,128]{2,1,0:T(8,128)S(1)} %copy-done.5), channel_id=1, source_target_pairs={{0,8},{1,9},{2,10},{3,11},{4,12},{5,13},{6,14},{7,15},{8,0},{9,1},... | collective-permute-start | bytes 3145736 | tf_op jit(solution)/shard_map/ppermute | solution.py:35
  125.7 12.0 %collective-permute-start.15 = (f32[6,256,128]{2,1,0:T(8,128)S(1)}, f32[6,256,128]{2,1,0:T(8,128)S(1)}, u32[]{:S(2)}, u32[]{:S(2)}) collective-permute-start(f32[6,256,128]{2,1,0:T(8,128)S(1)} %copy-done.35), channel_id=1, source_target_pairs={{0,1},{1,2},{2,3},{3,0},{4,5},{5,6},{6,7},{7,4},{8,11},{9,8},{10,9... | collective-permute-start | bytes 2359304 | tf_op jit(solution)/shard_map/ppermute | solution.py:35
  142.4 2.9 %collective-permute-start.20 = (f32[8,256,128]{2,1,0:T(8,128)S(1)}, f32[8,256,128]{2,1,0:T(8,128)}, u32[]{:S(2)}, u32[]{:S(2)}) collective-permute-start(f32[8,256,128]{2,1,0:T(8,128)S(1)} %pad_maximum_fusion.2), channel_id=1, source_target_pairs={{0,8},{1,9},{2,10},{3,11},{4,12},{5,13},{6,14},{7,15},{8,0},{9,1},... | collective-permute-start | bytes 3145736 | tf_op jit(solution)/shard_map/ppermute | solution.py:35
  142.5 34.1 %collective-permute-start.25 = (f32[8,256,128]{2,1,0:T(8,128)}, f32[8,256,128]{2,1,0:T(8,128)}, u32[]{:S(2)}, u32[]{:S(2)}) collective-permute-start(f32[8,256,128]{2,1,0:T(8,128)} %get-tuple-element.56.refs_3_), channel_id=1, source_target_pairs={{0,8},{1,9},{2,10},{3,11},{4,12},{5,13},{6,14},{7,15},{8,0},{9,1},... | collective-permute-start | bytes 3145736 | tf_op jit(solution)/shard_map/ppermute | solution.py:35
  158.2 45.0 %collective-permute-start.21 = (f32[2,256,128]{2,1,0:T(8,128)S(1)}, f32[2,256,128]{2,1,0:T(8,128)S(1)}, u32[]{:S(2)}, u32[]{:S(2)}) collective-permute-start(f32[2,256,128]{2,1,0:T(8,128)S(1)} %get-tuple-element.75), channel_id=1, source_target_pairs={{0,0},{1,16},{2,32},{3,48},{8,49},{9,1},{10,17},{11,33},{16,50},{1... | collective-permute-start | bytes 786440 | tf_op jit(solution)/shard_map/ppermute | solution.py:35
  158.8 44.3 %collective-permute-start.23 = (f32[2,256,128]{2,1,0:T(8,128)S(1)}, f32[2,256,128]{2,1,0:T(8,128)S(1)}, u32[]{:S(2)}, u32[]{:S(2)}) collective-permute-start(f32[2,256,128]{2,1,0:T(8,128)S(1)} %get-tuple-element.75), channel_id=1, source_target_pairs={{0,64},{1,80},{2,96},{3,112},{8,113},{9,65},{10,81},{11,97},{16,11... | collective-permute-start | bytes 786440 | tf_op jit(solution)/shard_map/ppermute | solution.py:35
  161.6 41.6 %collective-permute-start.22 = (f32[2,256,128]{2,1,0:T(8,128)S(1)}, f32[2,256,128]{2,1,0:T(8,128)S(1)}, u32[]{:S(2)}, u32[]{:S(2)}) collective-permute-start(f32[2,256,128]{2,1,0:T(8,128)S(1)} %get-tuple-element.74), channel_id=1, source_target_pairs={{0,8},{1,24},{2,40},{3,56},{8,57},{9,9},{10,25},{11,41},{16,58},{1... | collective-permute-start | bytes 786440 | tf_op jit(solution)/shard_map/ppermute | solution.py:35
  172.8 30.3 %collective-permute-start.24 = (f32[2,256,128]{2,1,0:T(8,128)S(1)}, f32[2,256,128]{2,1,0:T(8,128)}, u32[]{:S(2)}, u32[]{:S(2)}) collective-permute-start(f32[2,256,128]{2,1,0:T(8,128)S(1)} %get-tuple-element.74), channel_id=1, source_target_pairs={{0,72},{1,88},{2,104},{3,120},{8,121},{9,73},{10,89},{11,105},{16,... | collective-permute-start | bytes 786440 | tf_op jit(solution)/shard_map/ppermute | solution.py:35
  205.3 23.3 %collective-permute-start.26 = (f32[4,256,128]{2,1,0:T(8,128)S(1)}, f32[4,256,128]{2,1,0:T(8,128)S(1)}, u32[]{:S(2)}, u32[]{:S(2)}) collective-permute-start(f32[4,256,128]{2,1,0:T(8,128)S(1)} %pad_maximum_fusion.6.refs_0_), channel_id=1, source_target_pairs={{0,48},{1,49},{2,50},{3,51},{4,52},{5,53},{6,54},{7,55},{8,56},{9,... | collective-permute-start | bytes 1572872 | tf_op jit(solution)/shard_map/ppermute | solution.py:35
  205.4 23.2 %collective-permute-start.27 = (f32[4,256,128]{2,1,0:T(8,128)S(1)}, f32[4,256,128]{2,1,0:T(8,128)S(1)}, u32[]{:S(2)}, u32[]{:S(2)}) collective-permute-start(f32[4,256,128]{2,1,0:T(8,128)S(1)} %pad_maximum_fusion.6.refs_0_), channel_id=1, source_target_pairs={{0,16},{1,17},{2,18},{3,19},{4,20},{5,21},{6,22},{7,23},{8,24},{9,... | collective-permute-start | bytes 1572872 | tf_op jit(solution)/shard_map/ppermute | solution.py:35
  207.4 21.7 %collective-permute-start.28 = (f32[4,256,128]{2,1,0:T(8,128)S(1)}, f32[4,256,128]{2,1,0:T(8,128)S(1)}, u32[]{:S(2)}, u32[]{:S(2)}) collective-permute-start(f32[4,256,128]{2,1,0:T(8,128)S(1)} %pad_maximum_fusion.6.refs_0_), channel_id=1, source_target_pairs={{0,32},{1,33},{2,34},{3,35},{4,36},{5,37},{6,38},{7,39},{8,40},{9,... | collective-permute-start | bytes 1572872 | tf_op jit(solution)/shard_map/ppermute | solution.py:35
  207.4 21.8 %collective-permute-start.29 = (f32[4,256,128]{2,1,0:T(8,128)S(1)}, f32[4,256,128]{2,1,0:T(8,128)S(1)}, u32[]{:S(2)}, u32[]{:S(2)}) collective-permute-start(f32[4,256,128]{2,1,0:T(8,128)S(1)} %pad_maximum_fusion.6.refs_0_), channel_id=1, source_target_pairs={{0,8},{1,9},{2,10},{3,11},{4,12},{5,13},{6,14},{7,15},{8,0},{9,1},... | collective-permute-start | bytes 1572872 | tf_op jit(solution)/shard_map/ppermute | solution.py:35
  228.6 2.7 %collective-permute-start.31 = (f32[4,256,128]{2,1,0:T(8,128)S(1)}, f32[4,256,128]{2,1,0:T(8,128)S(1)}, u32[]{:S(2)}, u32[]{:S(2)}) collective-permute-start(f32[4,256,128]{2,1,0:T(8,128)S(1)} %collective-permute-done.27.refs_2_), channel_id=1, source_target_pairs={{0,8},{1,9},{2,10},{3,11},{4,12},{5,13},{6,14},{7,15},{8,0},{9,1},... | collective-permute-start | bytes 1572872 | tf_op jit(solution)/shard_map/ppermute | solution.py:35
  229.1 2.9 %collective-permute-start.32 = (f32[4,256,128]{2,1,0:T(8,128)S(1)}, f32[4,256,128]{2,1,0:T(8,128)S(1)}, u32[]{:S(2)}, u32[]{:S(2)}) collective-permute-start(f32[4,256,128]{2,1,0:T(8,128)S(1)} %collective-permute-done.28.refs_3_), channel_id=1, source_target_pairs={{0,8},{1,9},{2,10},{3,11},{4,12},{5,13},{6,14},{7,15},{8,0},{9,1},... | collective-permute-start | bytes 1572872 | tf_op jit(solution)/shard_map/ppermute | solution.py:35
  (43 other events, 326.1 us)

commit v4 on v3

--- a/solution.py
+++ b/solution.py
@@ -331,15 +331,15 @@
     pass
 
 
-def gate(values, after):
-    far = pl.BlockSpec(memory_space=pltpu.HBM)
+def gate(values, after, kind=pltpu.HBM, room=60):
+    far = pl.BlockSpec(memory_space=kind)
     return pl.pallas_call(
         gate_kernel,
         out_shape=[jax.ShapeDtypeStruct(v.shape, v.dtype) for v in values],
         in_specs=[far] * (len(values) + len(after)),
         out_specs=[far] * len(values),
         input_output_aliases={i: i for i in range(len(values))},
-        compiler_params=pltpu.CompilerParams(vmem_limit_bytes=60 * 1024 * 1024),
+        compiler_params=pltpu.CompilerParams(vmem_limit_bytes=room * 1024 * 1024),
         cost_estimate=pl.CostEstimate(flops=0, bytes_accessed=0, transcendentals=0),
         name="gate",
     )(*values, *after)
@@ -424,15 +424,17 @@
     )
     turn = (z - (2 * (x % 2) + core)) % 4
     mine = lax.dynamic_index_in_dim(to_send, turn, 0, keepdims=False)
-    pieces = scatter([mine[:2], mine[2:]]) + scatter([mine[:2], mine[2:]], True)
+    pieces = gate(scatter([mine[:2], mine[2:]]), [], pl.ANY, 1)
+    quarter = jnp.where(first, pieces[0], pieces[1])
     arrays.append(send(columns[3], twin))
-    assembled = update_step(spot, child_listed, flat, rh, rl, columns + arrays)
-    *pieces, assembled = gate(pieces + [assembled], [])
-    quarter = jnp.where(first, pieces[0], pieces[1])
-    other_quarter = jnp.where(first, pieces[2], pieces[3])
+    other_quarter, arrays[3] = gate([send(quarter, swap), arrays[3]], [], pl.ANY, 1)
     panels = [jnp.concatenate([quarter, other_quarter])]
     panels += [send(panels[0], pairs) for pairs in around]
-    panels += [send(value, twin) for value in panels]
+    assembled = update_step(spot, child_listed, flat, rh, rl, columns + arrays)
+    twins = [send(panels[0], twin)]
+    (assembled,) = gate([assembled], [])
+    panels[1:] = gate(panels[1:], [assembled], pl.ANY, 1)
+    panels += twins + [send(value, twin) for value in panels[1:]]
     factored = trail_step(
         spot, panel_listed, assembled.reshape(4 * BS, 16, 128), ph, pll, panels
     )

time: 254 us -> 244 us (0.961); the launches traced: 250 us -> 243 us
  waiting for transfers between devices: 81 us -> 67.9 us
  Pallas kernels: 53.8 us -> 57.2 us
    ppermute x33 -> x32, waiting for transfers between devices: 81 us -> 67.9 us  [send(): return lax.ppermute(value, AXES, pairs)]
    pallas_call x1, Pallas kernels: 17.5 us -> 21.2 us  [trail_step(): pl.pallas_call(trail_kernel, grid=(2, 4), out_shape=jax.ShapeDtypeStruct(...]
    ppermute x33 -> x32, starting transfers between devices: 53 us -> 54.2 us  [send(): return lax.ppermute(value, AXES, pairs)]
  transfers between devices with their start and end apart: 33 -> 32, of which waited for: 12 -> 13; matrix products, arithmetic and copies ran while one was open for 3% -> 3% of each run, Pallas kernels for 14% -> 14%
where the time goes in v4:
time: 244 us; the launch traced here: 243 us
  waiting for transfers between devices  67.9 us (28%)
  Pallas kernels  57.2 us (23%)
  starting transfers between devices  54.2 us (22%)
  blocking collectives  30.2 us (12%)
  local copies, waits for them, and re-layouts  22.3 us (9%)
  other arithmetic  9.62 us (4%)
    ppermute x32, waiting for transfers between devices, send(): return lax.ppermute(value, AXES, pairs)  67.9 us
    ppermute x32, starting transfers between devices, send(): return lax.ppermute(value, AXES, pairs)  54.2 us
    all_gather x2, blocking collectives, shards(): edges = lax.all_gather(lax.all_gather(mine[0], 'x')[0], ('ylo', 'yhi'))[:2]  30.2 us
    pallas_call x1, Pallas kernels, update_step(): pl.pallas_call(update_kernel, grid=(4,), out_shape=jax.ShapeDtypeStruct(f...  21.7 us
    pallas_call x1, Pallas kernels, trail_step(): pl.pallas_call(trail_kernel, grid=(2, 4), out_shape=jax.ShapeDtypeStruct(...  21.2 us
    unnamed x85, local copies, waits for them, and re-layouts  13.2 us
    pallas_call x1, Pallas kernels, rows_step(): pl.pallas_call(rows_kernel, out_shape=(jax.ShapeDtypeStruct((4, BS, 512),...  11.8 us
  transfers between devices with their start and end apart: 32, of which 13 were waited for; matrix products, arithmetic and copies ran while one was open for 3% of the time, Pallas kernels for 14%

profile of v4, /device:TPU:66, one launch (start us, length us, event | category | flops | bytes accessed | tf_op | source)
XLA Modules:
  0.0 242.6 jit_solution(2099028193134475875)
XLA Ops:
  2.1 2.5 %slice.75 = f32[4,256,2,128]{3,2,1,0:T(2,128)S(1)} slice(f32[4,256,16,128]{3,2,1,0:T(8,128)} %bitcast.34), slice={[0:4], [0:256], [0:2], [0:128]} | slice | bytes 2097152 | tf_op jit(solution)/shard_map/slice | solution.py:358
  4.5 2.4 place.1
  11.8 2.6 %collective-permute-start = (f32[2,256,128]{2,1,0:T(8,128)S(1)}, f32[2,256,128]{2,1,0:T(8,128)S(1)}, u32[]{:S(2)}, u32[]{:S(2)}) collective-permute-start(f32[2,256,128]{2,1,0:T(8,128)S(1)} %get-tuple-element.81), channel_id=1, source_target_pairs={{0,4},{1,5},{2,6},{3,7},{4,0},{5,1},{6,2},{7,3},{8,12},{9,13},{10,... | collective-permute-start | bytes 786440 | tf_op jit(solution)/shard_map/ppermute | solution.py:35
  16.1 13.4 %all-gather = f32[4,1,256,128]{3,2,1,0:T(8,128)S(1)} all-gather(f32[1,1,256,128]{3,2,1,0:T(8,128)S(1)} %slice.62), channel_id=2, replica_groups=mesh['ylo'=2,'x'=4,'core'=2,'yhi'=2,'z'=4] {'x'}, dimensions={0}, use_global_device_ids=true | all-gather | bytes 655360 | tf_op jit(solution)/shard_map/all_gather | solution.py:361
  31.2 2.3 pad_maximum_fusion.refs_0_
  33.5 1.6 collective-permute-start.4
  35.2 4.4 %collective-permute-start.5 = (f32[2,2,256,128]{3,2,1,0:T(8,128)S(1)}, f32[2,2,256,128]{3,2,1,0:T(8,128)S(1)}, u32[]{:S(2)}, u32[]{:S(2)}) collective-permute-start(f32[2,2,256,128]{3,2,1,0:T(8,128)S(1)} %slice_select_fusion), channel_id=1, source_target_pairs={{0,4},{1,5},{2,6},{3,7},{8,12},{9,13},{10,14},{11,15},{16,20},{17,... | collective-permute-start | bytes 1572872 | tf_op jit(solution)/shard_map/ppermute | solution.py:35
  41.2 6.2 %collective-permute-start.7 = (f32[4,256,128]{2,1,0:T(8,128)}, f32[4,256,128]{2,1,0:T(8,128)S(1)}, u32[]{:S(2)}, u32[]{:S(2)}) collective-permute-start(f32[4,256,128]{2,1,0:T(8,128)} %pad_maximum_fusion.5), channel_id=1, source_target_pairs={{0,8},{1,24},{2,40},{3,56},{8,57},{9,9},{10,25},{11,41},{16,58},{1... | collective-permute-start | bytes 1572872 | tf_op jit(solution)/shard_map/ppermute | solution.py:35
  47.3 16.8 %all-gather.1 = f32[4,1,256,128]{3,2,1,0:T(8,128)S(1)} all-gather(f32[1,1,256,128]{3,2,1,0:T(8,128)S(1)} %slice.78), channel_id=3, replica_groups=mesh['ylo'=2,'x'=4,'core'=2,'yhi'=2,'z'=4] {'ylo','yhi'}, dimensions={0}, use_global_device_ids=true | all-gather | bytes 655360 | tf_op jit(solution)/shard_map/all_gather | solution.py:361
  65.4 3.4 %collective-permute-start.8 = (f32[8,256,128]{2,1,0:T(8,128)}, f32[8,256,128]{2,1,0:T(8,128)}, u32[]{:S(2)}, u32[]{:S(2)}) collective-permute-start(f32[8,256,128]{2,1,0:T(8,128)} %get-tuple-element.43.refs_1_), channel_id=1, source_target_pairs={{0,1},{1,2},{2,3},{3,0},{4,5},{5,6},{6,7},{7,4},{8,11},{9,8},{10,9... | collective-permute-start | bytes 3145736 | tf_op jit(solution)/shard_map/ppermute | solution.py:35
  69.4 12.6 %collective-permute-done.10.refs_2_ = f32[4,256,128]{2,1,0:T(8,128)S(1)} collective-permute-done((f32[4,256,128]{2,1,0:T(8,128)S(1)}, f32[4,256,128]{2,1,0:T(8,128)S(1)}, u32[]{:S(2)}, u32[]{:S(2)}) %collective-permute-start.10) | collective-permute-done | bytes 524320 | tf_op jit(solution)/shard_map/ppermute | solution.py:35
  82.0 7.6 %collective-permute-done.9.refs_1_ = f32[6,256,128]{2,1,0:T(8,128)S(1)} collective-permute-done((f32[6,256,128]{2,1,0:T(8,128)S(1)}, f32[6,256,128]{2,1,0:T(8,128)S(1)}, u32[]{:S(2)}, u32[]{:S(2)}) %collective-permute-start.9) | collective-permute-done | bytes 786464 | tf_op jit(solution)/shard_map/ppermute | solution.py:35
  90.6 2.5 %collective-permute-start.11 = (f32[8,256,128]{2,1,0:T(8,128)}, f32[8,256,128]{2,1,0:T(8,128)S(1)}, u32[]{:S(2)}, u32[]{:S(2)}) collective-permute-start(f32[8,256,128]{2,1,0:T(8,128)} %get-tuple-element.47.refs_2_), channel_id=1, source_target_pairs={{0,1},{1,2},{2,3},{3,0},{4,5},{5,6},{6,7},{7,4},{8,11},{9,8},{10,9... | collective-permute-start | bytes 3145736 | tf_op jit(solution)/shard_map/ppermute | solution.py:35
  93.0 2.1 pad_maximum_fusion.1.refs_0_
  95.2 2.0 collective-permute-start.14
  98.4 15.6 %collective-permute-done.12.refs_1_ = f32[6,256,128]{2,1,0:T(8,128)S(1)} collective-permute-done((f32[6,256,128]{2,1,0:T(8,128)S(1)}, f32[6,256,128]{2,1,0:T(8,128)S(1)}, u32[]{:S(2)}, u32[]{:S(2)}) %collective-permute-start.12) | collective-permute-done | bytes 786464 | tf_op jit(solution)/shard_map/ppermute | solution.py:35
  114.0 5.2 %collective-permute-done.13.refs_2_ = f32[8,256,128]{2,1,0:T(8,128)S(1)} collective-permute-done((f32[8,256,128]{2,1,0:T(8,128)}, f32[8,256,128]{2,1,0:T(8,128)S(1)}, u32[]{:S(2)}, u32[]{:S(2)}) %collective-permute-start.13) | collective-permute-done | bytes 1048608 | tf_op jit(solution)/shard_map/ppermute | solution.py:35
  119.3 2.8 %collective-permute-done.14.refs_3_ = f32[8,256,128]{2,1,0:T(8,128)S(1)} collective-permute-done((f32[8,256,128]{2,1,0:T(8,128)}, f32[8,256,128]{2,1,0:T(8,128)S(1)}, u32[]{:S(2)}, u32[]{:S(2)}) %collective-permute-start.14) | collective-permute-done | bytes 1048608 | tf_op jit(solution)/shard_map/ppermute | solution.py:35
  125.7 2.2 collective-permute-start.15
  128.9 8.8 %collective-permute-done.15.refs_0_ = f32[6,256,128]{2,1,0:T(8,128)S(1)} collective-permute-done((f32[6,256,128]{2,1,0:T(8,128)S(1)}, f32[6,256,128]{2,1,0:T(8,128)S(1)}, u32[]{:S(2)}, u32[]{:S(2)}) %collective-permute-start.15) | collective-permute-done | bytes 786464 | tf_op jit(solution)/shard_map/ppermute | solution.py:35
  137.7 2.6 %collective-permute-done.16.refs_1_ = f32[8,256,128]{2,1,0:T(8,128)S(1)} collective-permute-done((f32[8,256,128]{2,1,0:T(8,128)S(1)}, f32[8,256,128]{2,1,0:T(8,128)S(1)}, u32[]{:S(2)}, u32[]{:S(2)}) %collective-permute-start.16) | collective-permute-done | bytes 1048608 | tf_op jit(solution)/shard_map/ppermute | solution.py:35
  145.4 1.9 collective-permute-done.20.refs_8_
  147.3 11.8 %rows.1 = (f32[4,256,512]{2,1,0:T(8,128)}, f32[4,4,256,128]{3,2,1,0:T(8,128)}, bf16[4,256,1024]{2,1,0:T(8,128)(2,1)}, bf16[4,256,1024]{2,1,0:T(8,128)(2,1)}, bf1...) custom-call(s32[5]{0:T(128)} %stack.23.spot, s32[2,32,32]{2,1,0:T(8,128)} %child_mask.3, f32[512,512]{1,0:T(8,128)} %inv.1, ...), custom_call_target="tpu_custom_call" | custom-call | flops 4000000000 | bytes 18000000 | tf_op jit(solution)/shard_map/rows/pallas_call | solution.py:169
  161.2 8.2 %collective-permute-start.22 = (f32[2,256,128]{2,1,0:T(8,128)S(1)}, f32[2,256,128]{2,1,0:T(8,128)S(1)}, u32[]{:S(2)}, u32[]{:S(2)}) collective-permute-start(f32[2,256,128]{2,1,0:T(8,128)S(1)} %get-tuple-element.78), channel_id=1, source_target_pairs={{0,8},{1,24},{2,40},{3,56},{8,57},{9,9},{10,25},{11,41},{16,58},{1... | collective-permute-start | bytes 786440 | tf_op jit(solution)/shard_map/ppermute | solution.py:35
  171.1 6.5 %collective-permute-done.23.refs_0_ = f32[2,256,128]{2,1,0:T(8,128)S(1)} collective-permute-done((f32[2,256,128]{2,1,0:T(8,128)S(1)}, f32[2,256,128]{2,1,0:T(8,128)S(1)}, u32[]{:S(2)}, u32[]{:S(2)}) %collective-permute-start.23) | collective-permute-done | bytes 262176 | tf_op jit(solution)/shard_map/ppermute | solution.py:35
  178.4 10.2 %collective-permute-start.25 = (f32[4,256,128]{2,1,0:T(8,128)}, f32[4,256,128]{2,1,0:T(8,128)S(1)}, u32[]{:S(2)}, u32[]{:S(2)}) collective-permute-start(f32[4,256,128]{2,1,0:T(8,128)} %pad_maximum_fusion.6.refs_0_), channel_id=1, source_target_pairs={{0,48},{1,49},{2,50},{3,51},{4,52},{5,53},{6,54},{7,55},{8,56},{9,... | collective-permute-start | bytes 1572872 | tf_op jit(solution)/shard_map/ppermute | solution.py:35
  188.7 2.1 collective-permute-start.27
  190.8 1.6 copy-done.14
  192.4 21.7 %update.1.refs_0_ = f32[16384,128]{1,0:T(8,128)} custom-call(s32[5]{0:T(128)S(1)} %copy-done.16, s32[2,32,32]{2,1,0:T(8,128)S(1)} %copy-done.15, f32[16384,128]{1,0:T(8,128)} %bitcast.35, bf16[4,256,1024]{2,1,0:T(8,128)(2,1)S(1)} %copy-done.13, bf16[4,256,1024]{2,1,0:T(8,128)(2,1)S(1)} %copy-done.14, f32[8,256,128]{2,1,0:T(8,128)} %pad_maximum_fusion.1.refs_0_, ...), custom_call_target="tpu_custom_call" | custom-call | flops 6400000000 | bytes 28000000 | tf_op jit(solution)/shard_map/update/pallas_call | solution.py:251
  214.2 3.5 %copy-done.2 = f32[16384,128]{1,0:T(8,128)S(1)} copy-done((f32[16384,128]{1,0:T(8,128)S(1)}, f32[16384,128]{1,0:T(8,128)}, u32[]{:S(2)}) %copy-start.2) | copy-done | bytes 8388632
  218.2 2.1 collective-permute-done.29.refs_5_
  221.3 21.2 %trail.1 = f32[1024,16,128]{2,1,0:T(8,128)} custom-call(s32[5]{0:T(128)S(1)} %copy-done.16, s32[64,64]{1,0:T(8,128)S(1)} %copy-done.17, f32[1024,16,128]{2,1,0:T(8,128)} %bitcast.33, bf16[4,256,512]{2,1,0:T(8,128)(2,1)S(1)} %copy-done.18, bf16[4,256,512]{2,1,0:T(8,128)(2,1)S(1)} %copy-done.19, f32[4,256,128]{2,1,0:T(8,128)} %pad_maximum_fusion.6.refs_0_, ...), custom_call_target="tpu_custom_call" | custom-call | flops 6400000000 | bytes 22000000 | tf_op jit(solution)/shard_map/trail/pallas_call | solution.py:314
  (159 shorter events, 31.1 us)
Async XLA Ops:
  9.8 19.8 %collective-permute-start.3 = (f32[2,2,256,128]{3,2,1,0:T(8,128)}, f32[2,2,256,128]{3,2,1,0:T(8,128)S(1)}, u32[]{:S(2)}, u32[]{:S(2)}) collective-permute-start(f32[2,2,256,128]{3,2,1,0:T(8,128)} %slice.76), channel_id=1, source_target_pairs={{0,3},{1,2},{8,11},{9,10},{16,19},{17,18},{24,27},{25,26},{32,35},... | collective-permute-start | bytes 1572872 | tf_op jit(solution)/shard_map/ppermute | solution.py:35
  11.8 17.7 %collective-permute-start = (f32[2,256,128]{2,1,0:T(8,128)S(1)}, f32[2,256,128]{2,1,0:T(8,128)S(1)}, u32[]{:S(2)}, u32[]{:S(2)}) collective-permute-start(f32[2,256,128]{2,1,0:T(8,128)S(1)} %get-tuple-element.81), channel_id=1, source_target_pairs={{0,4},{1,5},{2,6},{3,7},{4,0},{5,1},{6,2},{7,3},{8,12},{9,13},{10,... | collective-permute-start | bytes 786440 | tf_op jit(solution)/shard_map/ppermute | solution.py:35
  14.4 15.1 %collective-permute-start.1 = (f32[2,256,128]{2,1,0:T(8,128)}, f32[2,256,128]{2,1,0:T(8,128)S(1)}, u32[]{:S(2)}, u32[]{:S(2)}) collective-permute-start(f32[2,256,128]{2,1,0:T(8,128)} %get-tuple-element.80), channel_id=1, source_target_pairs={{0,64},{1,65},{2,66},{3,67},{4,68},{5,69},{6,70},{7,71},{8,72},{9,... | collective-permute-start | bytes 786440 | tf_op jit(solution)/shard_map/ppermute | solution.py:35
  15.1 14.5 %collective-permute-start.2 = (f32[2,256,128]{2,1,0:T(8,128)}, f32[2,256,128]{2,1,0:T(8,128)S(1)}, u32[]{:S(2)}, u32[]{:S(2)}) collective-permute-start(f32[2,256,128]{2,1,0:T(8,128)} %get-tuple-element.80), channel_id=1, source_target_pairs={{0,68},{1,69},{2,70},{3,71},{4,64},{5,65},{6,66},{7,67},{8,76},{9,... | collective-permute-start | bytes 786440 | tf_op jit(solution)/shard_map/ppermute | solution.py:35
  33.5 30.8 %collective-permute-start.4 = (f32[8,256,128]{2,1,0:T(8,128)}, f32[8,256,128]{2,1,0:T(8,128)}, u32[]{:S(2)}, u32[]{:S(2)}) collective-permute-start(f32[8,256,128]{2,1,0:T(8,128)} %pad_maximum_fusion.refs_0_), channel_id=1, source_target_pairs={{0,1},{1,2},{2,3},{3,0},{4,5},{5,6},{6,7},{7,4},{8,11},{9,8},{10,9... | collective-permute-start | bytes 3145736 | tf_op jit(solution)/shard_map/ppermute | solution.py:35
  35.2 29.0 %collective-permute-start.5 = (f32[2,2,256,128]{3,2,1,0:T(8,128)S(1)}, f32[2,2,256,128]{3,2,1,0:T(8,128)S(1)}, u32[]{:S(2)}, u32[]{:S(2)}) collective-permute-start(f32[2,2,256,128]{3,2,1,0:T(8,128)S(1)} %slice_select_fusion), channel_id=1, source_target_pairs={{0,4},{1,5},{2,6},{3,7},{8,12},{9,13},{10,14},{11,15},{16,20},{17,... | collective-permute-start | bytes 1572872 | tf_op jit(solution)/shard_map/ppermute | solution.py:35
  39.6 24.6 %collective-permute-start.6 = (f32[4,256,128]{2,1,0:T(8,128)S(1)}, f32[4,256,128]{2,1,0:T(8,128)S(1)}, u32[]{:S(2)}, u32[]{:S(2)}) collective-permute-start(f32[4,256,128]{2,1,0:T(8,128)S(1)} %pad_maximum_fusion.4), channel_id=1, source_target_pairs={{0,0},{1,16},{2,32},{3,48},{8,49},{9,1},{10,17},{11,33},{16,50},{1... | collective-permute-start | bytes 1572872 | tf_op jit(solution)/shard_map/ppermute | solution.py:35
  41.2 23.1 %collective-permute-start.7 = (f32[4,256,128]{2,1,0:T(8,128)}, f32[4,256,128]{2,1,0:T(8,128)S(1)}, u32[]{:S(2)}, u32[]{:S(2)}) collective-permute-start(f32[4,256,128]{2,1,0:T(8,128)} %pad_maximum_fusion.5), channel_id=1, source_target_pairs={{0,8},{1,24},{2,40},{3,56},{8,57},{9,9},{10,25},{11,41},{16,58},{1... | collective-permute-start | bytes 1572872 | tf_op jit(solution)/shard_map/ppermute | solution.py:35
  65.4 24.3 %collective-permute-start.8 = (f32[8,256,128]{2,1,0:T(8,128)}, f32[8,256,128]{2,1,0:T(8,128)}, u32[]{:S(2)}, u32[]{:S(2)}) collective-permute-start(f32[8,256,128]{2,1,0:T(8,128)} %get-tuple-element.43.refs_1_), channel_id=1, source_target_pairs={{0,1},{1,2},{2,3},{3,0},{4,5},{5,6},{6,7},{7,4},{8,11},{9,8},{10,9... | collective-permute-start | bytes 3145736 | tf_op jit(solution)/shard_map/ppermute | solution.py:35
  68.9 20.8 %collective-permute-start.9 = (f32[6,256,128]{2,1,0:T(8,128)S(1)}, f32[6,256,128]{2,1,0:T(8,128)S(1)}, u32[]{:S(2)}, u32[]{:S(2)}) collective-permute-start(f32[6,256,128]{2,1,0:T(8,128)S(1)} %pad_maximum_fusion.3.refs_4_), channel_id=1, source_target_pairs={{0,1},{1,2},{2,3},{3,0},{4,5},{5,6},{6,7},{7,4},{8,11},{9,8},{10,9... | collective-permute-start | bytes 2359304 | tf_op jit(solution)/shard_map/ppermute | solution.py:35
  69.0 13.0 %collective-permute-start.10 = (f32[4,256,128]{2,1,0:T(8,128)S(1)}, f32[4,256,128]{2,1,0:T(8,128)S(1)}, u32[]{:S(2)}, u32[]{:S(2)}) collective-permute-start(f32[4,256,128]{2,1,0:T(8,128)S(1)} %broadcast_select_fusion.1), channel_id=1, source_target_pairs={{0,64},{1,65},{2,66},{3,67},{4,68},{5,69},{6,70},{7,71},{8,72},{9,... | collective-permute-start | bytes 1572872 | tf_op jit(solution)/shard_map/ppermute | solution.py:35
  90.6 23.4 %collective-permute-start.11 = (f32[8,256,128]{2,1,0:T(8,128)}, f32[8,256,128]{2,1,0:T(8,128)S(1)}, u32[]{:S(2)}, u32[]{:S(2)}) collective-permute-start(f32[8,256,128]{2,1,0:T(8,128)} %get-tuple-element.47.refs_2_), channel_id=1, source_target_pairs={{0,1},{1,2},{2,3},{3,0},{4,5},{5,6},{6,7},{7,4},{8,11},{9,8},{10,9... | collective-permute-start | bytes 3145736 | tf_op jit(solution)/shard_map/ppermute | solution.py:35
  95.2 24.1 %collective-permute-start.13 = (f32[8,256,128]{2,1,0:T(8,128)}, f32[8,256,128]{2,1,0:T(8,128)S(1)}, u32[]{:S(2)}, u32[]{:S(2)}) collective-permute-start(f32[8,256,128]{2,1,0:T(8,128)} %pad_maximum_fusion.1.refs_0_), channel_id=1, source_target_pairs={{0,48},{1,49},{2,50},{3,51},{4,52},{5,53},{6,54},{7,55},{8,56},{9,... | collective-permute-start | bytes 3145736 | tf_op jit(solution)/shard_map/ppermute | solution.py:35
  95.2 26.9 %collective-permute-start.14 = (f32[8,256,128]{2,1,0:T(8,128)}, f32[8,256,128]{2,1,0:T(8,128)S(1)}, u32[]{:S(2)}, u32[]{:S(2)}) collective-permute-start(f32[8,256,128]{2,1,0:T(8,128)} %pad_maximum_fusion.1.refs_0_), channel_id=1, source_target_pairs={{0,16},{1,17},{2,18},{3,19},{4,20},{5,21},{6,22},{7,23},{8,24},{9,... | collective-permute-start | bytes 3145736 | tf_op jit(solution)/shard_map/ppermute | solution.py:35
  97.2 16.8 %collective-permute-start.12 = (f32[6,256,128]{2,1,0:T(8,128)S(1)}, f32[6,256,128]{2,1,0:T(8,128)S(1)}, u32[]{:S(2)}, u32[]{:S(2)}) collective-permute-start(f32[6,256,128]{2,1,0:T(8,128)S(1)} %copy-done.36), channel_id=1, source_target_pairs={{0,1},{1,2},{2,3},{3,0},{4,5},{5,6},{6,7},{7,4},{8,11},{9,8},{10,9... | collective-permute-start | bytes 2359304 | tf_op jit(solution)/shard_map/ppermute | solution.py:35
  98.4 30.5 %collective-permute-start.17 = (f32[8,256,128]{2,1,0:T(8,128)}, f32[8,256,128]{2,1,0:T(8,128)S(1)}, u32[]{:S(2)}, u32[]{:S(2)}) collective-permute-start(f32[8,256,128]{2,1,0:T(8,128)} %pad_maximum_fusion.1.refs_0_), channel_id=1, source_target_pairs={{0,8},{1,9},{2,10},{3,11},{4,12},{5,13},{6,14},{7,15},{8,0},{9,1},... | collective-permute-start | bytes 3145736 | tf_op jit(solution)/shard_map/ppermute | solution.py:35
  124.5 15.8 %collective-permute-start.16 = (f32[8,256,128]{2,1,0:T(8,128)S(1)}, f32[8,256,128]{2,1,0:T(8,128)S(1)}, u32[]{:S(2)}, u32[]{:S(2)}) collective-permute-start(f32[8,256,128]{2,1,0:T(8,128)S(1)} %broadcast_select_fusion), channel_id=1, source_target_pairs={{0,16},{1,17},{2,18},{3,19},{4,20},{5,21},{6,22},{7,23},{8,56},{9,... | collective-permute-start | bytes 3145736 | tf_op jit(solution)/shard_map/ppermute | solution.py:35
  125.2 15.1 %collective-permute-start.18 = (f32[8,256,128]{2,1,0:T(8,128)S(1)}, f32[8,256,128]{2,1,0:T(8,128)S(1)}, u32[]{:S(2)}, u32[]{:S(2)}) collective-permute-start(f32[8,256,128]{2,1,0:T(8,128)S(1)} %copy-done.4), channel_id=1, source_target_pairs={{0,8},{1,9},{2,10},{3,11},{4,12},{5,13},{6,14},{7,15},{8,0},{9,1},... | collective-permute-start | bytes 3145736 | tf_op jit(solution)/shard_map/ppermute | solution.py:35
  125.2 17.0 %collective-permute-start.19 = (f32[8,256,128]{2,1,0:T(8,128)S(1)}, f32[8,256,128]{2,1,0:T(8,128)}, u32[]{:S(2)}, u32[]{:S(2)}) collective-permute-start(f32[8,256,128]{2,1,0:T(8,128)S(1)} %copy-done.6), channel_id=1, source_target_pairs={{0,8},{1,9},{2,10},{3,11},{4,12},{5,13},{6,14},{7,15},{8,0},{9,1},... | collective-permute-start | bytes 3145736 | tf_op jit(solution)/shard_map/ppermute | solution.py:35
  125.7 12.0 %collective-permute-start.15 = (f32[6,256,128]{2,1,0:T(8,128)S(1)}, f32[6,256,128]{2,1,0:T(8,128)S(1)}, u32[]{:S(2)}, u32[]{:S(2)}) collective-permute-start(f32[6,256,128]{2,1,0:T(8,128)S(1)} %copy-done.38), channel_id=1, source_target_pairs={{0,1},{1,2},{2,3},{3,0},{4,5},{5,6},{6,7},{7,4},{8,11},{9,8},{10,9... | collective-permute-start | bytes 2359304 | tf_op jit(solution)/shard_map/ppermute | solution.py:35
  144.3 3.0 %collective-permute-start.20 = (f32[8,256,128]{2,1,0:T(8,128)}, f32[8,256,128]{2,1,0:T(8,128)}, u32[]{:S(2)}, u32[]{:S(2)}) collective-permute-start(f32[8,256,128]{2,1,0:T(8,128)} %pad_maximum_fusion.2), channel_id=1, source_target_pairs={{0,8},{1,9},{2,10},{3,11},{4,12},{5,13},{6,14},{7,15},{8,0},{9,1},... | collective-permute-start | bytes 3145736 | tf_op jit(solution)/shard_map/ppermute | solution.py:35
  144.9 26.2 %collective-permute-start.24 = (f32[8,256,128]{2,1,0:T(8,128)S(1)}, f32[8,256,128]{2,1,0:T(8,128)}, u32[]{:S(2)}, u32[]{:S(2)}) collective-permute-start(f32[8,256,128]{2,1,0:T(8,128)S(1)} %copy-done.10), channel_id=1, source_target_pairs={{0,8},{1,9},{2,10},{3,11},{4,12},{5,13},{6,14},{7,15},{8,0},{9,1},... | collective-permute-start | bytes 3145736 | tf_op jit(solution)/shard_map/ppermute | solution.py:35
  160.4 9.0 %collective-permute-start.21 = (f32[2,256,128]{2,1,0:T(8,128)S(1)}, f32[2,256,128]{2,1,0:T(8,128)S(1)}, u32[]{:S(2)}, u32[]{:S(2)}) collective-permute-start(f32[2,256,128]{2,1,0:T(8,128)S(1)} %get-tuple-element.79), channel_id=1, source_target_pairs={{0,0},{1,16},{2,32},{3,48},{8,49},{9,1},{10,17},{11,33},{16,50},{1... | collective-permute-start | bytes 786440 | tf_op jit(solution)/shard_map/ppermute | solution.py:35
  161.2 9.3 %collective-permute-start.22 = (f32[2,256,128]{2,1,0:T(8,128)S(1)}, f32[2,256,128]{2,1,0:T(8,128)S(1)}, u32[]{:S(2)}, u32[]{:S(2)}) collective-permute-start(f32[2,256,128]{2,1,0:T(8,128)S(1)} %get-tuple-element.78), channel_id=1, source_target_pairs={{0,8},{1,24},{2,40},{3,56},{8,57},{9,9},{10,25},{11,41},{16,58},{1... | collective-permute-start | bytes 786440 | tf_op jit(solution)/shard_map/ppermute | solution.py:35
  170.5 7.1 %collective-permute-start.23 = (f32[2,256,128]{2,1,0:T(8,128)S(1)}, f32[2,256,128]{2,1,0:T(8,128)S(1)}, u32[]{:S(2)}, u32[]{:S(2)}) collective-permute-start(f32[2,256,128]{2,1,0:T(8,128)S(1)} %broadcast_select_fusion.3), channel_id=1, source_target_pairs={{0,64},{1,65},{2,66},{3,67},{4,68},{5,69},{6,70},{7,71},{8,72},{9,... | collective-permute-start | bytes 786440 | tf_op jit(solution)/shard_map/ppermute | solution.py:35
  178.4 35.7 %collective-permute-start.25 = (f32[4,256,128]{2,1,0:T(8,128)}, f32[4,256,128]{2,1,0:T(8,128)S(1)}, u32[]{:S(2)}, u32[]{:S(2)}) collective-permute-start(f32[4,256,128]{2,1,0:T(8,128)} %pad_maximum_fusion.6.refs_0_), channel_id=1, source_target_pairs={{0,48},{1,49},{2,50},{3,51},{4,52},{5,53},{6,54},{7,55},{8,56},{9,... | collective-permute-start | bytes 1572872 | tf_op jit(solution)/shard_map/ppermute | solution.py:35
  188.7 25.5 %collective-permute-start.26 = (f32[4,256,128]{2,1,0:T(8,128)}, f32[4,256,128]{2,1,0:T(8,128)}, u32[]{:S(2)}, u32[]{:S(2)}) collective-permute-start(f32[4,256,128]{2,1,0:T(8,128)} %pad_maximum_fusion.6.refs_0_), channel_id=1, source_target_pairs={{0,16},{1,17},{2,18},{3,19},{4,20},{5,21},{6,22},{7,23},{8,24},{9,... | collective-permute-start | bytes 1572872 | tf_op jit(solution)/shard_map/ppermute | solution.py:35
  188.7 25.5 %collective-permute-start.27 = (f32[4,256,128]{2,1,0:T(8,128)}, f32[4,256,128]{2,1,0:T(8,128)}, u32[]{:S(2)}, u32[]{:S(2)}) collective-permute-start(f32[4,256,128]{2,1,0:T(8,128)} %pad_maximum_fusion.6.refs_0_), channel_id=1, source_target_pairs={{0,32},{1,33},{2,34},{3,35},{4,36},{5,37},{6,38},{7,39},{8,40},{9,... | collective-permute-start | bytes 1572872 | tf_op jit(solution)/shard_map/ppermute | solution.py:35
  190.7 27.5 %collective-permute-start.28 = (f32[4,256,128]{2,1,0:T(8,128)}, f32[4,256,128]{2,1,0:T(8,128)}, u32[]{:S(2)}, u32[]{:S(2)}) collective-permute-start(f32[4,256,128]{2,1,0:T(8,128)} %pad_maximum_fusion.6.refs_0_), channel_id=1, source_target_pairs={{0,8},{1,9},{2,10},{3,11},{4,12},{5,13},{6,14},{7,15},{8,0},{9,1},... | collective-permute-start | bytes 1572872 | tf_op jit(solution)/shard_map/ppermute | solution.py:35
  217.7 2.6 %collective-permute-start.29 = (f32[4,256,128]{2,1,0:T(8,128)S(1)}, f32[4,256,128]{2,1,0:T(8,128)S(1)}, u32[]{:S(2)}, u32[]{:S(2)}) collective-permute-start(f32[4,256,128]{2,1,0:T(8,128)S(1)} %get-tuple-element.68.refs_1_), channel_id=1, source_target_pairs={{0,8},{1,9},{2,10},{3,11},{4,12},{5,13},{6,14},{7,15},{8,0},{9,1},... | collective-permute-start | bytes 1572872 | tf_op jit(solution)/shard_map/ppermute | solution.py:35
  217.7 2.9 %collective-permute-start.30 = (f32[4,256,128]{2,1,0:T(8,128)}, f32[4,256,128]{2,1,0:T(8,128)S(1)}, u32[]{:S(2)}, u32[]{:S(2)}) collective-permute-start(f32[4,256,128]{2,1,0:T(8,128)} %get-tuple-element.69.refs_2_), channel_id=1, source_target_pairs={{0,8},{1,9},{2,10},{3,11},{4,12},{5,13},{6,14},{7,15},{8,0},{9,1},... | collective-permute-start | bytes 1572872 | tf_op jit(solution)/shard_map/ppermute | solution.py:35
  218.2 3.1 %collective-permute-start.31 = (f32[4,256,128]{2,1,0:T(8,128)}, f32[4,256,128]{2,1,0:T(8,128)S(1)}, u32[]{:S(2)}, u32[]{:S(2)}) collective-permute-start(f32[4,256,128]{2,1,0:T(8,128)} %get-tuple-element.70.refs_3_), channel_id=1, source_target_pairs={{0,8},{1,9},{2,10},{3,11},{4,12},{5,13},{6,14},{7,15},{8,0},{9,1},... | collective-permute-start | bytes 1572872 | tf_op jit(solution)/shard_map/ppermute | solution.py:35
  (42 other events, 327.5 us)

commit v5 on v4

--- a/solution.py
+++ b/solution.py
@@ -195,27 +195,41 @@
     )(spot, child_mask, inv, *gathered, *leads, edge_twin)
 
 
-def update_kernel(spot, child_mask, parent, rh, rl, *refs):
-    arrays, (out, ch, cl, acc) = refs[:8], refs[8:]
+def split_kernel(spot, *refs):
+    arrays, (ch, cl) = refs[:8], refs[8:]
+    p, x, core, yhi, z = (spot[n] for n in range(5))
+    for n in range(8):
+        lane = core if n < 4 else 1 - core
+        z_from = lax.rem(z + x + (0, 1, 3, 2)[n % 4] - (2 * yhi + z // 2) + 4, 4)
+        for part in range(2):
+            plane = p if part == 0 else 1 - p
+            child = lax.rem(plane + lane, 2)
+            for yr in range(2):
+                start = pl.multiple_of(z_from * 256 + lax.rem(yhi + yr, 2) * 128, 128)
+                for i in range(2):
+                    a, b = halves(arrays[n][part * 4 + yr * 2 + i])
+                    ch[child * 4 + plane + 2 * i, :, pl.ds(start, 128)] = a
+                    cl[child * 4 + plane + 2 * i, :, pl.ds(start, 128)] = b
+
+
+def split_step(spot, arrays):
+    vmem = pl.BlockSpec(memory_space=pltpu.VMEM)
+    return pl.pallas_call(
+        split_kernel,
+        out_shape=[jax.ShapeDtypeStruct((8, BS, 1024), jnp.bfloat16)] * 2,
+        in_specs=[pl.BlockSpec(memory_space=pltpu.SMEM)] + [vmem] * 8,
+        out_specs=[vmem] * 2,
+        compiler_params=pltpu.CompilerParams(vmem_limit_bytes=40 * 1024 * 1024),
+        cost_estimate=pl.CostEstimate(flops=0, bytes_accessed=16_000_000, transcendentals=0),
+        name="split",
+    )(spot, *arrays)
+
+
+def update_kernel(spot, child_mask, parent, rh, rl, ch, cl, out, acc):
     p, x, core, yhi, z = (spot[n] for n in range(5))
     q = 2 * x + core
     c = 4 * yhi + z
     slot = pl.program_id(0)
-
-    @pl.when(slot == 0)
-    def _():
-        for n in range(8):
-            lane = core if n < 4 else 1 - core
-            z_from = lax.rem(z + x + (0, 1, 3, 2)[n % 4] - (2 * yhi + z // 2) + 4, 4)
-            for part in range(2):
-                plane = p if part == 0 else 1 - p
-                child = lax.rem(plane + lane, 2)
-                for yr in range(2):
-                    start = pl.multiple_of(z_from * 256 + lax.rem(yhi + yr, 2) * 128, 128)
-                    for i in range(2):
-                        a, b = halves(arrays[n][part * 4 + yr * 2 + i])
-                        ch[child * 4 + plane + 2 * i, :, pl.ds(start, 128)] = a
-                        cl[child * 4 + plane + 2 * i, :, pl.ds(start, 128)] = b
 
     for j in range(8):
         touched = j < 6
@@ -255,8 +269,6 @@
         in_specs=[smem, smem, block] + [vmem] * (2 + len(arrays)),
         out_specs=block,
         scratch_shapes=[
-            pltpu.VMEM((8, BS, 1024), jnp.bfloat16),
-            pltpu.VMEM((8, BS, 1024), jnp.bfloat16),
             pltpu.VMEM((BS, BS), jnp.float32),
         ],
         compiler_params=pltpu.CompilerParams(vmem_limit_bytes=40 * 1024 * 1024),
@@ -418,19 +430,21 @@
     columns.append(relayed)
 
     edge_own = jnp.concatenate([block[4:] for block in leads])
-    edge_twin = send(edge_own, twin)
+    edge_twin, last = gate([send(edge_own, twin), send(columns[3], twin)], [])
+    arrays.append(last)
     panel, to_send, rh, rl, ph, pll = rows_step(
         spot, child_listed, inv_diag, gathered, leads, edge_twin
     )
     turn = (z - (2 * (x % 2) + core)) % 4
     mine = lax.dynamic_index_in_dim(to_send, turn, 0, keepdims=False)
-    pieces = gate(scatter([mine[:2], mine[2:]]), [], pl.ANY, 1)
+    pieces = scatter([mine[:2], mine[2:]])
+    split = list(split_step(spot, columns + arrays))
+    pieces = gate(pieces, split, pl.ANY, 1)
     quarter = jnp.where(first, pieces[0], pieces[1])
-    arrays.append(send(columns[3], twin))
-    other_quarter, arrays[3] = gate([send(quarter, swap), arrays[3]], [], pl.ANY, 1)
+    (other_quarter,) = gate([send(quarter, swap)], [], pl.ANY, 1)
     panels = [jnp.concatenate([quarter, other_quarter])]
     panels += [send(panels[0], pairs) for pairs in around]
-    assembled = update_step(spot, child_listed, flat, rh, rl, columns + arrays)
+    assembled = update_step(spot, child_listed, flat, rh, rl, split)
     twins = [send(panels[0], twin)]
     (assembled,) = gate([assembled], [])
     panels[1:] = gate(panels[1:], [assembled], pl.ANY, 1)

time: 244 us -> 254 us (1.041)
  the two profiles are of different devices: /device:TPU:66 before, /device:TPU:58 now
where the time goes in v5:
time: 254 us; the launch traced here: 252 us
  waiting for transfers between devices  74.9 us (29%)
  Pallas kernels  57.8 us (23%)
  blocking collectives  45.2 us (18%)
  local copies, waits for them, and re-layouts  33.2 us (13%)
  starting transfers between devices  27.2 us (11%)
  other arithmetic  12.7 us (5%)
    ppermute x32, waiting for transfers between devices, send(): return lax.ppermute(value, AXES, pairs)  74.9 us
    all_gather x2, blocking collectives, shards(): edges = lax.all_gather(lax.all_gather(mine[0], 'x')[0], ('ylo', 'yhi'))[:2]  45.2 us
    ppermute x32, starting transfers between devices, send(): return lax.ppermute(value, AXES, pairs)  27.2 us
    unnamed x81, local copies, waits for them, and re-layouts  22.6 us
    pallas_call x1, Pallas kernels, trail_step(): pl.pallas_call(trail_kernel, grid=(2, 4), out_shape=jax.ShapeDtypeStruct(...  19 us
    pallas_call x1, Pallas kernels, update_step(): pl.pallas_call(update_kernel, grid=(4,), out_shape=jax.ShapeDtypeStruct(f...  18.6 us
    pallas_call x1, Pallas kernels, rows_step(): pl.pallas_call(rows_kernel, out_shape=(jax.ShapeDtypeStruct((4, BS, 512),...  11.8 us
    pallas_call x1, Pallas kernels, split_step(): pl.pallas_call(split_kernel, out_shape=[jax.ShapeDtypeStruct((8, BS, 1024...  6.01 us
  transfers between devices with their start and end apart: 32, of which 12 were waited for; matrix products, arithmetic and copies ran while one was open for 4% of the time, Pallas kernels for 10%

profile of v5, /device:TPU:58, one launch (start us, length us, event | category | flops | bytes accessed | tf_op | source)
XLA Modules:
  0.0 252.2 jit_solution(16756217636601193451)
XLA Ops:
  2.1 2.4 place.1
  5.7 2.5 slice.75
  11.2 3.4 %collective-permute-start.2 = (f32[2,256,128]{2,1,0:T(8,128)}, f32[2,256,128]{2,1,0:T(8,128)S(1)}, u32[]{:S(2)}, u32[]{:S(2)}) collective-permute-start(f32[2,256,128]{2,1,0:T(8,128)} %get-tuple-element.84), channel_id=1, source_target_pairs={{0,68},{1,69},{2,70},{3,71},{4,64},{5,65},{6,66},{7,67},{8,76},{9,... | collective-permute-start | bytes 786440 | tf_op jit(solution)/shard_map/ppermute | solution.py:35
  16.1 13.5 %all-gather = f32[4,1,256,128]{3,2,1,0:T(8,128)S(1)} all-gather(f32[1,1,256,128]{3,2,1,0:T(8,128)S(1)} %slice.62), channel_id=2, replica_groups=mesh['ylo'=2,'x'=4,'core'=2,'yhi'=2,'z'=4] {'x'}, dimensions={0}, use_global_device_ids=true | all-gather | bytes 655360 | tf_op jit(solution)/shard_map/all_gather | solution.py:373
  32.5 2.2 pad_maximum_fusion.refs_0_
  35.4 1.8 collective-permute-start.4
  37.2 1.8 pad_maximum_fusion.4
  41.6 31.7 %all-gather.1 = f32[4,1,256,128]{3,2,1,0:T(8,128)S(1)} all-gather(f32[1,1,256,128]{3,2,1,0:T(8,128)S(1)} %slice.78), channel_id=3, replica_groups=mesh['ylo'=2,'x'=4,'core'=2,'yhi'=2,'z'=4] {'ylo','yhi'}, dimensions={0}, use_global_device_ids=true | all-gather | bytes 655360 | tf_op jit(solution)/shard_map/all_gather | solution.py:373
  75.7 1.4 collective-permute-start.9
  78.8 12.0 %collective-permute-done.10.refs_2_ = f32[4,256,128]{2,1,0:T(8,128)S(1)} collective-permute-done((f32[4,256,128]{2,1,0:T(8,128)S(1)}, f32[4,256,128]{2,1,0:T(8,128)S(1)}, u32[]{:S(2)}, u32[]{:S(2)}) %collective-permute-start.10) | collective-permute-done | bytes 524320 | tf_op jit(solution)/shard_map/ppermute | solution.py:35
  90.7 7.2 %collective-permute-done.9.refs_1_ = f32[6,256,128]{2,1,0:T(8,128)S(1)} collective-permute-done((f32[6,256,128]{2,1,0:T(8,128)S(1)}, f32[6,256,128]{2,1,0:T(8,128)S(1)}, u32[]{:S(2)}, u32[]{:S(2)}) %collective-permute-start.9) | collective-permute-done | bytes 786464 | tf_op jit(solution)/shard_map/ppermute | solution.py:35
  99.8 2.1 pad_maximum_fusion.1.refs_0_
  102.2 1.7 collective-permute-start.13
  105.3 22.4 %collective-permute-done.12.refs_1_ = f32[6,256,128]{2,1,0:T(8,128)S(1)} collective-permute-done((f32[6,256,128]{2,1,0:T(8,128)}, f32[6,256,128]{2,1,0:T(8,128)S(1)}, u32[]{:S(2)}, u32[]{:S(2)}) %collective-permute-start.12) | collective-permute-done | bytes 786464 | tf_op jit(solution)/shard_map/ppermute | solution.py:35
  129.5 1.3 broadcast_select_fusion
  130.9 1.5 collective-permute-start.16
  134.3 1.7 slice.67
  136.0 10.3 %collective-permute-done.15.refs_0_ = f32[6,256,128]{2,1,0:T(8,128)S(1)} collective-permute-done((f32[6,256,128]{2,1,0:T(8,128)}, f32[6,256,128]{2,1,0:T(8,128)S(1)}, u32[]{:S(2)}, u32[]{:S(2)}) %collective-permute-start.15) | collective-permute-done | bytes 786464 | tf_op jit(solution)/shard_map/ppermute | solution.py:35
  151.5 1.5 collective-permute-done.20.refs_0_
  153.0 1.7 collective-permute-done.21.refs_1_
  155.7 11.8 %rows.1 = (f32[4,256,512]{2,1,0:T(8,128)}, f32[4,4,256,128]{3,2,1,0:T(8,128)}, bf16[4,256,1024]{2,1,0:T(8,128)(2,1)}, bf16[4,256,1024]{2,1,0:T(8,128)(2,1)}, bf1...) custom-call(s32[5]{0:T(128)} %stack.23.spot, s32[2,32,32]{2,1,0:T(8,128)} %child_mask.3, f32[512,512]{1,0:T(8,128)} %inv.1, ...), custom_call_target="tpu_custom_call" | custom-call | flops 4000000000 | bytes 18000000 | tf_op jit(solution)/shard_map/rows/pallas_call | solution.py:169
  174.3 6.0 %split.1 = (bf16[8,256,1024]{2,1,0:T(8,128)(2,1)S(1)}, bf16[8,256,1024]{2,1,0:T(8,128)(2,1)}) custom-call(s32[5]{0:T(128)S(1)} %copy-done.20, f32[8,256,128]{2,1,0:T(8,128)} %pad_maximum_fusion.1.refs_0_, f32[8,256,128]{2,1,0:T(8,128)S(1)} %copy-done.8, f32[8,256,128]{2,1,0:T(8,128)S(1)} %copy-done.6, f32[8,256,128]{2,1,0:T(8,128)S(1)} %copy-done.12, ...), custom_call_target="tpu_custom_call" | custom-call | bytes 16000000 | tf_op jit(solution)/shard_map/split/pallas_call | solution.py:217
  180.3 7.1 %collective-permute-done.22.refs_0_ = f32[2,256,128]{2,1,0:T(8,128)S(1)} collective-permute-done((f32[2,256,128]{2,1,0:T(8,128)S(1)}, f32[2,256,128]{2,1,0:T(8,128)S(1)}, u32[]{:S(2)}, u32[]{:S(2)}) %collective-permute-start.22) | collective-permute-done | bytes 262176 | tf_op jit(solution)/shard_map/ppermute | solution.py:35
  187.4 2.2 copy-done.3
  190.2 5.9 %collective-permute-done.24.refs_0_ = f32[2,256,128]{2,1,0:T(8,128)S(1)} collective-permute-done((f32[2,256,128]{2,1,0:T(8,128)S(1)}, f32[2,256,128]{2,1,0:T(8,128)S(1)}, u32[]{:S(2)}, u32[]{:S(2)}) %collective-permute-start.24) | collective-permute-done | bytes 262176 | tf_op jit(solution)/shard_map/ppermute | solution.py:35
  196.1 3.2 %collective-permute-start.27 = (f32[4,256,128]{2,1,0:T(8,128)S(1)}, f32[4,256,128]{2,1,0:T(8,128)S(1)}, u32[]{:S(2)}, u32[]{:S(2)}) collective-permute-start(f32[4,256,128]{2,1,0:T(8,128)S(1)} %pad_maximum_fusion.6.refs_0_), channel_id=1, source_target_pairs={{0,32},{1,33},{2,34},{3,35},{4,36},{5,37},{6,38},{7,39},{8,40},{9,... | collective-permute-start | bytes 1572872 | tf_op jit(solution)/shard_map/ppermute | solution.py:35
  199.3 2.0 collective-permute-start.25
  201.4 18.6 %update.1.refs_0_ = f32[16384,128]{1,0:T(8,128)} custom-call(s32[5]{0:T(128)S(1)} %copy-done.20, s32[2,32,32]{2,1,0:T(8,128)S(1)} %copy-done.19, f32[16384,128]{1,0:T(8,128)} %bitcast.35, bf16[4,256,1024]{2,1,0:T(8,128)(2,1)S(1)} %copy-done.17, bf16[4,256,1024]{2,1,0:T(8,128)(2,1)S(1)} %copy-done.18, bf16[8,256,1024]{2,1,0:T(8,128)(2,1)S(1)} %get-tuple-element.65.ch.refs_2_, ...), custom_call_target="tpu_custom_call" | custom-call | flops 6400000000 | bytes 28000000 | tf_op jit(solution)/shard_map/update/pallas_call | solution.py:265
  219.9 3.9 %collective-permute-done.26.refs_1_ = f32[4,256,128]{2,1,0:T(8,128)S(1)} collective-permute-done((f32[4,256,128]{2,1,0:T(8,128)S(1)}, f32[4,256,128]{2,1,0:T(8,128)S(1)}, u32[]{:S(2)}, u32[]{:S(2)}) %collective-permute-start.26) | collective-permute-done | bytes 524320 | tf_op jit(solution)/shard_map/ppermute | solution.py:35
  223.9 3.4 %copy-done.2 = f32[16384,128]{1,0:T(8,128)S(1)} copy-done((f32[16384,128]{1,0:T(8,128)S(1)}, f32[16384,128]{1,0:T(8,128)}, u32[]{:S(2)}) %copy-start.2) | copy-done | bytes 8388632
  227.8 1.4 collective-permute-done.29.refs_5_
  233.1 19.0 %trail.1 = f32[1024,16,128]{2,1,0:T(8,128)} custom-call(s32[5]{0:T(128)S(1)} %copy-done.20, s32[64,64]{1,0:T(8,128)S(1)} %copy-done.21, f32[1024,16,128]{2,1,0:T(8,128)} %bitcast.33, bf16[4,256,512]{2,1,0:T(8,128)(2,1)S(1)} %copy-done.22, bf16[4,256,512]{2,1,0:T(8,128)(2,1)S(1)} %copy-done.23, f32[4,256,128]{2,1,0:T(8,128)S(1)} %pad_maximum_fusion.6.refs_0_, ...), custom_call_target="tpu_custom_call" | custom-call | flops 6400000000 | bytes 22000000 | tf_op jit(solution)/shard_map/trail/pallas_call | solution.py:326
  (157 shorter events, 42.6 us)
Async XLA Ops:
  9.8 19.9 %collective-permute-start.3 = (f32[2,2,256,128]{3,2,1,0:T(8,128)}, f32[2,2,256,128]{3,2,1,0:T(8,128)S(1)}, u32[]{:S(2)}, u32[]{:S(2)}) collective-permute-start(f32[2,2,256,128]{3,2,1,0:T(8,128)} %slice.76), channel_id=1, source_target_pairs={{0,3},{1,2},{8,11},{9,10},{16,19},{17,18},{24,27},{25,26},{32,35},... | collective-permute-start | bytes 1572872 | tf_op jit(solution)/shard_map/ppermute | solution.py:35
  11.2 18.4 %collective-permute-start.2 = (f32[2,256,128]{2,1,0:T(8,128)}, f32[2,256,128]{2,1,0:T(8,128)S(1)}, u32[]{:S(2)}, u32[]{:S(2)}) collective-permute-start(f32[2,256,128]{2,1,0:T(8,128)} %get-tuple-element.84), channel_id=1, source_target_pairs={{0,68},{1,69},{2,70},{3,71},{4,64},{5,65},{6,66},{7,67},{8,76},{9,... | collective-permute-start | bytes 786440 | tf_op jit(solution)/shard_map/ppermute | solution.py:35
  14.6 15.1 %collective-permute-start.1 = (f32[2,256,128]{2,1,0:T(8,128)}, f32[2,256,128]{2,1,0:T(8,128)S(1)}, u32[]{:S(2)}, u32[]{:S(2)}) collective-permute-start(f32[2,256,128]{2,1,0:T(8,128)} %get-tuple-element.84), channel_id=1, source_target_pairs={{0,64},{1,65},{2,66},{3,67},{4,68},{5,69},{6,70},{7,71},{8,72},{9,... | collective-permute-start | bytes 786440 | tf_op jit(solution)/shard_map/ppermute | solution.py:35
  15.6 14.1 %collective-permute-start = (f32[2,256,128]{2,1,0:T(8,128)S(1)}, f32[2,256,128]{2,1,0:T(8,128)S(1)}, u32[]{:S(2)}, u32[]{:S(2)}) collective-permute-start(f32[2,256,128]{2,1,0:T(8,128)S(1)} %get-tuple-element.85), channel_id=1, source_target_pairs={{0,4},{1,5},{2,6},{3,7},{4,0},{5,1},{6,2},{7,3},{8,12},{9,13},{10,... | collective-permute-start | bytes 786440 | tf_op jit(solution)/shard_map/ppermute | solution.py:35
  34.7 38.7 %collective-permute-start.7 = (f32[4,256,128]{2,1,0:T(8,128)S(1)}, f32[4,256,128]{2,1,0:T(8,128)S(1)}, u32[]{:S(2)}, u32[]{:S(2)}) collective-permute-start(f32[4,256,128]{2,1,0:T(8,128)S(1)} %pad_maximum_fusion.5), channel_id=1, source_target_pairs={{0,8},{1,24},{2,40},{3,56},{8,57},{9,9},{10,25},{11,41},{16,58},{1... | collective-permute-start | bytes 1572872 | tf_op jit(solution)/shard_map/ppermute | solution.py:35
  35.4 38.1 %collective-permute-start.4 = (f32[8,256,128]{2,1,0:T(8,128)}, f32[8,256,128]{2,1,0:T(8,128)}, u32[]{:S(2)}, u32[]{:S(2)}) collective-permute-start(f32[8,256,128]{2,1,0:T(8,128)} %pad_maximum_fusion.refs_0_), channel_id=1, source_target_pairs={{0,1},{1,2},{2,3},{3,0},{4,5},{5,6},{6,7},{7,4},{8,11},{9,8},{10,9... | collective-permute-start | bytes 3145736 | tf_op jit(solution)/shard_map/ppermute | solution.py:35
  39.0 34.4 %collective-permute-start.6 = (f32[4,256,128]{2,1,0:T(8,128)}, f32[4,256,128]{2,1,0:T(8,128)S(1)}, u32[]{:S(2)}, u32[]{:S(2)}) collective-permute-start(f32[4,256,128]{2,1,0:T(8,128)} %pad_maximum_fusion.4), channel_id=1, source_target_pairs={{0,0},{1,16},{2,32},{3,48},{8,49},{9,1},{10,17},{11,33},{16,50},{1... | collective-permute-start | bytes 1572872 | tf_op jit(solution)/shard_map/ppermute | solution.py:35
  40.3 33.1 %collective-permute-start.5 = (f32[2,2,256,128]{3,2,1,0:T(8,128)S(1)}, f32[2,2,256,128]{3,2,1,0:T(8,128)S(1)}, u32[]{:S(2)}, u32[]{:S(2)}) collective-permute-start(f32[2,2,256,128]{3,2,1,0:T(8,128)S(1)} %slice_select_fusion), channel_id=1, source_target_pairs={{0,4},{1,5},{2,6},{3,7},{8,12},{9,13},{10,14},{11,15},{16,20},{17,... | collective-permute-start | bytes 1572872 | tf_op jit(solution)/shard_map/ppermute | solution.py:35
  74.5 23.4 %collective-permute-start.8 = (f32[8,256,128]{2,1,0:T(8,128)}, f32[8,256,128]{2,1,0:T(8,128)S(1)}, u32[]{:S(2)}, u32[]{:S(2)}) collective-permute-start(f32[8,256,128]{2,1,0:T(8,128)} %get-tuple-element.45.refs_1_), channel_id=1, source_target_pairs={{0,1},{1,2},{2,3},{3,0},{4,5},{5,6},{6,7},{7,4},{8,11},{9,8},{10,9... | collective-permute-start | bytes 3145736 | tf_op jit(solution)/shard_map/ppermute | solution.py:35
  75.7 22.3 %collective-permute-start.9 = (f32[6,256,128]{2,1,0:T(8,128)S(1)}, f32[6,256,128]{2,1,0:T(8,128)S(1)}, u32[]{:S(2)}, u32[]{:S(2)}) collective-permute-start(f32[6,256,128]{2,1,0:T(8,128)S(1)} %pad_maximum_fusion.3.refs_4_), channel_id=1, source_target_pairs={{0,1},{1,2},{2,3},{3,0},{4,5},{5,6},{6,7},{7,4},{8,11},{9,8},{10,9... | collective-permute-start | bytes 2359304 | tf_op jit(solution)/shard_map/ppermute | solution.py:35
  78.2 12.5 %collective-permute-start.10 = (f32[4,256,128]{2,1,0:T(8,128)S(1)}, f32[4,256,128]{2,1,0:T(8,128)S(1)}, u32[]{:S(2)}, u32[]{:S(2)}) collective-permute-start(f32[4,256,128]{2,1,0:T(8,128)S(1)} %broadcast_select_fusion.1), channel_id=1, source_target_pairs={{0,64},{1,65},{2,66},{3,67},{4,68},{5,69},{6,70},{7,71},{8,72},{9,... | collective-permute-start | bytes 1572872 | tf_op jit(solution)/shard_map/ppermute | solution.py:35
  101.9 25.7 %collective-permute-start.14 = (f32[8,256,128]{2,1,0:T(8,128)}, f32[8,256,128]{2,1,0:T(8,128)S(1)}, u32[]{:S(2)}, u32[]{:S(2)}) collective-permute-start(f32[8,256,128]{2,1,0:T(8,128)} %pad_maximum_fusion.1.refs_0_), channel_id=1, source_target_pairs={{0,16},{1,17},{2,18},{3,19},{4,20},{5,21},{6,22},{7,23},{8,24},{9,... | collective-permute-start | bytes 3145736 | tf_op jit(solution)/shard_map/ppermute | solution.py:35
  102.2 25.4 %collective-permute-start.13 = (f32[8,256,128]{2,1,0:T(8,128)}, f32[8,256,128]{2,1,0:T(8,128)S(1)}, u32[]{:S(2)}, u32[]{:S(2)}) collective-permute-start(f32[8,256,128]{2,1,0:T(8,128)} %pad_maximum_fusion.1.refs_0_), channel_id=1, source_target_pairs={{0,48},{1,49},{2,50},{3,51},{4,52},{5,53},{6,54},{7,55},{8,56},{9,... | collective-permute-start | bytes 3145736 | tf_op jit(solution)/shard_map/ppermute | solution.py:35
  104.0 24.6 %collective-permute-start.11 = (f32[8,256,128]{2,1,0:T(8,128)}, f32[8,256,128]{2,1,0:T(8,128)}, u32[]{:S(2)}, u32[]{:S(2)}) collective-permute-start(f32[8,256,128]{2,1,0:T(8,128)} %get-tuple-element.49.refs_2_), channel_id=1, source_target_pairs={{0,1},{1,2},{2,3},{3,0},{4,5},{5,6},{6,7},{7,4},{8,11},{9,8},{10,9... | collective-permute-start | bytes 3145736 | tf_op jit(solution)/shard_map/ppermute | solution.py:35
  104.0 23.6 %collective-permute-start.12 = (f32[6,256,128]{2,1,0:T(8,128)}, f32[6,256,128]{2,1,0:T(8,128)S(1)}, u32[]{:S(2)}, u32[]{:S(2)}) collective-permute-start(f32[6,256,128]{2,1,0:T(8,128)} %get-tuple-element.50.refs_5_), channel_id=1, source_target_pairs={{0,1},{1,2},{2,3},{3,0},{4,5},{5,6},{6,7},{7,4},{8,11},{9,8},{10,9... | collective-permute-start | bytes 2359304 | tf_op jit(solution)/shard_map/ppermute | solution.py:35
  105.3 30.7 %collective-permute-start.17 = (f32[8,256,128]{2,1,0:T(8,128)}, f32[8,256,128]{2,1,0:T(8,128)S(1)}, u32[]{:S(2)}, u32[]{:S(2)}) collective-permute-start(f32[8,256,128]{2,1,0:T(8,128)} %pad_maximum_fusion.1.refs_0_), channel_id=1, source_target_pairs={{0,8},{1,9},{2,10},{3,11},{4,12},{5,13},{6,14},{7,15},{8,0},{9,1},... | collective-permute-start | bytes 3145736 | tf_op jit(solution)/shard_map/ppermute | solution.py:35
  130.9 15.4 %collective-permute-start.16 = (f32[8,256,128]{2,1,0:T(8,128)S(1)}, f32[8,256,128]{2,1,0:T(8,128)S(1)}, u32[]{:S(2)}, u32[]{:S(2)}) collective-permute-start(f32[8,256,128]{2,1,0:T(8,128)S(1)} %broadcast_select_fusion), channel_id=1, source_target_pairs={{0,16},{1,17},{2,18},{3,19},{4,20},{5,21},{6,22},{7,23},{8,56},{9,... | collective-permute-start | bytes 3145736 | tf_op jit(solution)/shard_map/ppermute | solution.py:35
  132.4 13.9 %collective-permute-start.19 = (f32[8,256,128]{2,1,0:T(8,128)}, f32[8,256,128]{2,1,0:T(8,128)S(1)}, u32[]{:S(2)}, u32[]{:S(2)}) collective-permute-start(f32[8,256,128]{2,1,0:T(8,128)} %get-tuple-element.54.refs_2_), channel_id=1, source_target_pairs={{0,8},{1,9},{2,10},{3,11},{4,12},{5,13},{6,14},{7,15},{8,0},{9,1},... | collective-permute-start | bytes 3145736 | tf_op jit(solution)/shard_map/ppermute | solution.py:35
  132.4 14.8 %collective-permute-start.18 = (f32[8,256,128]{2,1,0:T(8,128)}, f32[8,256,128]{2,1,0:T(8,128)}, u32[]{:S(2)}, u32[]{:S(2)}) collective-permute-start(f32[8,256,128]{2,1,0:T(8,128)} %get-tuple-element.55.refs_1_), channel_id=1, source_target_pairs={{0,8},{1,9},{2,10},{3,11},{4,12},{5,13},{6,14},{7,15},{8,0},{9,1},... | collective-permute-start | bytes 3145736 | tf_op jit(solution)/shard_map/ppermute | solution.py:35
  132.9 13.4 %collective-permute-start.15 = (f32[6,256,128]{2,1,0:T(8,128)}, f32[6,256,128]{2,1,0:T(8,128)S(1)}, u32[]{:S(2)}, u32[]{:S(2)}) collective-permute-start(f32[6,256,128]{2,1,0:T(8,128)} %get-tuple-element.53.refs_6_), channel_id=1, source_target_pairs={{0,1},{1,2},{2,3},{3,0},{4,5},{5,6},{6,7},{7,4},{8,11},{9,8},{10,9... | collective-permute-start | bytes 2359304 | tf_op jit(solution)/shard_map/ppermute | solution.py:35
  150.2 2.7 %collective-permute-start.20 = (f32[8,256,128]{2,1,0:T(8,128)S(1)}, f32[8,256,128]{2,1,0:T(8,128)S(1)}, u32[]{:S(2)}, u32[]{:S(2)}) collective-permute-start(f32[8,256,128]{2,1,0:T(8,128)S(1)} %pad_maximum_fusion.2), channel_id=1, source_target_pairs={{0,8},{1,9},{2,10},{3,11},{4,12},{5,13},{6,14},{7,15},{8,0},{9,1},... | collective-permute-start | bytes 3145736 | tf_op jit(solution)/shard_map/ppermute | solution.py:35
  150.3 4.4 %collective-permute-start.21 = (f32[8,256,128]{2,1,0:T(8,128)}, f32[8,256,128]{2,1,0:T(8,128)S(1)}, u32[]{:S(2)}, u32[]{:S(2)}) collective-permute-start(f32[8,256,128]{2,1,0:T(8,128)} %get-tuple-element.57.refs_3_), channel_id=1, source_target_pairs={{0,8},{1,9},{2,10},{3,11},{4,12},{5,13},{6,14},{7,15},{8,0},{9,1},... | collective-permute-start | bytes 3145736 | tf_op jit(solution)/shard_map/ppermute | solution.py:35
  168.6 11.7 %collective-permute-start.23 = (f32[2,256,128]{2,1,0:T(8,128)S(1)}, f32[2,256,128]{2,1,0:T(8,128)S(1)}, u32[]{:S(2)}, u32[]{:S(2)}) collective-permute-start(f32[2,256,128]{2,1,0:T(8,128)S(1)} %get-tuple-element.82), channel_id=1, source_target_pairs={{0,8},{1,24},{2,40},{3,56},{8,57},{9,9},{10,25},{11,41},{16,58},{1... | collective-permute-start | bytes 786440 | tf_op jit(solution)/shard_map/ppermute | solution.py:35
  169.3 18.1 %collective-permute-start.22 = (f32[2,256,128]{2,1,0:T(8,128)S(1)}, f32[2,256,128]{2,1,0:T(8,128)S(1)}, u32[]{:S(2)}, u32[]{:S(2)}) collective-permute-start(f32[2,256,128]{2,1,0:T(8,128)S(1)} %get-tuple-element.83), channel_id=1, source_target_pairs={{0,0},{1,16},{2,32},{3,48},{8,49},{9,1},{10,17},{11,33},{16,50},{1... | collective-permute-start | bytes 786440 | tf_op jit(solution)/shard_map/ppermute | solution.py:35
  189.7 6.5 %collective-permute-start.24 = (f32[2,256,128]{2,1,0:T(8,128)S(1)}, f32[2,256,128]{2,1,0:T(8,128)S(1)}, u32[]{:S(2)}, u32[]{:S(2)}) collective-permute-start(f32[2,256,128]{2,1,0:T(8,128)S(1)} %broadcast_select_fusion.3), channel_id=1, source_target_pairs={{0,64},{1,65},{2,66},{3,67},{4,68},{5,69},{6,70},{7,71},{8,72},{9,... | collective-permute-start | bytes 786440 | tf_op jit(solution)/shard_map/ppermute | solution.py:35
  196.1 23.8 %collective-permute-start.27 = (f32[4,256,128]{2,1,0:T(8,128)S(1)}, f32[4,256,128]{2,1,0:T(8,128)S(1)}, u32[]{:S(2)}, u32[]{:S(2)}) collective-permute-start(f32[4,256,128]{2,1,0:T(8,128)S(1)} %pad_maximum_fusion.6.refs_0_), channel_id=1, source_target_pairs={{0,32},{1,33},{2,34},{3,35},{4,36},{5,37},{6,38},{7,39},{8,40},{9,... | collective-permute-start | bytes 1572872 | tf_op jit(solution)/shard_map/ppermute | solution.py:35
  199.3 24.5 %collective-permute-start.26 = (f32[4,256,128]{2,1,0:T(8,128)S(1)}, f32[4,256,128]{2,1,0:T(8,128)S(1)}, u32[]{:S(2)}, u32[]{:S(2)}) collective-permute-start(f32[4,256,128]{2,1,0:T(8,128)S(1)} %pad_maximum_fusion.6.refs_0_), channel_id=1, source_target_pairs={{0,16},{1,17},{2,18},{3,19},{4,20},{5,21},{6,22},{7,23},{8,24},{9,... | collective-permute-start | bytes 1572872 | tf_op jit(solution)/shard_map/ppermute | solution.py:35
  199.3 24.5 %collective-permute-start.25 = (f32[4,256,128]{2,1,0:T(8,128)S(1)}, f32[4,256,128]{2,1,0:T(8,128)S(1)}, u32[]{:S(2)}, u32[]{:S(2)}) collective-permute-start(f32[4,256,128]{2,1,0:T(8,128)S(1)} %pad_maximum_fusion.6.refs_0_), channel_id=1, source_target_pairs={{0,48},{1,49},{2,50},{3,51},{4,52},{5,53},{6,54},{7,55},{8,56},{9,... | collective-permute-start | bytes 1572872 | tf_op jit(solution)/shard_map/ppermute | solution.py:35
  219.9 7.8 %collective-permute-start.28 = (f32[4,256,128]{2,1,0:T(8,128)S(1)}, f32[4,256,128]{2,1,0:T(8,128)S(1)}, u32[]{:S(2)}, u32[]{:S(2)}) collective-permute-start(f32[4,256,128]{2,1,0:T(8,128)S(1)} %pad_maximum_fusion.6.refs_0_), channel_id=1, source_target_pairs={{0,8},{1,9},{2,10},{3,11},{4,12},{5,13},{6,14},{7,15},{8,0},{9,1},... | collective-permute-start | bytes 1572872 | tf_op jit(solution)/shard_map/ppermute | solution.py:35
  227.3 1.9 collective-permute-start.29
  227.3 2.7 %collective-permute-start.30 = (f32[4,256,128]{2,1,0:T(8,128)S(1)}, f32[4,256,128]{2,1,0:T(8,128)S(1)}, u32[]{:S(2)}, u32[]{:S(2)}) collective-permute-start(f32[4,256,128]{2,1,0:T(8,128)S(1)} %get-tuple-element.73.refs_2_), channel_id=1, source_target_pairs={{0,8},{1,9},{2,10},{3,11},{4,12},{5,13},{6,14},{7,15},{8,0},{9,1},... | collective-permute-start | bytes 1572872 | tf_op jit(solution)/shard_map/ppermute | solution.py:35
  227.8 2.9 %collective-permute-start.31 = (f32[4,256,128]{2,1,0:T(8,128)S(1)}, f32[4,256,128]{2,1,0:T(8,128)S(1)}, u32[]{:S(2)}, u32[]{:S(2)}) collective-permute-start(f32[4,256,128]{2,1,0:T(8,128)S(1)} %get-tuple-element.74.refs_3_), channel_id=1, source_target_pairs={{0,8},{1,9},{2,10},{3,11},{4,12},{5,13},{6,14},{7,15},{8,0},{9,1},... | collective-permute-start | bytes 1572872 | tf_op jit(solution)/shard_map/ppermute | solution.py:35
  (40 other events, 223.4 us)
